TPU v7x, 32 devices: a whole 2x2x4 slice. The times are simulated.
32 devices in a mesh: segment: 2 (over y), tm: 4 (over z), rows: 4 (over x, core).
Axes of the slice: x: 2, y: 2, z: 4, core: 2. Of those that a mesh axis runs over, the one named last changes fastest.
Arguments:
- input_clip: bfloat16 [8, 8, 128, 128], P('tm', 'rows'), may hold values from -6 to 6
- cotangent: bfloat16 [8, 8, 128, 128], P('tm', 'rows'), may hold values from -0.125 to 0.125
- kernel_in: bfloat16 [2, 3456, 256], P('segment'), may hold values from -0.109375 to 0.109375
- kernel_out: bfloat16 [2, 6912, 128], P('segment'), may hold values from -0.078125 to 0.078125
Outputs:
- sections: bfloat16 [2, 8, 8, 128, 128], P('segment', 'tm', 'rows')
- grad_in: float32 [2, 884736], P('segment', ('tm', 'rows'))
- grad_out: float32 [2, 884736], P('segment', ('tm', 'rows'))
All inputs are finite; a program needn't handle non-finite values.
Results may differ from a plain program's by a relative error of at most 0.007.
Values may be sent and summed in bfloat16 or wider, within the bound.
No kernel may reach another device: no remote copies, remote signals or barrier semaphores. Data moves between devices by JAX's collectives and lax.ppermute only.
A program may use at most 128 MiB of HBM per device.

v0:
```python
from functools import partial

import jax
import jax.numpy as jnp
from jax import lax
from jax.sharding import PartitionSpec as P


def padded_2(cells, sides, width):
    for axis, dim in sides:
        count = lax.axis_size(axis)
        ends = count - 1
        head = lax.slice_in_dim(cells, 0, width, axis=dim)
        tail = lax.slice_in_dim(cells, cells.shape[dim] - width, cells.shape[dim], axis=dim)
        cells = jnp.concatenate(
            [
                lax.ppermute(tail, axis, [(i, (i + 1) % count) for i in range(ends)]),
                cells,
                lax.ppermute(head, axis, [((i + 1) % count, i) for i in range(ends)]),
            ],
            axis=dim,
        )
    return cells


def passed_along(block, axis, distance):
    devices = range(lax.axis_size(axis))
    route = [(i - distance, i) for i in devices if i - distance in devices]
    return lax.ppermute(block, axis, route)


def swapped(block, axis, apart):
    count = lax.axis_size(axis)
    route = []
    for low in range(count):
        high = low | 1 << apart
        if high != low and high < count:
            route += [(low, high), (high, low)]
    return lax.ppermute(block, axis, route)


def extend_rims(longer):
    widened = padded_2(longer, (("rows", 1),), 1)
    extended = jnp.pad(widened, ((0, 0), (0, 0), (1, 1), (0, 0)))
    return extended


def past_padded(volume):
    before = passed_along(volume, "tm", 1)
    return extend_rims(jnp.concatenate([before, volume], axis=0))


def future_padded(volume):
    after = passed_along(volume, "tm", -1)
    return extend_rims(jnp.concatenate([volume, after], axis=0))


def tap_matrix(padded, shape, reverse):
    frames, height, width = (shape[0], shape[1], shape[2])
    columns = []
    for depth in range(3):
        for row_step in range(3):
            for col_step in range(3):
                if reverse:
                    lead, mid, tail = (2 - depth, 2 - row_step, 2 - col_step)
                else:
                    lead, mid, tail = (depth, row_step, col_step)
                columns.append(
                    padded[lead : lead + frames, mid : mid + height, tail : tail + width, :]
                )
    stacked = jnp.concatenate(columns, axis=3)
    return stacked.reshape(frames * height * width, -1)


def flipped(kernel, inputs):
    return kernel.reshape(27, inputs, -1).transpose(0, 2, 1).reshape(-1, inputs)


def gate_grad(upstream, hidden):
    sigmoid_h = jax.nn.sigmoid(hidden)
    return (upstream * sigmoid_h * (1.0 + hidden * (1.0 - sigmoid_h))).astype(jnp.bfloat16)


def masked_dot(flag, taps, kernel):
    return lax.cond(
        flag,
        lambda: jnp.dot(taps, kernel, preferred_element_type=jnp.float32),
        lambda: jnp.zeros((taps.shape[0], kernel.shape[1]), jnp.float32),
    )


def forward(volume, kernel_a, kernel_b, product):
    shape = volume.shape
    first_taps = tap_matrix(past_padded(volume), shape, False)
    hidden = product(first_taps, kernel_a)
    active = jax.nn.silu(hidden).astype(jnp.bfloat16).reshape(shape[0], shape[1], shape[2], -1)
    second_taps = tap_matrix(past_padded(active), shape, False)
    branch = product(second_taps, kernel_b)
    result = (
        (volume.reshape(-1, shape[3]).astype(jnp.float32) + branch)
        .astype(jnp.bfloat16)
        .reshape(shape)
    )
    return (result, first_taps, hidden, active, second_taps)


def contract(taps, upstream):
    return lax.dot_general(
        taps, upstream, (((0,), (0,)), ((), ())), preferred_element_type=jnp.float32
    ).reshape(-1)


def across(volume):
    return swapped(volume, "segment", 0)


def relay_plan(input_clip, cotangent, kernel_in, kernel_out):
    kernel_a = kernel_in[0]
    kernel_b = kernel_out[0]
    shape = input_clip.shape
    channels = shape[3]
    hidden_width = kernel_a.shape[1]
    on_encoder = lax.axis_index("segment") == 0
    on_decoder = jnp.logical_not(on_encoder)
    enc_dot = partial(masked_dot, on_encoder)
    dec_dot = partial(masked_dot, on_decoder)
    enc_result, enc_first, enc_hidden, enc_active, enc_second = forward(
        input_clip, kernel_a, kernel_b, enc_dot
    )
    linked = across(enc_result)
    dec_result, dec_first, dec_hidden, dec_active, dec_second = forward(
        linked, kernel_a, kernel_b, dec_dot
    )
    sections = jnp.where(on_encoder, enc_result, dec_result)
    role_hidden = jnp.where(on_encoder, enc_hidden, dec_hidden)
    back_out = flipped(kernel_b, hidden_width)
    back_in = flipped(kernel_a, channels)
    upstream = dec_dot(tap_matrix(future_padded(cotangent), shape, True), back_out)
    gated = gate_grad(upstream, dec_hidden).reshape(shape[0], shape[1], shape[2], -1)
    inner = dec_dot(tap_matrix(future_padded(gated), shape, True), back_in)
    passed = (
        (cotangent.reshape(-1, channels).astype(jnp.float32) + inner)
        .astype(jnp.bfloat16)
        .reshape(shape)
    )
    returned = across(passed)
    role_grad = jnp.where(on_encoder, returned, cotangent)
    enc_upstream = enc_dot(tap_matrix(future_padded(returned), shape, True), back_out)
    role_upstream = jnp.where(on_encoder, enc_upstream, upstream)
    role_gated = gate_grad(role_upstream, role_hidden)
    first_role = jnp.where(on_encoder, enc_first, dec_first)
    second_role = jnp.where(on_encoder, enc_second, dec_second)
    out_term = contract(second_role, role_grad.reshape(-1, channels))
    in_term = contract(first_role, role_gated)
    in_sum, out_sum = (
        lax.psum_scatter(in_term, ("tm", "rows"), scatter_dimension=0, tiled=True),
        lax.psum_scatter(out_term, ("tm", "rows"), scatter_dimension=0, tiled=True),
    )
    return (sections[None], in_sum[None], out_sum[None])


def on_device(input_clip, cotangent, kernel_in, kernel_out):
    outputs = relay_plan(input_clip, cotangent, kernel_in, kernel_out)
    return outputs


def solution(mesh):
    in_specs = (
        P("tm", "rows", None, None),
        P("tm", "rows", None, None),
        P("segment", None, None),
        P("segment", None, None),
    )
    out_specs = (
        P("segment", "tm", "rows", None, None),
        P("segment", ("tm", "rows")),
        P("segment", ("tm", "rows")),
    )
    return jax.shard_map(
        on_device, mesh=mesh, in_specs=in_specs, out_specs=out_specs, check_vma=False
    )
```

profile of v0, /device:TPU:0, one launch (start us, length us, event | category | flops | bytes accessed | tf_op | source)
XLA Modules:
  0.0 332.5 jit_solution(1455460534903321464)
XLA Ops:
  7.2 5.1 %collective-permute-start = (bf16[2,2,128,128]{3,2,1,0:T(8,128)(2,1)}, bf16[2,2,128,128]{3,2,1,0:T(8,128)(2,1)S(1)}, u32[]{:S(2)}, u32[]{:S(2)}) collective-permute-start(bf16[2,2,128,128]{3,2,1,0:T(8,128)(2,1)} %param.18), channel_id=1, source_target_pairs={{0,4},{4,8},{8,12},{1,5},{5,9},{9,13},{2,6},{6,10},{10,14},{3,7},{... | collective-permute-start | bytes 393224 | tf_op jit(solution)/shard_map/ppermute | solution.py:29
  12.3 1.3 collective-permute-start.13
  13.6 3.9 %copy.12 = bf16[27,256,128]{1,2,0:T(8,128)(2,1)} copy(bf16[27,256,128]{2,1,0:T(8,128)(2,1)} %bitcast.80) | data formatting | bytes 3538944 | tf_op jit(solution)/shard_map/reshape;squeeze | solution.py:76
  17.6 1.5 collective-permute-start.1
  19.1 1.3 collective-permute-start.2
  20.4 4.6 %collective-permute-start.14 = (bf16[4,1,128,128]{3,2,1,0:T(8,128)(2,1)S(1)}, bf16[4,1,128,128]{3,2,1,0:T(8,128)(2,1)S(1)}, u32[]{:S(2)}, u32[]{:S(2)}) collective-permute-start(bf16[4,1,128,128]{3,2,1,0:T(8,128)(2,1)S(1)} %get-tuple-element.94), channel_id=1, source_target_pairs={{0,1},{1,2},{2,3},{4,5},{5,6},{6,7},{8,9},{9,10},{10,11},{12,13},{... | collective-permute-start | bytes 393224 | tf_op jit(solution)/shard_map/ppermute | solution.py:17
  25.0 1.3 collective-permute-start.15
  28.2 1.4 copy-done.8
  29.6 1.1 conditional.7
  29.6 1.1 fusion.48
  30.9 4.6 %collective-permute-start.3 = (bf16[2,2,128,256]{3,2,1,0:T(8,128)(2,1)S(1)}, bf16[2,2,128,256]{3,2,1,0:T(8,128)(2,1)S(1)}, u32[]{:S(2)}, u32[]{:S(2)}) collective-permute-start(bf16[2,2,128,256]{3,2,1,0:T(8,128)(2,1)S(1)} %bitcast.65), channel_id=1, source_target_pairs={{0,4},{4,8},{8,12},{1,5},{5,9},{9,13},{2,6},{6,10},{10,14},{3,7},{... | collective-permute-start | bytes 786440 | tf_op jit(solution)/shard_map/ppermute | solution.py:29
  36.7 4.0 %collective-permute-done.3 = bf16[2,2,128,256]{3,2,1,0:T(8,128)(2,1)S(1)} collective-permute-done((bf16[2,2,128,256]{3,2,1,0:T(8,128)(2,1)S(1)}, bf16[2,2,128,256]{3,2,1,0:T(8,128)(2,1)S(1)}, u32[]{:S(2)}, u32[]{:S(2)}) %collective-permute-start.3) | collective-permute-done | bytes 262176 | tf_op jit(solution)/shard_map/ppermute | solution.py:29
  40.7 3.5 %collective-permute-start.4 = (bf16[4,1,128,256]{3,2,1,0:T(8,128)(2,1)S(1)}, bf16[4,1,128,256]{3,2,1,0:T(8,128)(2,1)S(1)}, u32[]{:S(2)}, u32[]{:S(2)}) collective-permute-start(bf16[4,1,128,256]{3,2,1,0:T(8,128)(2,1)S(1)} %get-tuple-element.90), channel_id=1, source_target_pairs={{0,1},{1,2},{2,3},{4,5},{5,6},{6,7},{8,9},{9,10},{10,11},{12,13},{... | collective-permute-start | bytes 786440 | tf_op jit(solution)/shard_map/ppermute | solution.py:17
  44.2 1.3 collective-permute-start.5
  45.6 1.8 copy-done.9
  47.5 1.4 collective-permute-done.5
  50.6 0.9 copy-done.1
  51.5 1.9 copy-done.6
  53.4 2.0 conditional.8
  53.4 2.0 fusion.49
  56.3 4.3 %collective-permute-done.6 = bf16[2,2,128,128]{3,2,1,0:T(8,128)(2,1)S(1)} collective-permute-done((bf16[2,2,128,128]{3,2,1,0:T(8,128)(2,1)S(1)}, bf16[2,2,128,128]{3,2,1,0:T(8,128)(2,1)S(1)}, u32[]{:S(2)}, u32[]{:S(2)}) %collective-permute-start.6) | collective-permute-done | bytes 131104 | tf_op jit(solution)/shard_map/ppermute | solution.py:39
  60.5 4.4 %collective-permute-start.7 = (bf16[2,2,128,128]{3,2,1,0:T(8,128)(2,1)S(1)}, bf16[2,2,128,128]{3,2,1,0:T(8,128)(2,1)S(1)}, u32[]{:S(2)}, u32[]{:S(2)}) collective-permute-start(bf16[2,2,128,128]{3,2,1,0:T(8,128)(2,1)S(1)} %collective-permute-done.6), channel_id=1, source_target_pairs={{0,4},{4,8},{8,12},{1,5},{5,9},{9,13},{2,6},{6,10},{10,14},{3,7},{... | collective-permute-start | bytes 393224 | tf_op jit(solution)/shard_map/ppermute | solution.py:29
  66.3 1.1 collective-permute-done.7
  67.5 4.7 %collective-permute-start.8 = (bf16[4,1,128,128]{3,2,1,0:T(8,128)(2,1)S(1)}, bf16[4,1,128,128]{3,2,1,0:T(8,128)(2,1)S(1)}, u32[]{:S(2)}, u32[]{:S(2)}) collective-permute-start(bf16[4,1,128,128]{3,2,1,0:T(8,128)(2,1)S(1)} %get-tuple-element.96), channel_id=1, source_target_pairs={{0,1},{1,2},{2,3},{4,5},{5,6},{6,7},{8,9},{9,10},{10,11},{12,13},{... | collective-permute-start | bytes 393224 | tf_op jit(solution)/shard_map/ppermute | solution.py:17
  72.1 1.3 collective-permute-start.9
  74.2 2.5 collective-permute-done.9
  78.2 1.8 copy-done.10
  80.3 1.3 collective-permute-start.16
  81.6 5.0 %collective-permute-start.10 = (bf16[2,2,128,256]{3,2,1,0:T(8,128)(2,1)S(1)}, bf16[2,2,128,256]{3,2,1,0:T(8,128)(2,1)S(1)}, u32[]{:S(2)}, u32[]{:S(2)}) collective-permute-start(bf16[2,2,128,256]{3,2,1,0:T(8,128)(2,1)S(1)} %bitcast.59), channel_id=1, source_target_pairs={{0,4},{4,8},{8,12},{1,5},{5,9},{9,13},{2,6},{6,10},{10,14},{3,7},{... | collective-permute-start | bytes 786440 | tf_op jit(solution)/shard_map/ppermute | solution.py:29
  86.6 2.4 collective-permute-done.16
  89.1 4.6 %collective-permute-start.17 = (bf16[4,1,128,256]{3,2,1,0:T(8,128)(2,1)S(1)}, bf16[4,1,128,256]{3,2,1,0:T(8,128)(2,1)S(1)}, u32[]{:S(2)}, u32[]{:S(2)}) collective-permute-start(bf16[4,1,128,256]{3,2,1,0:T(8,128)(2,1)S(1)} %get-tuple-element.80), channel_id=1, source_target_pairs={{0,1},{1,2},{2,3},{4,5},{5,6},{6,7},{8,9},{9,10},{10,11},{12,13},{... | collective-permute-start | bytes 786440 | tf_op jit(solution)/shard_map/ppermute | solution.py:17
  93.7 1.5 collective-permute-start.18
  95.2 0.9 fusion.16
  96.0 3.3 collective-permute-start.11
  99.3 1.3 collective-permute-start.12
  101.1 0.8 constant_dynamic-update-slice_fusion.167
  102.0 0.8 constant_dynamic-update-slice_fusion.166
  103.5 0.8 constant_dynamic-update-slice_fusion.164
  105.0 0.8 constant_dynamic-update-slice_fusion.162
  105.8 0.8 constant_dynamic-update-slice_fusion.161
  108.1 0.8 constant_dynamic-update-slice_fusion.158
  108.9 0.8 constant_dynamic-update-slice_fusion.157
  110.5 0.8 constant_dynamic-update-slice_fusion.155
  112.7 0.8 constant_dynamic-update-slice_fusion.152
  114.3 0.8 constant_dynamic-update-slice_fusion.150
  115.1 0.8 constant_dynamic-update-slice_fusion.149
  117.4 0.8 constant_dynamic-update-slice_fusion.146
  118.1 0.8 constant_dynamic-update-slice_fusion.145
  119.7 0.8 constant_dynamic-update-slice_fusion.143
  121.2 0.8 constant_dynamic-update-slice_fusion.141
  122.1 17.7 %collective-permute-start.19 = (bf16[2,2,128,128]{3,2,1,0:T(8,128)(2,1)S(1)}, bf16[2,2,128,128]{3,2,1,0:T(8,128)(2,1)S(1)}, u32[]{:S(2)}, u32[]{:S(2)}) collective-permute-start(bf16[2,2,128,128]{3,2,1,0:T(8,128)(2,1)S(1)} %bitcast.89), channel_id=1, source_target_pairs={{0,16},{16,0},{1,17},{17,1},{2,18},{18,2},{3,19},{19,3},{4,20},{20... | collective-permute-start | bytes 393224 | tf_op jit(solution)/shard_map/ppermute | solution.py:39
  141.4 1.3 collective-permute-done.19
  142.7 1.3 collective-permute-start.20
  144.1 6.5 %collective-permute-done.20 = bf16[2,2,128,128]{3,2,1,0:T(8,128)(2,1)S(1)} collective-permute-done((bf16[2,2,128,128]{3,2,1,0:T(8,128)(2,1)S(1)}, bf16[2,2,128,128]{3,2,1,0:T(8,128)(2,1)S(1)}, u32[]{:S(2)}, u32[]{:S(2)}) %collective-permute-start.20) | collective-permute-done | bytes 131104 | tf_op jit(solution)/shard_map/ppermute | solution.py:29
  150.6 2.1 collective-permute-start.21
  152.8 1.3 collective-permute-start.22
  154.1 3.9 %convolution_bitcast_fusion = f32[884736]{0:T(1024)} fusion(bf16[2,2,128,6912]{3,2,1,0:T(8,128)(2,1)S(1)} %bitcast.92, bf16[2,2,128,6912]{3,2,1,0:T(8,128)(2,1)S(1)} %constant_dynamic-update-slice_fusion.85, pred[]{:T(512)S(6)} %eq.3, bf16[2,2,128,128]{3,2,1,0:T(8,128)(2,1)S(1)} %collective-permute-done.19, bf16[2,2,128,128]{3,2,1,0:T(8,128)(2,1)S(1)} %copy-done.5), kind=kOutput, calls=%fused_computation | convolution fusion | flops 909574144 | bytes 17956864 | tf_op jit(solution)/shard_map/dot_general | solution.py:108
  160.1 1.3 conditional.13
  160.1 1.1 fusion.54
  161.4 3.3 fusion.6
  164.7 3.6 %copy.17 = f32[432,2,8,128]{3,1,2,0:T(2,128)} copy(f32[432,2,8,128]{3,2,1,0:T(8,128)S(1)} %fusion.6) | data formatting | bytes 7077888
  171.0 151.4 %all-reduce.12.cloned.1.call-done = (f32[884736]{0:T(1024)}, f32[884736]{0:T(1024)}) async-done(((f32[884736]{0:T(1024)}, f32[884736]{0:T(1024)}), (f32[884736]{0:T(1024)}, f32[884736]{0:T(1024)})) %all-reduce.12.cloned.1.call-update) | async-done | bytes 7077904
  322.4 1.6 dynamic-slice.1
  324.0 1.6 dynamic-slice.3
  (254 shorter events, 24.4 us)
Async XLA Ops:
  7.2 10.4 %copy-start.4 = (bf16[2,2,128,128]{3,2,1,0:T(8,128)(2,1)S(1)}, bf16[2,2,128,128]{3,2,1,0:T(8,128)(2,1)}, u32[]{:S(2)}) copy-start(bf16[2,2,128,128]{3,2,1,0:T(8,128)(2,1)} %param.18) | copy-start | bytes 393220
  7.2 10.3 %copy-start.5 = (bf16[2,2,128,128]{3,2,1,0:T(8,128)(2,1)S(1)}, bf16[2,2,128,128]{3,2,1,0:T(8,128)(2,1)}, u32[]{:S(2)}) copy-start(bf16[2,2,128,128]{3,2,1,0:T(8,128)(2,1)} %param.19) | copy-start | bytes 393220
  7.2 315.2 %all-reduce.12.cloned.1.call-start = ((), (), s32[]{:S(2)}) async-start(), calls=%async_computation | async-start | bytes 14155776
  7.2 10.3 %collective-permute-start = (bf16[2,2,128,128]{3,2,1,0:T(8,128)(2,1)}, bf16[2,2,128,128]{3,2,1,0:T(8,128)(2,1)S(1)}, u32[]{:S(2)}, u32[]{:S(2)}) collective-permute-start(bf16[2,2,128,128]{3,2,1,0:T(8,128)(2,1)} %param.18), channel_id=1, source_target_pairs={{0,4},{4,8},{8,12},{1,5},{5,9},{9,13},{2,6},{6,10},{10,14},{3,7},{... | collective-permute-start | bytes 393224 | tf_op jit(solution)/shard_map/ppermute | solution.py:29
  12.3 8.1 %collective-permute-start.13 = (bf16[2,2,128,128]{3,2,1,0:T(8,128)(2,1)}, bf16[2,2,128,128]{3,2,1,0:T(8,128)(2,1)S(1)}, u32[]{:S(2)}, u32[]{:S(2)}) collective-permute-start(bf16[2,2,128,128]{3,2,1,0:T(8,128)(2,1)} %param.19), channel_id=1, source_target_pairs={{4,0},{8,4},{12,8},{5,1},{9,5},{13,9},{6,2},{10,6},{14,10},{7,3},{... | collective-permute-start | bytes 393224 | tf_op jit(solution)/shard_map/ppermute | solution.py:29
  17.6 8.7 %collective-permute-start.1 = (bf16[4,1,128,128]{3,2,1,0:T(8,128)(2,1)S(1)}, bf16[4,1,128,128]{3,2,1,0:T(8,128)(2,1)S(1)}, u32[]{:S(2)}, u32[]{:S(2)}) collective-permute-start(bf16[4,1,128,128]{3,2,1,0:T(8,128)(2,1)S(1)} %get-tuple-element.98), channel_id=1, source_target_pairs={{0,1},{1,2},{2,3},{4,5},{5,6},{6,7},{8,9},{9,10},{10,11},{12,13},{... | collective-permute-start | bytes 393224 | tf_op jit(solution)/shard_map/ppermute | solution.py:17
  19.1 7.3 %collective-permute-start.2 = (bf16[4,1,128,128]{3,2,1,0:T(8,128)(2,1)S(1)}, bf16[4,1,128,128]{3,2,1,0:T(8,128)(2,1)S(1)}, u32[]{:S(2)}, u32[]{:S(2)}) collective-permute-start(bf16[4,1,128,128]{3,2,1,0:T(8,128)(2,1)S(1)} %get-tuple-element.99), channel_id=1, source_target_pairs={{1,0},{2,1},{3,2},{5,4},{6,5},{7,6},{9,8},{10,9},{11,10},{13,12},{... | collective-permute-start | bytes 393224 | tf_op jit(solution)/shard_map/ppermute | solution.py:19
  20.4 15.0 %collective-permute-start.14 = (bf16[4,1,128,128]{3,2,1,0:T(8,128)(2,1)S(1)}, bf16[4,1,128,128]{3,2,1,0:T(8,128)(2,1)S(1)}, u32[]{:S(2)}, u32[]{:S(2)}) collective-permute-start(bf16[4,1,128,128]{3,2,1,0:T(8,128)(2,1)S(1)} %get-tuple-element.94), channel_id=1, source_target_pairs={{0,1},{1,2},{2,3},{4,5},{5,6},{6,7},{8,9},{9,10},{10,11},{12,13},{... | collective-permute-start | bytes 393224 | tf_op jit(solution)/shard_map/ppermute | solution.py:17
  25.0 10.4 %collective-permute-start.15 = (bf16[4,1,128,128]{3,2,1,0:T(8,128)(2,1)S(1)}, bf16[4,1,128,128]{3,2,1,0:T(8,128)(2,1)S(1)}, u32[]{:S(2)}, u32[]{:S(2)}) collective-permute-start(bf16[4,1,128,128]{3,2,1,0:T(8,128)(2,1)S(1)} %get-tuple-element.95), channel_id=1, source_target_pairs={{1,0},{2,1},{3,2},{5,4},{6,5},{7,6},{9,8},{10,9},{11,10},{13,12},{... | collective-permute-start | bytes 393224 | tf_op jit(solution)/shard_map/ppermute | solution.py:19
  26.7 1.5 copy-start
  27.8 1.8 copy-start.8
  30.9 9.8 %collective-permute-start.3 = (bf16[2,2,128,256]{3,2,1,0:T(8,128)(2,1)S(1)}, bf16[2,2,128,256]{3,2,1,0:T(8,128)(2,1)S(1)}, u32[]{:S(2)}, u32[]{:S(2)}) collective-permute-start(bf16[2,2,128,256]{3,2,1,0:T(8,128)(2,1)S(1)} %bitcast.65), channel_id=1, source_target_pairs={{0,4},{4,8},{8,12},{1,5},{5,9},{9,13},{2,6},{6,10},{10,14},{3,7},{... | collective-permute-start | bytes 786440 | tf_op jit(solution)/shard_map/ppermute | solution.py:29
  40.7 4.9 %collective-permute-start.4 = (bf16[4,1,128,256]{3,2,1,0:T(8,128)(2,1)S(1)}, bf16[4,1,128,256]{3,2,1,0:T(8,128)(2,1)S(1)}, u32[]{:S(2)}, u32[]{:S(2)}) collective-permute-start(bf16[4,1,128,256]{3,2,1,0:T(8,128)(2,1)S(1)} %get-tuple-element.90), channel_id=1, source_target_pairs={{0,1},{1,2},{2,3},{4,5},{5,6},{6,7},{8,9},{9,10},{10,11},{12,13},{... | collective-permute-start | bytes 786440 | tf_op jit(solution)/shard_map/ppermute | solution.py:17
  44.2 4.7 %collective-permute-start.5 = (bf16[4,1,128,256]{3,2,1,0:T(8,128)(2,1)S(1)}, bf16[4,1,128,256]{3,2,1,0:T(8,128)(2,1)S(1)}, u32[]{:S(2)}, u32[]{:S(2)}) collective-permute-start(bf16[4,1,128,256]{3,2,1,0:T(8,128)(2,1)S(1)} %get-tuple-element.91), channel_id=1, source_target_pairs={{1,0},{2,1},{3,2},{5,4},{6,5},{7,6},{9,8},{10,9},{11,10},{13,12},{... | collective-permute-start | bytes 786440 | tf_op jit(solution)/shard_map/ppermute | solution.py:19
  45.6 1.9 copy-start.9
  50.0 1.5 copy-start.1
  50.6 2.8 copy-start.6
  55.5 5.0 %collective-permute-start.6 = (bf16[2,2,128,128]{3,2,1,0:T(8,128)(2,1)S(1)}, bf16[2,2,128,128]{3,2,1,0:T(8,128)(2,1)S(1)}, u32[]{:S(2)}, u32[]{:S(2)}) collective-permute-start(bf16[2,2,128,128]{3,2,1,0:T(8,128)(2,1)S(1)} %bitcast.86), channel_id=1, source_target_pairs={{0,16},{16,0},{1,17},{17,1},{2,18},{18,2},{3,19},{19,3},{4,20},{20... | collective-permute-start | bytes 393224 | tf_op jit(solution)/shard_map/ppermute | solution.py:39
  60.5 6.9 %collective-permute-start.7 = (bf16[2,2,128,128]{3,2,1,0:T(8,128)(2,1)S(1)}, bf16[2,2,128,128]{3,2,1,0:T(8,128)(2,1)S(1)}, u32[]{:S(2)}, u32[]{:S(2)}) collective-permute-start(bf16[2,2,128,128]{3,2,1,0:T(8,128)(2,1)S(1)} %collective-permute-done.6), channel_id=1, source_target_pairs={{0,4},{4,8},{8,12},{1,5},{5,9},{9,13},{2,6},{6,10},{10,14},{3,7},{... | collective-permute-start | bytes 393224 | tf_op jit(solution)/shard_map/ppermute | solution.py:29
  67.5 6.8 %collective-permute-start.8 = (bf16[4,1,128,128]{3,2,1,0:T(8,128)(2,1)S(1)}, bf16[4,1,128,128]{3,2,1,0:T(8,128)(2,1)S(1)}, u32[]{:S(2)}, u32[]{:S(2)}) collective-permute-start(bf16[4,1,128,128]{3,2,1,0:T(8,128)(2,1)S(1)} %get-tuple-element.96), channel_id=1, source_target_pairs={{0,1},{1,2},{2,3},{4,5},{5,6},{6,7},{8,9},{9,10},{10,11},{12,13},{... | collective-permute-start | bytes 393224 | tf_op jit(solution)/shard_map/ppermute | solution.py:17
  72.1 4.6 %collective-permute-start.9 = (bf16[4,1,128,128]{3,2,1,0:T(8,128)(2,1)S(1)}, bf16[4,1,128,128]{3,2,1,0:T(8,128)(2,1)S(1)}, u32[]{:S(2)}, u32[]{:S(2)}) collective-permute-start(bf16[4,1,128,128]{3,2,1,0:T(8,128)(2,1)S(1)} %get-tuple-element.97), channel_id=1, source_target_pairs={{1,0},{2,1},{3,2},{5,4},{6,5},{7,6},{9,8},{10,9},{11,10},{13,12},{... | collective-permute-start | bytes 393224 | tf_op jit(solution)/shard_map/ppermute | solution.py:19
  78.2 1.8 copy-start.10
  80.3 8.7 %collective-permute-start.16 = (bf16[2,2,128,256]{3,2,1,0:T(8,128)(2,1)S(1)}, bf16[2,2,128,256]{3,2,1,0:T(8,128)(2,1)S(1)}, u32[]{:S(2)}, u32[]{:S(2)}) collective-permute-start(bf16[2,2,128,256]{3,2,1,0:T(8,128)(2,1)S(1)} %bitcast.71), channel_id=1, source_target_pairs={{4,0},{8,4},{12,8},{5,1},{9,5},{13,9},{6,2},{10,6},{14,10},{7,3},{... | collective-permute-start | bytes 786440 | tf_op jit(solution)/shard_map/ppermute | solution.py:29
  81.6 13.5 %collective-permute-start.10 = (bf16[2,2,128,256]{3,2,1,0:T(8,128)(2,1)S(1)}, bf16[2,2,128,256]{3,2,1,0:T(8,128)(2,1)S(1)}, u32[]{:S(2)}, u32[]{:S(2)}) collective-permute-start(bf16[2,2,128,256]{3,2,1,0:T(8,128)(2,1)S(1)} %bitcast.59), channel_id=1, source_target_pairs={{0,4},{4,8},{8,12},{1,5},{5,9},{9,13},{2,6},{6,10},{10,14},{3,7},{... | collective-permute-start | bytes 786440 | tf_op jit(solution)/shard_map/ppermute | solution.py:29
  89.1 11.5 %collective-permute-start.17 = (bf16[4,1,128,256]{3,2,1,0:T(8,128)(2,1)S(1)}, bf16[4,1,128,256]{3,2,1,0:T(8,128)(2,1)S(1)}, u32[]{:S(2)}, u32[]{:S(2)}) collective-permute-start(bf16[4,1,128,256]{3,2,1,0:T(8,128)(2,1)S(1)} %get-tuple-element.80), channel_id=1, source_target_pairs={{0,1},{1,2},{2,3},{4,5},{5,6},{6,7},{8,9},{9,10},{10,11},{12,13},{... | collective-permute-start | bytes 786440 | tf_op jit(solution)/shard_map/ppermute | solution.py:17
  93.7 7.0 %collective-permute-start.18 = (bf16[4,1,128,256]{3,2,1,0:T(8,128)(2,1)S(1)}, bf16[4,1,128,256]{3,2,1,0:T(8,128)(2,1)S(1)}, u32[]{:S(2)}, u32[]{:S(2)}) collective-permute-start(bf16[4,1,128,256]{3,2,1,0:T(8,128)(2,1)S(1)} %get-tuple-element.81), channel_id=1, source_target_pairs={{1,0},{2,1},{3,2},{5,4},{6,5},{7,6},{9,8},{10,9},{11,10},{13,12},{... | collective-permute-start | bytes 786440 | tf_op jit(solution)/shard_map/ppermute | solution.py:19
  96.0 43.7 %collective-permute-start.11 = (bf16[4,1,128,256]{3,2,1,0:T(8,128)(2,1)}, bf16[4,1,128,256]{3,2,1,0:T(8,128)(2,1)S(1)}, u32[]{:S(2)}, u32[]{:S(2)}) collective-permute-start(bf16[4,1,128,256]{3,2,1,0:T(8,128)(2,1)} %get-tuple-element.86), channel_id=1, source_target_pairs={{0,1},{1,2},{2,3},{4,5},{5,6},{6,7},{8,9},{9,10},{10,11},{12,13},{... | collective-permute-start | bytes 786440 | tf_op jit(solution)/shard_map/ppermute | solution.py:17
  99.3 40.5 %collective-permute-start.12 = (bf16[4,1,128,256]{3,2,1,0:T(8,128)(2,1)}, bf16[4,1,128,256]{3,2,1,0:T(8,128)(2,1)S(1)}, u32[]{:S(2)}, u32[]{:S(2)}) collective-permute-start(bf16[4,1,128,256]{3,2,1,0:T(8,128)(2,1)} %get-tuple-element.87), channel_id=1, source_target_pairs={{1,0},{2,1},{3,2},{5,4},{6,5},{7,6},{9,8},{10,9},{11,10},{13,12},{... | collective-permute-start | bytes 786440 | tf_op jit(solution)/shard_map/ppermute | solution.py:19
  122.1 20.6 %collective-permute-start.19 = (bf16[2,2,128,128]{3,2,1,0:T(8,128)(2,1)S(1)}, bf16[2,2,128,128]{3,2,1,0:T(8,128)(2,1)S(1)}, u32[]{:S(2)}, u32[]{:S(2)}) collective-permute-start(bf16[2,2,128,128]{3,2,1,0:T(8,128)(2,1)S(1)} %bitcast.89), channel_id=1, source_target_pairs={{0,16},{16,0},{1,17},{17,1},{2,18},{18,2},{3,19},{19,3},{4,20},{20... | collective-permute-start | bytes 393224 | tf_op jit(solution)/shard_map/ppermute | solution.py:39
  140.2 13.8 %slice-start = ((s8[7077888]{0:T(1024)(128)(4,1)}), s8[4194304]{0:T(1024)(128)(4,1)S(1)}, s32[]{:S(2)}) async-start(s8[7077888]{0:T(1024)(128)(4,1)} %bitcast.91), calls=%async_computation.1 | async-start | bytes 8388608
  140.8 13.2 %slice-start.1 = ((s8[7077888]{0:T(1024)(128)(4,1)}), s8[2883584]{0:T(1024)(128)(4,1)S(1)}, s32[]{:S(2)}) async-start(s8[7077888]{0:T(1024)(128)(4,1)} %bitcast.91), calls=%async_computation.2 | async-start | bytes 5767168
  142.7 7.9 %collective-permute-start.20 = (bf16[2,2,128,128]{3,2,1,0:T(8,128)(2,1)S(1)}, bf16[2,2,128,128]{3,2,1,0:T(8,128)(2,1)S(1)}, u32[]{:S(2)}, u32[]{:S(2)}) collective-permute-start(bf16[2,2,128,128]{3,2,1,0:T(8,128)(2,1)S(1)} %collective-permute-done.19), channel_id=1, source_target_pairs={{4,0},{8,4},{12,8},{5,1},{9,5},{13,9},{6,2},{10,6},{14,10},{7,3},{... | collective-permute-start | bytes 393224 | tf_op jit(solution)/shard_map/ppermute | solution.py:29
  144.1 14.0 %copy-start.7 = (bf16[2,2,128,6912]{3,2,1,0:T(8,128)(2,1)}, bf16[2,2,128,6912]{3,2,1,0:T(8,128)(2,1)S(1)}, u32[]{:S(2)}) copy-start(bf16[2,2,128,6912]{3,2,1,0:T(8,128)(2,1)S(1)} %constant_dynamic-update-slice_fusion.85) | copy-start | bytes 21233668
  150.6 7.4 %collective-permute-start.21 = (bf16[4,1,128,128]{3,2,1,0:T(8,128)(2,1)S(1)}, bf16[4,1,128,128]{3,2,1,0:T(8,128)(2,1)S(1)}, u32[]{:S(2)}, u32[]{:S(2)}) collective-permute-start(bf16[4,1,128,128]{3,2,1,0:T(8,128)(2,1)S(1)} %get-tuple-element.92), channel_id=1, source_target_pairs={{0,1},{1,2},{2,3},{4,5},{5,6},{6,7},{8,9},{9,10},{10,11},{12,13},{... | collective-permute-start | bytes 393224 | tf_op jit(solution)/shard_map/ppermute | solution.py:17
  152.8 5.4 %collective-permute-start.22 = (bf16[4,1,128,128]{3,2,1,0:T(8,128)(2,1)S(1)}, bf16[4,1,128,128]{3,2,1,0:T(8,128)(2,1)S(1)}, u32[]{:S(2)}, u32[]{:S(2)}) collective-permute-start(bf16[4,1,128,128]{3,2,1,0:T(8,128)(2,1)S(1)} %get-tuple-element.93), channel_id=1, source_target_pairs={{1,0},{2,1},{3,2},{5,4},{6,5},{7,6},{9,8},{10,9},{11,10},{13,12},{... | collective-permute-start | bytes 393224 | tf_op jit(solution)/shard_map/ppermute | solution.py:19
  158.6 1.5 copy-start.3
  168.3 0.7 copy-start.12
  168.3 1.9 copy-start.2
Sparse Core Ops, SparseCore 0:
  168.5 153.8 all-reduce.11
where the time goes:
time: 334 us; the launch traced here: 332 us
  waiting for transfers between devices  175 us (52%)
  starting transfers between devices  74.1 us (22%)
  local copies, waits for them, and re-layouts  48.6 us (15%)
  between operations  16.4 us (5%)
  matrix products  11.5 us (3%)
  other arithmetic  6.63 us (2%)
    unnamed x2, waiting for transfers between devices  151 us
    unnamed x191, local copies, waits for them, and re-layouts  42.7 us
    ppermute x7, starting transfers between devices, padded_2(): lax.ppermute(tail, axis, [(i, (i + 1) % count) for i in range(ends)])  24.2 us
    ppermute x7, starting transfers between devices, passed_along(): return lax.ppermute(block, axis, route)  22.9 us
    ppermute x2, starting transfers between devices, swapped(): return lax.ppermute(block, axis, route)  17.8 us
    ppermute x7, waiting for transfers between devices, passed_along(): return lax.ppermute(block, axis, route)  13.9 us
    ppermute x7, starting transfers between devices, padded_2(): lax.ppermute(head, axis, [((i + 1) % count, i) for i in range(ends)])  9.23 us
    dot_general x2, matrix products, contract(): lax.dot_general(taps, upstream, (((0,), (0,)), ((), ())), preferred_eleme...  7.25 us
  transfers between devices with their start and end apart: 24, of which 10 were waited for; matrix products, arithmetic and copies ran while one was open for 12% of the time, Pallas kernels for 0%

commit v1 on v0

v1 whole, which is shorter than its diff:
```python
from functools import partial

import jax
import jax.numpy as jnp
from jax import lax
from jax.experimental import pallas as pl
from jax.experimental.pallas import tpu as pltpu
from jax.sharding import PartitionSpec as P

BF = jnp.bfloat16
F32 = jnp.float32
NT = (((1,), (1,)), ((), ()))
TN = (((0,), (0,)), ((), ()))
VMEM_LIMIT = 56 * 1024 * 1024


class Dims:
    def __init__(self, mesh, frames_here, rows_here, width, channels, hidden):
        self.tm, self.rows = mesh["tm"], mesh["rows"]
        self.n = self.tm * self.rows
        self.f_here, self.r_here = frames_here, rows_here
        self.fr = frames_here * rows_here
        self.F, self.H = self.tm * frames_here, self.rows * rows_here
        self.W, self.C, self.D = width, channels, hidden
        self.cell = self.F * self.H
        self.own = width // self.n


def patches(v, dst, at, dims, reverse):
    F, H, c = dims.F, dims.H, v.shape[1]
    v = v.reshape(F, H, c)
    row = lax.broadcasted_iota(jnp.int32, v.shape, 1)
    for i in range(3):
        d = 1 - i if reverse else i - 1
        if d == 1:
            s = jnp.where(row == H - 1, 0.0, pltpu.roll(v, H - 1, 1))
        elif d == -1:
            s = jnp.where(row == 0, 0.0, pltpu.roll(v, 1, 1))
        else:
            s = v
        for t in range(3):
            m = 2 - t
            if m == 0:
                moved = s
            elif reverse:
                moved = jnp.concatenate([s[m:], jnp.zeros((m, H, c), F32)], axis=0)
            else:
                moved = jnp.concatenate([jnp.zeros((m, H, c), F32), s[: F - m]], axis=0)
            lane = (3 * t + i) * c
            dst[at * dims.cell : (at + 1) * dims.cell, lane : lane + c] = moved.reshape(
                F * H, c
            ).astype(BF)


def taps_of(k_ref, j, rows, axis):
    return jnp.concatenate(
        [k_ref[(3 * ti + j) * rows : (3 * ti + j + 1) * rows, :] for ti in range(9)], axis=axis
    )


def conv(p_ref, k_ref, columns, c, cell, acc_ref):
    for j in range(3):
        part = jnp.dot(
            p_ref[j * cell : (j + columns) * cell, : 9 * c],
            taps_of(k_ref, j, c, 0),
            preferred_element_type=F32,
        )
        rows = slice(0, columns * cell)
        if j == 0:
            acc_ref[rows, :] = part
        else:
            acc_ref[rows, :] += part


def conv_back(p_ref, k_ref, columns, c, c_out, cell, acc_ref):
    for j in range(3):
        part = lax.dot_general(
            p_ref[(2 - j) * cell : (2 - j + columns) * cell, : 9 * c],
            taps_of(k_ref, j, c_out, 1),
            NT,
            preferred_element_type=F32,
        )
        rows = slice(0, columns * cell)
        if j == 0:
            acc_ref[rows, :] = part
        else:
            acc_ref[rows, :] += part


def inside(meta, w, halo, dims):
    col = meta[1] * dims.own + (w - halo)
    return jnp.logical_and(col >= 0, col < dims.W)


def sigmoid(h):
    return 1.0 / (1.0 + jnp.exp(-h))


def gate(d, h):
    s = sigmoid(h)
    return d * s * (1.0 + h * (1.0 - s))


def pack_kernel(dims, meta, x_ref, g_ref, out_ref, pad, buf):
    n_cols = dims.own + 10
    pad[...] = jnp.zeros_like(pad)

    @pl.when(meta[0] == 0)
    def _():
        pad[:, 8 : 8 + dims.W, :] = x_ref[...].astype(F32)

    @pl.when(meta[0] != 0)
    def _():
        pad[:, 8 : 8 + dims.W, :] = g_ref[...].astype(F32)

    for k in range(dims.n):
        start = k * dims.own + 3
        for q in range(dims.fr):
            buf[k, q * n_cols : (q + 1) * n_cols, :] = pad[q, start : start + n_cols, :]
    out_ref[...] = buf[...].astype(BF)


def first_kernel(
    dims, meta, recv, kin_any, kout_any, slab_out, x1_out, hd_out, a_out,
    kin, kout, rbuf, slab, p1, p2, h_ref, y_ref, sems,
):
    cell, own, C, D = dims.cell, dims.own, dims.C, dims.D
    load_in = pltpu.make_async_copy(kin_any, kin, sems.at[0])
    load_out = pltpu.make_async_copy(kout_any, kout, sems.at[1])
    load_in.start()
    load_out.start()
    n_cols = own + 10
    rbuf[...] = recv[...].astype(F32)
    for s in range(dims.n):
        i, j = s // dims.rows, s % dims.rows
        for q in range(dims.fr):
            f, r = i * dims.f_here + q // dims.r_here, j * dims.r_here + q % dims.r_here
            slab[pl.ds(f * dims.H + r, n_cols, stride=cell), :] = rbuf[
                s, q * n_cols : (q + 1) * n_cols, :
            ]
    slab_out[...] = slab[4 * cell : (6 + own) * cell, :].astype(BF)

    @pl.when(meta[0] == 0)
    def _():
        for w in range(n_cols):
            patches(slab[w * cell : (w + 1) * cell, :], p1, w, dims, False)
        load_in.wait()
        conv(p1, kin, own + 8, C, cell, h_ref)
        hd_out[...] = h_ref[2 * cell : (6 + own) * cell, :]
        for w in range(own + 8):
            h = h_ref[w * cell : (w + 1) * cell, :]
            a = jnp.where(inside(meta, w, 4, dims), h * sigmoid(h), 0.0)
            if 3 <= w < 5 + own:
                a_out[(w - 3) * cell : (w - 2) * cell, :] = a.astype(BF)
            patches(a, p2, w, dims, False)
        load_out.wait()
        conv(p2, kout, own + 6, D, cell, y_ref)
        for w in range(own + 6):
            v = slab[(w + 2) * cell : (w + 3) * cell, :] + y_ref[w * cell : (w + 1) * cell, :]
            x1_out[w * cell : (w + 1) * cell, :] = jnp.where(
                inside(meta, w, 3, dims), v, 0.0
            ).astype(BF)

    @pl.when(meta[0] != 0)
    def _():
        for w in range(own + 6):
            patches(slab[(w + 2) * cell : (w + 3) * cell, :], p1, w, dims, True)
        load_in.wait()
        load_out.wait()
        conv_back(p1, kout, own + 4, C, D, cell, h_ref)
        hd_out[...] = h_ref[: (own + 4) * cell, :]
        x1_out[...] = jnp.zeros_like(x1_out)
        a_out[...] = jnp.zeros_like(a_out)


def second_kernel(
    dims, meta, x1, hd, gslab, a_in, kin_any, g0_out, a_out, e_out,
    kin, p1, p2, h_ref, y_ref, sems,
):
    cell, own, C, D = dims.cell, dims.own, dims.C, dims.D

    @pl.when(meta[0] == 0)
    def _():
        a_out[...] = a_in[...]
        g0_out[...] = jnp.zeros_like(g0_out)
        e_out[...] = jnp.zeros_like(e_out)

    @pl.when(meta[0] != 0)
    def _():
        load_in = pltpu.make_async_copy(kin_any, kin, sems.at[0])
        load_in.start()
        for w in range(own + 6):
            patches(x1[w * cell : (w + 1) * cell, :].astype(F32), p1, w, dims, False)
        load_in.wait()
        conv(p1, kin, own + 4, C, cell, h_ref)
        for w in range(own + 4):
            rows = slice(w * cell, (w + 1) * cell)
            h = h_ref[rows, :]
            if 1 <= w < 3 + own:
                a = jnp.where(inside(meta, w, 2, dims), h * sigmoid(h), 0.0)
                a_out[(w - 1) * cell : w * cell, :] = a.astype(BF)
            e = jnp.where(inside(meta, w, 2, dims), gate(hd[rows, :], h), 0.0)
            if 2 <= w < 2 + own:
                e_out[(w - 2) * cell : (w - 1) * cell, :] = e.astype(BF)
            patches(e, p2, w, dims, True)
        conv_back(p2, kin, own + 2, D, C, cell, y_ref)
        for w in range(own + 2):
            rows = slice(w * cell, (w + 1) * cell)
            v = gslab[rows, :].astype(F32) + y_ref[rows, :]
            g0_out[rows, :] = jnp.where(inside(meta, w, 1, dims), v, 0.0).astype(BF)


def third_kernel(
    dims, meta, g0, hd, x1, a_in, e_in, kout_any, e_out, sec_out,
    kout, p2, h_ref, y_ref, sems,
):
    cell, own, C, D = dims.cell, dims.own, dims.C, dims.D
    load_out = pltpu.make_async_copy(kout_any, kout, sems.at[0])
    load_out.start()

    @pl.when(meta[0] == 0)
    def _():
        for w in range(own + 2):
            patches(g0[w * cell : (w + 1) * cell, :].astype(F32), p2, w, dims, True)
        load_out.wait()
        conv_back(p2, kout, own, C, D, cell, h_ref)
        for w in range(own):
            rows = slice(w * cell, (w + 1) * cell)
            e_out[rows, :] = gate(
                h_ref[rows, :], hd[(w + 2) * cell : (w + 3) * cell, :]
            ).astype(BF)
        sec_out[...] = x1[3 * cell : (3 + own) * cell, :]

    @pl.when(meta[0] != 0)
    def _():
        for w in range(own + 2):
            patches(a_in[w * cell : (w + 1) * cell, :].astype(F32), p2, w, dims, False)
        load_out.wait()
        conv(p2, kout, own, D, cell, y_ref)
        sec_out[...] = (
            x1[3 * cell : (3 + own) * cell, :].astype(F32) + y_ref[: own * cell, :]
        ).astype(BF)
        e_out[...] = e_in[...]


def grad_kernel(dims, c, v_ref, u_ref, out_ref, p):
    cell, own = dims.cell, dims.own
    for w in range(own + 2):
        patches(v_ref[w * cell : (w + 1) * cell, :].astype(F32), p, w, dims, False)
    for j in range(3):
        g = lax.dot_general(
            p[j * cell : (j + own) * cell, :], u_ref[...], TN, preferred_element_type=F32
        )
        for ti in range(9):
            out_ref[(3 * ti + j) * c : (3 * ti + j + 1) * c, :] = g[ti * c : (ti + 1) * c, :]


def call(kernel, shapes, ins, scratch, cost, name):
    return pl.pallas_call(
        kernel,
        out_shape=shapes,
        in_specs=ins,
        out_specs=jax.tree.map(lambda _: pl.BlockSpec(memory_space=pltpu.VMEM), shapes),
        scratch_shapes=scratch,
        compiler_params=pltpu.CompilerParams(vmem_limit_bytes=VMEM_LIMIT),
        cost_estimate=pl.CostEstimate(flops=cost, bytes_accessed=4 << 20, transcendentals=0),
        name=name,
    )


def halved(parts, axis, mine, bit, dim, apart):
    count = lax.axis_size(axis)
    flag = mine == 1
    low = lax.index_in_dim(parts, 0, dim, keepdims=False)
    high = lax.index_in_dim(parts, 1, dim, keepdims=False)
    send = jnp.where(flag, low, high).astype(BF)
    keep = jnp.where(flag, high, low)
    got = lax.ppermute(send, axis, [(i, i ^ apart) for i in range(count)])
    return keep + got.astype(F32)


def reduce_scatter(parts, dims):
    m = parts.shape[0] // dims.n
    order = []
    for axis, size in (("rows", dims.rows), ("tm", dims.tm)):
        apart = 1
        while apart < size:
            order.append((axis, apart))
            apart *= 2
    tm_bits = dims.tm.bit_length() - 1
    row_bits = dims.rows.bit_length() - 1
    names = [("tm", 1 << b) for b in reversed(range(tm_bits))]
    names += [("rows", 1 << b) for b in reversed(range(row_bits))]
    parts = parts.reshape((2,) * len(names) + (m, 128))
    for axis, apart in order:
        dim = names.index((axis, apart))
        mine = (lax.axis_index(axis) // apart) % 2
        parts = halved(parts, axis, mine, None, dim, apart)
        names.pop(dim)
    return parts


def on_device(shape, input_clip, cotangent, kernel_in, kernel_out):
    f_here, r_here, W, C = input_clip.shape
    D = kernel_in.shape[2]
    dims = Dims(shape, f_here, r_here, W, C, D)
    own, cell, n = dims.own, dims.cell, dims.n
    kin, kout = kernel_in[0], kernel_out[0]
    role = lax.axis_index("segment")
    k = lax.axis_index("tm") * dims.rows + lax.axis_index("rows")
    meta = jnp.stack([role, k]).astype(jnp.int32)
    smem = pl.BlockSpec(memory_space=pltpu.SMEM)
    vm = pl.BlockSpec(memory_space=pltpu.VMEM)
    hbm = pl.BlockSpec(memory_space=pl.ANY)
    sds = jax.ShapeDtypeStruct
    n_cols = own + 10
    fr = dims.fr
    conv_flops = 2 * 27 * C * D * cell

    send = call(
        partial(pack_kernel, dims), sds((n, fr * n_cols, C), BF), [smem, vm, vm],
        [pltpu.VMEM((fr, W + 16, C), F32), pltpu.VMEM((n, fr * n_cols, C), F32)], 0, "pack",
    )(meta, input_clip.reshape(fr, W, C), cotangent.reshape(fr, W, C))
    recv = lax.all_to_all(send, ("tm", "rows"), 0, 0)

    slab, x1, hd, a0 = call(
        partial(first_kernel, dims),
        (
            sds(((own + 2) * cell, C), BF), sds(((own + 6) * cell, C), BF),
            sds(((own + 4) * cell, D), F32), sds(((own + 2) * cell, D), BF),
        ),
        [smem, vm, hbm, hbm],
        [
            pltpu.VMEM(kin.shape, BF), pltpu.VMEM(kout.shape, BF),
            pltpu.VMEM((n, fr * n_cols, C), F32), pltpu.VMEM((n_cols * cell, C), F32),
            pltpu.VMEM((n_cols * cell, 9 * C), BF), pltpu.VMEM(((own + 8) * cell, 9 * D), BF),
            pltpu.VMEM(((own + 8) * cell, D), F32), pltpu.VMEM(((own + 6) * cell, C), F32),
            pltpu.SemaphoreType.DMA((2,)),
        ],
        conv_flops * 2 * (own + 7), "first",
    )(meta, recv, kin, kout)

    swap = [(0, 1), (1, 0)]
    x1_there = lax.ppermute(x1, "segment", swap)

    g0_here, a, e1 = call(
        partial(second_kernel, dims),
        (
            sds(((own + 2) * cell, C), BF), sds(((own + 2) * cell, D), BF),
            sds((own * cell, D), BF),
        ),
        [smem, vm, vm, vm, vm, hbm],
        [
            pltpu.VMEM(kin.shape, BF),
            pltpu.VMEM(((own + 6) * cell, 9 * C), BF), pltpu.VMEM(((own + 4) * cell, 9 * D), BF),
            pltpu.VMEM(((own + 4) * cell, D), F32), pltpu.VMEM(((own + 2) * cell, C), F32),
            pltpu.SemaphoreType.DMA((1,)),
        ],
        conv_flops * 2 * (own + 3), "second",
    )(meta, x1_there, hd, slab, a0, kin)

    g0_there = lax.ppermute(g0_here, "segment", swap)
    on_encoder = role == 0
    x_here = jnp.where(on_encoder, x1, x1_there)

    e, sec = call(
        partial(third_kernel, dims),
        (sds((own * cell, D), BF), sds((own * cell, C), BF)),
        [smem, vm, vm, vm, vm, vm, hbm],
        [
            pltpu.VMEM(kout.shape, BF), pltpu.VMEM(((own + 2) * cell, 9 * D), BF),
            pltpu.VMEM((own * cell, D), F32), pltpu.VMEM((own * cell, C), F32),
            pltpu.SemaphoreType.DMA((1,)),
        ],
        conv_flops * own, "third",
    )(meta, g0_there, hd, x_here, a, e1, kout)

    g = jnp.where(on_encoder, g0_there, slab)[cell : (1 + own) * cell]
    x = jnp.where(on_encoder, slab, x1_there[2 * cell : (4 + own) * cell])

    def grad(c, c_out, v, u, name):
        return call(
            partial(grad_kernel, dims, c), sds((27 * c, c_out), F32), [vm, vm],
            [pltpu.VMEM(((own + 2) * cell, 9 * c), BF)], conv_flops * own, name,
        )(v, u)

    out_part = grad(D, C, a, g, "grad_out")
    in_part = grad(C, D, x, e, "grad_in")
    out_sum = reduce_scatter(out_part.reshape(-1, 128), dims).reshape(-1)
    in_sum = reduce_scatter(in_part.reshape(-1, 128), dims).reshape(-1)

    back = sec.reshape(own, dims.tm, f_here, dims.rows, r_here, C)
    back = back.transpose(1, 3, 2, 4, 0, 5).reshape(n, fr * own, C)
    back = lax.all_to_all(back, ("tm", "rows"), 0, 0)
    sections = back.reshape(n, fr, own, C).transpose(1, 0, 2, 3).reshape(f_here, r_here, W, C)
    return sections[None], in_sum[None], out_sum[None]


def solution(mesh):
    in_specs = (
        P("tm", "rows", None, None),
        P("tm", "rows", None, None),
        P("segment", None, None),
        P("segment", None, None),
    )
    out_specs = (
        P("segment", "tm", "rows", None, None),
        P("segment", ("tm", "rows")),
        P("segment", ("tm", "rows")),
    )
    return jax.shard_map(
        partial(on_device, dict(mesh.shape)), mesh=mesh, in_specs=in_specs,
        out_specs=out_specs, check_vma=False,
    )
```

time: 334 us -> 137 us (0.41)
  waiting for transfers between devices: 175 us -> 33.9 us
  starting transfers between devices: 74.1 us -> 23.8 us
  local copies, waits for them, and re-layouts: 48.6 us -> 15.7 us
  Pallas kernels: 0 us -> 31.3 us
  blocking collectives: 0 us -> 18 us
  between operations: 16.4 us -> 0.88 us
  matrix products: 11.5 us -> 0 us
  other arithmetic: 6.63 us -> 12.9 us
    unnamed x2 -> x0, waiting for transfers between devices: 151 us -> none
    ppermute x23 -> x10, starting transfers between devices: 74 us -> 19.5 us  [the longest x8 10.5 us: halved(): got = lax.ppermute(send, axis, [(i, i ^ apart) for i in range(count)])]
    unnamed x191 -> x16, local copies, waits for them, and re-layouts: 42.7 us -> 1.4 us
    pallas_call x0 -> x6, Pallas kernels: none -> 31.3 us  [the longest x1 13.3 us: on_device(): call(partial(first_kernel, dims), (sds(((own + 2) * cell, C), BF), sds(((...]
    all_to_all x0 -> x1, blocking collectives: none -> 18 us  [on_device(): recv = lax.all_to_all(send, ('tm', 'rows'), 0, 0)]
    dot_general x5 -> x0, matrix products: 11.5 us -> none  [the longest x2 7.25 us: contract(): lax.dot_general(taps, upstream, (((0,), (0,)), ((), ())), preferred_eleme...]
    ppermute x23 -> x10, waiting for transfers between devices: 23.6 us -> 33.9 us  [the longest x8 24.8 us: halved(): got = lax.ppermute(send, axis, [(i, i ^ apart) for i in range(count)])]
    slice x4 -> x3, local copies, waits for them, and re-layouts: 0.08 us -> 6.42 us  [halved(): low = lax.index_in_dim(parts, 0, dim, keepdims=False)]
  transfers between devices with their start and end apart: 24 -> 11, of which waited for: 10 -> 6; matrix products, arithmetic and copies ran while one was open for 12% -> 18% of each run, Pallas kernels for 0% -> 6%
where the time goes in v1:
time: 137 us
  waiting for transfers between devices  33.9 us (25%)
  Pallas kernels  31.3 us (23%)
  starting transfers between devices  23.8 us (17%)
  blocking collectives  18 us (13%)
  local copies, waits for them, and re-layouts  15.7 us (11%)
  other arithmetic  12.9 us (9%)
    ppermute x8, waiting for transfers between devices, halved(): got = lax.ppermute(send, axis, [(i, i ^ apart) for i in range(count)])  24.8 us
    all_to_all x1, blocking collectives, on_device(): recv = lax.all_to_all(send, ('tm', 'rows'), 0, 0)  18 us
    pallas_call x1, Pallas kernels, on_device(): call(partial(first_kernel, dims), (sds(((own + 2) * cell, C), BF), sds(((...  13.3 us
    ppermute x8, starting transfers between devices, halved(): got = lax.ppermute(send, axis, [(i, i ^ apart) for i in range(count)])  10.5 us
    ppermute x1, starting transfers between devices, on_device(): g0_there = lax.ppermute(g0_here, 'segment', swap)  8.86 us
    pallas_call x2, Pallas kernels, grad(): call(partial(grad_kernel, dims, c), sds((27 * c, c_out), F32), [vm, vm],...  8.85 us
    ppermute x1, waiting for transfers between devices, on_device(): x1_there = lax.ppermute(x1, 'segment', swap)  7.51 us
    slice x3, local copies, waits for them, and re-layouts, halved(): low = lax.index_in_dim(parts, 0, dim, keepdims=False)  6.42 us
  transfers between devices with their start and end apart: 11, of which 6 were waited for; matrix products, arithmetic and copies ran while one was open for 18% of the time, Pallas kernels for 6%

profile of v1, /device:TPU:0, one launch (start us, length us, event | category | flops | bytes accessed | tf_op | source)
XLA Modules:
  0.0 136.5 jit_solution(1219798154976645574)
XLA Ops:
  0.6 0.7 pad_add_fusion.meta
  1.3 1.8 %pack.1 = bf16[16,72,128]{2,1,0:T(8,128)(2,1)} custom-call(s32[2]{0:T(128)} %pad_add_fusion.meta, bf16[4,128,128]{2,1,0:T(8,128)(2,1)} %bitcast.73, bf16[4,128,128]{2,1,0:T(8,128)(2,1)} %bitcast.74), custom_call_target="tpu_custom_call" | custom-call | bytes 4194304 | tf_op jit(solution)/shard_map/pack/pallas_call | solution.py:320
  3.1 18.0 %all_to_all.10.recv = bf16[16,72,128]{2,1,0:T(8,128)(2,1)} all-to-all(bf16[16,72,128]{2,1,0:T(8,128)(2,1)} %pack.1), channel_id=1, replica_groups=mesh['segment'=2,'tm'=4,'rows'=4] {'tm','rows'}, dimensions={0} | all-to-all | bytes 589824 | tf_op jit(solution)/shard_map/all_to_all | solution.py:324
  21.1 13.3 %first.1 = (bf16[640,128]{1,0:T(8,128)(2,1)}, bf16[896,128]{1,0:T(8,128)(2,1)}, f32[768,256]{1,0:T(8,128)}, bf16[640,256]{1,0:T(8,128)(2,1)}) custom-call(s32[2]{0:T(128)} %pad_add_fusion.meta, bf16[16,72,128]{2,1,0:T(8,128)(2,1)} %all_to_all.10.recv, bf16[3456,256]{1,0:T(8,128)(2,1)} %bitcast.77, bf16[6912,128]{1,0:T(8,128)(2,1)} %bitcast.69), custom_call_target="tpu_custom_call" | custom-call | flops 3397386240 | bytes 4194304 | tf_op jit(solution)/shard_map/first/pallas_call | solution.py:326
  34.5 0.1 collective-permute-start
  34.6 7.5 %collective-permute-done.x1 = bf16[896,128]{1,0:T(8,128)(2,1)S(1)} collective-permute-done((bf16[896,128]{1,0:T(8,128)(2,1)}, bf16[896,128]{1,0:T(8,128)(2,1)S(1)}, u32[]{:S(2)}, u32[]{:S(2)}) %collective-permute-start) | collective-permute-done | bytes 229408 | tf_op jit(solution)/shard_map/ppermute | solution.py:344
  42.1 0.0 copy-start.2
  42.1 0.7 copy-done.2
  42.8 0.0 copy-start.7
  42.8 0.0 copy-start.3
  42.8 2.5 %second.1 = (bf16[640,128]{1,0:T(8,128)(2,1)}, bf16[640,256]{1,0:T(8,128)(2,1)}, bf16[512,256]{1,0:T(8,128)(2,1)}) custom-call(s32[2]{0:T(128)} %pad_add_fusion.meta, bf16[896,128]{1,0:T(8,128)(2,1)} %copy-done.2, f32[768,256]{1,0:T(8,128)} %get-tuple-element.13.hd, bf16[640,128]{1,0:T(8,128)(2,1)} %get-tuple-element.14.gslab, ...), custom_call_target="tpu_custom_call" | custom-call | flops 2491416576 | bytes 4194304 | tf_op jit(solution)/shard_map/second/pallas_call | solution.py:346
  45.4 8.9 %collective-permute-start.1 = (bf16[640,128]{1,0:T(8,128)(2,1)}, bf16[640,128]{1,0:T(8,128)(2,1)S(1)}, u32[]{:S(2)}, u32[]{:S(2)}) collective-permute-start(bf16[640,128]{1,0:T(8,128)(2,1)} %get-tuple-element.16), channel_id=1, source_target_pairs={{0,16},{16,0},{1,17},{17,1},{2,18},{18,2},{3,19},{19,3},{4,20},{20... | collective-permute-start | bytes 491528 | tf_op jit(solution)/shard_map/ppermute | solution.py:362
  54.2 0.0 copy-done.7
  54.2 0.7 broadcast_select_fusion.x1
  54.9 0.0 copy-done.3
  54.9 1.6 %slice_select_fusion.v_ref = bf16[640,128]{1,0:T(8,128)(2,1)} fusion(bf16[640,128]{1,0:T(8,128)(2,1)S(1)} %copy-done.3, bf16[896,128]{1,0:T(8,128)(2,1)} %copy-done.2, pred[]{:T(512)S(6)} %eq.28), kind=kLoop, calls=%fused_computation.29 | loop fusion | flops 81920 | bytes 491521 | tf_op jit(solution)/shard_map/jit(_where)/select_n | solution.py:379
  56.5 1.6 %collective-permute-done.1.g0 = bf16[640,128]{1,0:T(8,128)(2,1)S(1)} collective-permute-done((bf16[640,128]{1,0:T(8,128)(2,1)}, bf16[640,128]{1,0:T(8,128)(2,1)S(1)}, u32[]{:S(2)}, u32[]{:S(2)}) %collective-permute-start.1) | collective-permute-done | bytes 163872 | tf_op jit(solution)/shard_map/ppermute | solution.py:362
  58.1 0.7 copy-done.5
  58.8 4.9 %third.1 = (bf16[512,256]{1,0:T(8,128)(2,1)}, bf16[512,128]{1,0:T(8,128)(2,1)}) custom-call(s32[2]{0:T(128)} %pad_add_fusion.meta, bf16[640,128]{1,0:T(8,128)(2,1)} %copy-done.5, f32[768,256]{1,0:T(8,128)} %get-tuple-element.13.hd, bf16[896,128]{1,0:T(8,128)(2,1)} %broadcast_select_fusion.x1, bf16[640,256]{1,0:T(8,128)(2,1)} %get-tuple-element.17.a_in.v_ref, ...), custom_call_target="tpu_custom_call" | custom-call | flops 905969664 | bytes 4194304 | tf_op jit(solution)/shard_map/third/pallas_call | solution.py:366
  63.7 1.7 %copy.40 = bf16[8,4,2,4,2,128]{5,0,4,2,3,1:T(8,128)(2,1)} copy(bf16[8,4,2,4,2,128]{5,4,3,2,1,0:T(2,128)(2,1)} %bitcast.76) | data formatting | bytes 262144 | tf_op jit(solution)/shard_map/reshape | solution.py:392
  65.4 4.4 %all-to-all-start.1 = ((bf16[16,32,128]{2,1,0:T(8,128)(2,1)}), bf16[16,32,128]{2,1,0:T(8,128)(2,1)}, u32[]{:S(2)}, u32[]{:S(2)}) async-start(bf16[16,32,128]{2,1,0:T(8,128)(2,1)} %bitcast.8), calls=%async_computation.1 | async-start | bytes 262144 | tf_op jit(solution)/shard_map/all_to_all | solution.py:394
  69.8 4.0 %grad_in.1 = f32[3456,256]{1,0:T(8,128)} custom-call(bf16[640,128]{1,0:T(8,128)(2,1)} %slice_select_fusion.v_ref, bf16[512,256]{1,0:T(8,128)(2,1)} %get-tuple-element.20.u_ref), custom_call_target="tpu_custom_call" | custom-call | flops 905969664 | bytes 4194304 | tf_op jit(solution)/shard_map/grad_in/pallas_call | solution.py:382
  73.8 4.6 %reshape_reshape.3 = f32[2,2,2,2,432,128]{5,4,3,2,1,0:T(8,128)} reshape(f32[3456,256]{1,0:T(8,128)} %grad_in.1) | data formatting | bytes 7077888 | tf_op jit(solution)/shard_map/reshape;reshape | solution.py:294
  78.4 2.3 %fusion.13 = (f32[2,2,2,1,432,128]{5,4,3,2,1,0:T(8,128)S(1)}, f32[2,2,2,1,432,128]{5,4,3,2,1,0:T(8,128)S(1)}) fusion(f32[2,2,2,2,432,128]{5,4,3,2,1,0:T(8,128)} %reshape_reshape.3), kind=kLoop, calls=%fused_computation.35 | loop fusion | bytes 7077888 | tf_op jit(solution)/shard_map/slice | solution.py:274
  80.6 0.0 copy-start.4
  80.7 0.0 copy-start.6
  80.7 1.1 fusion.1
  81.7 0.0 collective-permute-start.2
  81.7 0.0 copy-done.4
  81.7 0.0 copy-done.6
  81.8 0.7 slice_select_fusion.1.u_ref
  82.4 4.8 %grad_out.1 = f32[6912,128]{1,0:T(8,128)} custom-call(bf16[640,256]{1,0:T(8,128)(2,1)} %get-tuple-element.17.a_in.v_ref, bf16[512,128]{1,0:T(8,128)(2,1)} %slice_select_fusion.1.u_ref), custom_call_target="tpu_custom_call" | custom-call | flops 905969664 | bytes 4194304 | tf_op jit(solution)/shard_map/grad_out/pallas_call | solution.py:382
  87.2 3.1 %fusion.2 = bf16[2,2,2,432,128]{4,3,2,1,0:T(8,128)(2,1)} fusion(pred[]{:T(512)S(6)} %eq.32, f32[2,2,2,2,432,128]{5,4,3,2,1,0:T(8,128)} %bitcast.67), kind=kLoop, calls=%fused_computation.7 | loop fusion | flops 442368 | bytes 2654209 | tf_op jit(solution)/shard_map/convert_element_type | solution.py:276
  90.3 0.5 collective-permute-start.6
  90.8 4.0 %fusion.12 = (f32[2,2,2,1,432,128]{5,4,3,2,1,0:T(8,128)}, f32[2,2,2,1,432,128]{5,4,3,2,1,0:T(8,128)}) fusion(f32[2,2,2,2,432,128]{5,4,3,2,1,0:T(8,128)} %bitcast.68), kind=kLoop, calls=%fused_computation.34 | loop fusion | bytes 7077888 | tf_op jit(solution)/shard_map/slice | solution.py:274
  94.9 0.0 all-to-all-done.1
  94.9 1.6 %copy.41 = bf16[4,16,8,128]{3,2,1,0:T(8,128)(2,1)} copy(bf16[4,16,8,128]{3,2,0,1:T(8,128)(2,1)} %bitcast.10) | data formatting | bytes 262144 | tf_op jit(solution)/shard_map/transpose | solution.py:395
  96.5 0.0 collective-permute-done.2
  96.5 1.5 %bitcast_add_fusion = f32[2,2,2,432,128]{4,3,0,1,2:T(8,128)S(1)} fusion(bf16[2,2,2,432,128]{4,3,0,1,2:T(8,128)(2,1)} %collective-permute-done.2, f32[2,2,2,1,432,128]{5,4,3,2,1,0:T(8,128)S(1)} %get-tuple-element.23, f32[2,2,2,1,432,128]{5,4,3,2,1,0:T(8,128)S(1)} %get-tuple-element.24, pred[]{:T(512)S(6)} %eq.32), kind=kLoop, calls=%fused_computation.2 | loop fusion | flops 1327104 | bytes 6193153 | tf_op jit(solution)/shard_map/add | solution.py:279
  98.0 0.1 fusion.4
  98.1 1.6 %collective-permute-start.3 = (bf16[2,2,432,128]{3,2,0,1:T(8,128)(2,1)S(1)}, bf16[2,2,432,128]{3,2,0,1:T(8,128)(2,1)S(1)}, u32[]{:S(2)}, u32[]{:S(2)}) collective-permute-start(bf16[2,2,432,128]{3,2,0,1:T(8,128)(2,1)S(1)} %fusion.4), channel_id=1, source_target_pairs={{0,2},{1,3},{2,0},{3,1},{4,6},{5,7},{6,4},{7,5},{8,10},{9,11},{10,... | collective-permute-start | bytes 1327112 | tf_op jit(solution)/shard_map/ppermute | solution.py:278
  99.7 0.0 collective-permute-done.6
  99.7 0.0 copy-done
  99.7 0.0 copy-done.1
  99.7 1.4 %copy_add_fusion = f32[2,2,2,432,128]{4,3,2,1,0:T(8,128)S(1)} fusion(bf16[2,2,2,432,128]{4,3,2,1,0:T(8,128)(2,1)} %collective-permute-done.6, f32[2,2,2,1,432,128]{5,4,3,2,1,0:T(8,128)S(1)} %copy-done.1, f32[2,2,2,1,432,128]{5,4,3,2,1,0:T(8,128)S(1)} %copy-done, pred[]{:T(512)S(6)} %eq.32), kind=kLoop, calls=%fused_computation.3 | loop fusion | flops 1327104 | bytes 6193153 | tf_op jit(solution)/shard_map/add | solution.py:279
  101.1 0.1 fusion.5
  101.2 0.6 collective-permute-start.7
  101.9 0.1 fusion.14
  102.0 9.2 %collective-permute-done.3 = bf16[2,2,432,128]{3,2,0,1:T(8,128)(2,1)S(1)} collective-permute-done((bf16[2,2,432,128]{3,2,0,1:T(8,128)(2,1)S(1)}, bf16[2,2,432,128]{3,2,0,1:T(8,128)(2,1)S(1)}, u32[]{:S(2)}, u32[]{:S(2)}) %collective-permute-start.3) | collective-permute-done | bytes 442400 | tf_op jit(solution)/shard_map/ppermute | solution.py:278
  111.2 0.1 bitcast_add_fusion.1
  111.4 1.7 %collective-permute-start.4 = (bf16[2,432,128]{2,1,0:T(8,128)(2,1)S(1)}, bf16[2,432,128]{2,1,0:T(8,128)(2,1)S(1)}, u32[]{:S(2)}, u32[]{:S(2)}) collective-permute-start(bf16[2,432,128]{2,1,0:T(8,128)(2,1)S(1)} %fusion.8), channel_id=1, source_target_pairs={{0,4},{4,0},{8,12},{12,8},{1,5},{5,1},{9,13},{13,9},{2,6},{6,2},{1... | collective-permute-start | bytes 663560 | tf_op jit(solution)/shard_map/ppermute | solution.py:278
  113.1 6.6 %collective-permute-done.7 = bf16[2,2,432,128]{3,2,1,0:T(8,128)(2,1)S(1)} collective-permute-done((bf16[2,2,432,128]{3,2,1,0:T(8,128)(2,1)S(1)}, bf16[2,2,432,128]{3,2,1,0:T(8,128)(2,1)S(1)}, u32[]{:S(2)}, u32[]{:S(2)}) %collective-permute-start.7) | collective-permute-done | bytes 442400 | tf_op jit(solution)/shard_map/ppermute | solution.py:278
  119.7 0.1 copy_add_fusion.1
  119.9 1.8 %collective-permute-start.8 = (bf16[2,432,128]{2,1,0:T(8,128)(2,1)S(1)}, bf16[2,432,128]{2,1,0:T(8,128)(2,1)S(1)}, u32[]{:S(2)}, u32[]{:S(2)}) collective-permute-start(bf16[2,432,128]{2,1,0:T(8,128)(2,1)S(1)} %fusion.9), channel_id=1, source_target_pairs={{0,4},{4,0},{8,12},{12,8},{1,5},{5,1},{9,13},{13,9},{2,6},{6,2},{1... | collective-permute-start | bytes 663560 | tf_op jit(solution)/shard_map/ppermute | solution.py:278
  121.6 0.0 collective-permute-done.4
  121.6 0.1 bitcast_add_fusion.2
  121.7 2.5 %collective-permute-start.5 = (bf16[432,128]{1,0:T(8,128)(2,1)S(1)}, bf16[432,128]{1,0:T(8,128)(2,1)S(1)}, u32[]{:S(2)}, u32[]{:S(2)}) collective-permute-start(bf16[432,128]{1,0:T(8,128)(2,1)S(1)} %fusion.10), channel_id=1, source_target_pairs={{0,8},{4,12},{8,0},{12,4},{1,9},{5,13},{9,1},{13,5},{2,10},{6,14},... | collective-permute-start | bytes 331784 | tf_op jit(solution)/shard_map/ppermute | solution.py:278
  124.2 4.6 %collective-permute-done.8 = bf16[2,432,128]{2,1,0:T(8,128)(2,1)S(1)} collective-permute-done((bf16[2,432,128]{2,1,0:T(8,128)(2,1)S(1)}, bf16[2,432,128]{2,1,0:T(8,128)(2,1)S(1)}, u32[]{:S(2)}, u32[]{:S(2)}) %collective-permute-start.8) | collective-permute-done | bytes 221216 | tf_op jit(solution)/shard_map/ppermute | solution.py:278
  128.8 0.1 fusion.7
  128.9 1.8 %collective-permute-start.9 = (bf16[432,128]{1,0:T(8,128)(2,1)S(1)}, bf16[432,128]{1,0:T(8,128)(2,1)S(1)}, u32[]{:S(2)}, u32[]{:S(2)}) collective-permute-start(bf16[432,128]{1,0:T(8,128)(2,1)S(1)} %fusion.11), channel_id=1, source_target_pairs={{0,8},{4,12},{8,0},{12,4},{1,9},{5,13},{9,1},{13,5},{2,10},{6,14},... | collective-permute-start | bytes 331784 | tf_op jit(solution)/shard_map/ppermute | solution.py:278
  130.8 0.0 collective-permute-done.5
  130.8 0.7 bitcast_add_fusion.4
  131.5 4.3 %collective-permute-done.9 = bf16[432,128]{1,0:T(8,128)(2,1)S(1)} collective-permute-done((bf16[432,128]{1,0:T(8,128)(2,1)S(1)}, bf16[432,128]{1,0:T(8,128)(2,1)S(1)}, u32[]{:S(2)}, u32[]{:S(2)}) %collective-permute-start.9) | collective-permute-done | bytes 110624 | tf_op jit(solution)/shard_map/ppermute | solution.py:278
  135.8 0.7 bitcast_add_fusion.3
  (7 shorter events, 0.1 us)
Async XLA Ops:
  34.5 7.7 %collective-permute-start = (bf16[896,128]{1,0:T(8,128)(2,1)}, bf16[896,128]{1,0:T(8,128)(2,1)S(1)}, u32[]{:S(2)}, u32[]{:S(2)}) collective-permute-start(bf16[896,128]{1,0:T(8,128)(2,1)} %get-tuple-element.12), channel_id=1, source_target_pairs={{0,16},{16,0},{1,17},{17,1},{2,18},{18,2},{3,19},{19,3},{4,20},{20... | collective-permute-start | bytes 688136 | tf_op jit(solution)/shard_map/ppermute | solution.py:344
  42.1 0.7 copy-start.2
  42.8 11.4 %copy-start.7 = (bf16[896,128]{1,0:T(8,128)(2,1)S(1)}, bf16[896,128]{1,0:T(8,128)(2,1)}, u32[]{:S(2)}) copy-start(bf16[896,128]{1,0:T(8,128)(2,1)} %get-tuple-element.12) | copy-start | bytes 688132
  42.8 12.1 %copy-start.3 = (bf16[640,128]{1,0:T(8,128)(2,1)S(1)}, bf16[640,128]{1,0:T(8,128)(2,1)}, u32[]{:S(2)}) copy-start(bf16[640,128]{1,0:T(8,128)(2,1)} %get-tuple-element.14.gslab) | copy-start | bytes 491524
  45.4 12.8 %collective-permute-start.1 = (bf16[640,128]{1,0:T(8,128)(2,1)}, bf16[640,128]{1,0:T(8,128)(2,1)S(1)}, u32[]{:S(2)}, u32[]{:S(2)}) collective-permute-start(bf16[640,128]{1,0:T(8,128)(2,1)} %get-tuple-element.16), channel_id=1, source_target_pairs={{0,16},{16,0},{1,17},{17,1},{2,18},{18,2},{3,19},{19,3},{4,20},{20... | collective-permute-start | bytes 491528 | tf_op jit(solution)/shard_map/ppermute | solution.py:362
  58.1 0.7 copy-start.5
  65.4 29.5 %all-to-all-start.1 = ((bf16[16,32,128]{2,1,0:T(8,128)(2,1)}), bf16[16,32,128]{2,1,0:T(8,128)(2,1)}, u32[]{:S(2)}, u32[]{:S(2)}) async-start(bf16[16,32,128]{2,1,0:T(8,128)(2,1)} %bitcast.8), calls=%async_computation.1 | async-start | bytes 262144 | tf_op jit(solution)/shard_map/all_to_all | solution.py:394
  80.6 1.1 copy-start.4
  80.7 1.1 copy-start.6
  81.7 14.7 %collective-permute-start.2 = (bf16[2,2,2,432,128]{4,3,0,1,2:T(8,128)(2,1)}, bf16[2,2,2,432,128]{4,3,0,1,2:T(8,128)(2,1)}, u32[]{:S(2)}, u32[]{:S(2)}) collective-permute-start(bf16[2,2,2,432,128]{4,3,0,1,2:T(8,128)(2,1)} %fusion.1), channel_id=1, source_target_pairs={{0,1},{1,0},{2,3},{3,2},{4,5},{5,4},{6,7},{7,6},{8,9},{9,8},{10,11... | collective-permute-start | bytes 2654216 | tf_op jit(solution)/shard_map/ppermute | solution.py:278
  90.3 9.4 %collective-permute-start.6 = (bf16[2,2,2,432,128]{4,3,2,1,0:T(8,128)(2,1)}, bf16[2,2,2,432,128]{4,3,2,1,0:T(8,128)(2,1)}, u32[]{:S(2)}, u32[]{:S(2)}) collective-permute-start(bf16[2,2,2,432,128]{4,3,2,1,0:T(8,128)(2,1)} %fusion.2), channel_id=1, source_target_pairs={{0,1},{1,0},{2,3},{3,2},{4,5},{5,4},{6,7},{7,6},{8,9},{9,8},{10,11... | collective-permute-start | bytes 2654216 | tf_op jit(solution)/shard_map/ppermute | solution.py:278
  96.5 3.2 %copy-start = (f32[2,2,2,1,432,128]{5,4,3,2,1,0:T(8,128)S(1)}, f32[2,2,2,1,432,128]{5,4,3,2,1,0:T(8,128)}, u32[]{:S(2)}) copy-start(f32[2,2,2,1,432,128]{5,4,3,2,1,0:T(8,128)} %get-tuple-element.21) | copy-start | bytes 5308420
  96.5 3.2 %copy-start.1 = (f32[2,2,2,1,432,128]{5,4,3,2,1,0:T(8,128)S(1)}, f32[2,2,2,1,432,128]{5,4,3,2,1,0:T(8,128)}, u32[]{:S(2)}) copy-start(f32[2,2,2,1,432,128]{5,4,3,2,1,0:T(8,128)} %get-tuple-element.22) | copy-start | bytes 5308420
  98.1 13.1 %collective-permute-start.3 = (bf16[2,2,432,128]{3,2,0,1:T(8,128)(2,1)S(1)}, bf16[2,2,432,128]{3,2,0,1:T(8,128)(2,1)S(1)}, u32[]{:S(2)}, u32[]{:S(2)}) collective-permute-start(bf16[2,2,432,128]{3,2,0,1:T(8,128)(2,1)S(1)} %fusion.4), channel_id=1, source_target_pairs={{0,2},{1,3},{2,0},{3,1},{4,6},{5,7},{6,4},{7,5},{8,10},{9,11},{10,... | collective-permute-start | bytes 1327112 | tf_op jit(solution)/shard_map/ppermute | solution.py:278
  101.2 18.5 %collective-permute-start.7 = (bf16[2,2,432,128]{3,2,1,0:T(8,128)(2,1)S(1)}, bf16[2,2,432,128]{3,2,1,0:T(8,128)(2,1)S(1)}, u32[]{:S(2)}, u32[]{:S(2)}) collective-permute-start(bf16[2,2,432,128]{3,2,1,0:T(8,128)(2,1)S(1)} %fusion.5), channel_id=1, source_target_pairs={{0,2},{1,3},{2,0},{3,1},{4,6},{5,7},{6,4},{7,5},{8,10},{9,11},{10,... | collective-permute-start | bytes 1327112 | tf_op jit(solution)/shard_map/ppermute | solution.py:278
  111.4 10.3 %collective-permute-start.4 = (bf16[2,432,128]{2,1,0:T(8,128)(2,1)S(1)}, bf16[2,432,128]{2,1,0:T(8,128)(2,1)S(1)}, u32[]{:S(2)}, u32[]{:S(2)}) collective-permute-start(bf16[2,432,128]{2,1,0:T(8,128)(2,1)S(1)} %fusion.8), channel_id=1, source_target_pairs={{0,4},{4,0},{8,12},{12,8},{1,5},{5,1},{9,13},{13,9},{2,6},{6,2},{1... | collective-permute-start | bytes 663560 | tf_op jit(solution)/shard_map/ppermute | solution.py:278
  119.9 8.9 %collective-permute-start.8 = (bf16[2,432,128]{2,1,0:T(8,128)(2,1)S(1)}, bf16[2,432,128]{2,1,0:T(8,128)(2,1)S(1)}, u32[]{:S(2)}, u32[]{:S(2)}) collective-permute-start(bf16[2,432,128]{2,1,0:T(8,128)(2,1)S(1)} %fusion.9), channel_id=1, source_target_pairs={{0,4},{4,0},{8,12},{12,8},{1,5},{5,1},{9,13},{13,9},{2,6},{6,2},{1... | collective-permute-start | bytes 663560 | tf_op jit(solution)/shard_map/ppermute | solution.py:278
  121.7 9.0 %collective-permute-start.5 = (bf16[432,128]{1,0:T(8,128)(2,1)S(1)}, bf16[432,128]{1,0:T(8,128)(2,1)S(1)}, u32[]{:S(2)}, u32[]{:S(2)}) collective-permute-start(bf16[432,128]{1,0:T(8,128)(2,1)S(1)} %fusion.10), channel_id=1, source_target_pairs={{0,8},{4,12},{8,0},{12,4},{1,9},{5,13},{9,1},{13,5},{2,10},{6,14},... | collective-permute-start | bytes 331784 | tf_op jit(solution)/shard_map/ppermute | solution.py:278
  128.9 6.9 %collective-permute-start.9 = (bf16[432,128]{1,0:T(8,128)(2,1)S(1)}, bf16[432,128]{1,0:T(8,128)(2,1)S(1)}, u32[]{:S(2)}, u32[]{:S(2)}) collective-permute-start(bf16[432,128]{1,0:T(8,128)(2,1)S(1)} %fusion.11), channel_id=1, source_target_pairs={{0,8},{4,12},{8,0},{12,4},{1,9},{5,13},{9,1},{13,5},{2,10},{6,14},... | collective-permute-start | bytes 331784 | tf_op jit(solution)/shard_map/ppermute | solution.py:278

commit v2 on v1

v2 whole, which is shorter than its diff:
```python
from functools import partial

import jax
import jax.numpy as jnp
from jax import lax
from jax.experimental import pallas as pl
from jax.experimental.pallas import tpu as pltpu
from jax.sharding import PartitionSpec as P

BF = jnp.bfloat16
F32 = jnp.float32
NT = (((1,), (1,)), ((), ()))
LANES = 128
IN_GATHER = ("rows", 2)
OUT_GATHER = ("tm", 1)
IN_ORDER = (("tm", 1), ("tm", 2))
OUT_ORDER = (("rows", 2), ("tm", 2))


class Dims:
    def __init__(self, mesh, frames_here, rows_here, width, channels, hidden):
        self.tm, self.rows = mesh["tm"], mesh["rows"]
        self.n = self.tm * self.rows
        self.f_here, self.r_here = frames_here, rows_here
        self.fr = frames_here * rows_here
        self.F, self.H = self.tm * frames_here, self.rows * rows_here
        self.W, self.C, self.D = width, channels, hidden
        self.cell = self.F * self.H
        self.own = width // self.n
        self.vmem = (24 << 20) if self.cell <= 64 else (56 << 20)

    def slab_of(self, device):
        i, j = device // self.rows, device % self.rows
        return i * self.rows + (j if i % 2 == 0 else self.rows - 1 - j)

    def my_role(self):
        return lax.axis_index("segment")

    def my_device(self):
        return lax.axis_index("tm") * self.rows + lax.axis_index("rows")

    def my_slab(self):
        i, j = lax.axis_index("tm"), lax.axis_index("rows")
        return i * self.rows + jnp.where(lax.rem(i, 2) == 0, j, self.rows - 1 - j)

    def edge(self, halo):
        columns = min(self.own, halo)
        return columns, halo // columns


def sides_of(v, dims):
    v = v.reshape(dims.F, dims.H, v.shape[1])
    row = lax.broadcasted_iota(jnp.int32, v.shape, 1)
    before = jnp.where(row == 0, 0.0, pltpu.roll(v, 1, 1))
    after = jnp.where(row == dims.H - 1, 0.0, pltpu.roll(v, dims.H - 1, 1))
    return before, v, after


def patches(v, dst, at, dims, reverse):
    F, H, c = dims.F, dims.H, v.shape[1]
    sides = sides_of(v, dims)
    for i in range(3):
        s = sides[2 - i] if reverse else sides[i]
        for t in range(3):
            m = 2 - t
            if m == 0:
                moved = s
            elif reverse:
                moved = jnp.concatenate([s[m:], jnp.zeros((m, H, c), F32)], axis=0)
            else:
                moved = jnp.concatenate([jnp.zeros((m, H, c), F32), s[: F - m]], axis=0)
            lane = (3 * t + i) * c
            dst[at * dims.cell : (at + 1) * dims.cell, lane : lane + c] = moved.reshape(
                F * H, c
            ).astype(BF)


def taps_of(k_ref, j, rows, axis):
    return jnp.concatenate(
        [k_ref[(3 * ti + j) * rows : (3 * ti + j + 1) * rows, :] for ti in range(9)], axis=axis
    )


def conv(p_ref, k_ref, columns, c, cell, acc_ref):
    for j in range(3):
        part = jnp.dot(
            p_ref[j * cell : (j + columns) * cell, :],
            taps_of(k_ref, j, c, 0),
            preferred_element_type=F32,
        )
        if j == 0:
            acc_ref[...] = part
        else:
            acc_ref[...] += part


def conv_back(p_ref, k_ref, columns, c_out, cell, acc_ref):
    for j in range(3):
        part = lax.dot_general(
            p_ref[(2 - j) * cell : (2 - j + columns) * cell, :],
            taps_of(k_ref, j, c_out, 1),
            NT,
            preferred_element_type=F32,
        )
        if j == 0:
            acc_ref[...] = part
        else:
            acc_ref[...] += part


def sigmoid(h):
    return 1.0 / (1.0 + jnp.exp(-h))


def gate(d, h):
    s = sigmoid(h)
    return d * s * (1.0 + h * (1.0 - s))


def column(w, dims):
    return slice(w * dims.cell, (w + 1) * dims.cell)


def within(w, halo, slab, dims):
    at = slab * dims.own + (w - halo)
    return jnp.logical_and(at >= 0, at < dims.W)


def load(pairs, sems):
    copies = [pltpu.make_async_copy(src, dst, sems.at[at]) for at, (src, dst) in enumerate(pairs)]
    for copy in copies:
        copy.start()
    return copies


def store_hidden(dst, w, a, dims):
    a = a.astype(BF)
    for h in range(dims.D // LANES):
        dst[column(h * (dims.own + 2) + w, dims), :] = a[:, h * LANES : (h + 1) * LANES]


def hidden_column(src, w, dims):
    parts = [src[column(h * (dims.own + 2) + w, dims), :] for h in range(dims.D // LANES)]
    return jnp.concatenate([part.astype(F32) for part in parts], axis=1)


def pack_kernel(dims, z_ref, out_ref, pad, buf):
    cols = dims.own + 6
    pad[:, :8, :] = jnp.zeros((dims.fr, 8, dims.C), F32)
    pad[:, 8 + dims.W :, :] = jnp.zeros((dims.fr, 8, dims.C), F32)
    pad[:, 8 : 8 + dims.W, :] = z_ref[...].astype(F32)
    for d in range(dims.n):
        start = dims.slab_of(d) * dims.own + 5
        for q in range(dims.fr):
            at = (d * dims.fr + q) * cols
            buf[at : at + cols, :] = pad[q, start : start + cols, :]
    out_ref[...] = buf[...].astype(BF)


def first_kernel(
    dims, recv_hbm, kin_hbm, kout_hbm, z_out, a_out, x1_out, lo_out, hi_out, hd_out,
    recv, kin, kout, rbuf, slab, p1, p2, y_ref, sems,
):
    cell, own, C, D = dims.cell, dims.own, dims.C, dims.D
    load_recv, load_in, load_out = load(
        [(recv_hbm, recv), (kin_hbm, kin), (kout_hbm, kout)], sems
    )
    cols = own + 6
    role, k = dims.my_role(), dims.my_slab()
    load_recv.wait()
    rbuf[...] = recv[...].astype(F32)
    for s in range(dims.n):
        i, j = s // dims.rows, s % dims.rows
        for q in range(dims.fr):
            f, r = i * dims.f_here + q // dims.r_here, j * dims.r_here + q % dims.r_here
            at = (s * dims.fr + q) * cols
            slab[pl.ds(f * dims.H + r, cols, stride=cell), :] = rbuf[at : at + cols, :]
    z_out[...] = slab[2 * cell : (4 + own) * cell, :].astype(BF)

    @pl.when(role == 0)
    def _():
        for w in range(own + 4):
            patches(slab[column(w + 1, dims), :], p1, w, dims, False)
        load_in.wait()
        mine = slice(cell, (3 + own) * cell)
        conv(p1, kin, own + 2, C, cell, hd_out.at[mine])
        for w in range(own + 2):
            h = hd_out[column(w + 1, dims), :]
            a = jnp.where(within(w, 1, k, dims), h * sigmoid(h), 0.0)
            store_hidden(a_out, w, a, dims)
            patches(a, p2, w, dims, False)
        load_out.wait()
        conv(p2, kout, own, D, cell, y_ref)
        x1_out[...] = (slab[3 * cell : (3 + own) * cell, :] + y_ref[...]).astype(BF)
        e_rows = lo_out.shape[0]
        lo_out[...] = x1_out[:e_rows, :]
        hi_out[...] = x1_out[own * cell - e_rows :, :]

    @pl.when(role != 0)
    def _():
        for w in range(cols):
            patches(slab[column(w, dims), :], p1, w, dims, True)
        load_in.wait()
        load_out.wait()
        conv_back(p1, kout, own + 4, D, cell, hd_out)


def second_kernel(dims, n_edge, *refs):
    edges = 2 * n_edge + 1
    x_hbm = refs[:edges]
    hd_hbm, z_hbm, a_hbm, kin_hbm = refs[edges : edges + 4]
    g0_out, x_out, a_out, e_out = refs[edges + 4 : edges + 8]
    kin, x1, hd, z, p1, p2, h_ref, y_ref, sems = refs[edges + 8 :]
    cell, own, C, D = dims.cell, dims.own, dims.C, dims.D
    role, k = dims.my_role(), dims.my_slab()

    @pl.when(role == 0)
    def _():
        for copy in load([(z_hbm, x_out), (a_hbm, a_out)], sems):
            copy.wait()

    @pl.when(role != 0)
    def _():
        pairs, at = [], 0
        for ref in x_hbm:
            rows = ref.shape[0]
            pairs.append((ref, x1.at[pl.ds(at, rows), :]))
            at += rows
        copies = load(pairs + [(kin_hbm, kin), (hd_hbm, hd), (z_hbm, z)], sems)
        for copy in copies[:edges]:
            copy.wait()
        x_out[...] = x1[2 * cell : (4 + own) * cell, :]
        for w in range(own + 6):
            patches(x1[column(w, dims), :].astype(F32), p1, w, dims, False)
        for copy in copies[edges:]:
            copy.wait()
        conv(p1, kin, own + 4, C, cell, h_ref)
        for w in range(own + 4):
            h = h_ref[column(w, dims), :]
            ok = within(w, 2, k, dims)
            s = sigmoid(h)
            if 1 <= w < 3 + own:
                store_hidden(a_out, w - 1, jnp.where(ok, h * s, 0.0), dims)
            e = hd[column(w, dims), :] * s * (1.0 + h * (1.0 - s))
            e = jnp.where(ok, e, 0.0)
            if 2 <= w < 2 + own:
                e_out[column(w - 2, dims), :] = e.astype(BF)
            patches(e, p2, w, dims, True)
        conv_back(p2, kin, own + 2, C, cell, y_ref)
        for w in range(own + 2):
            v = z[column(w, dims), :].astype(F32) + y_ref[column(w, dims), :]
            g0_out[column(w, dims), :] = jnp.where(within(w, 1, k, dims), v, 0.0).astype(BF)


def third_kernel(
    dims, g0_hbm, hd_hbm, x1_hbm, z_hbm, x_hbm, a_hbm, e_hbm, kout_hbm, e_out, g_out, sec_out,
    g0, hd, x1, z, x, a, kout, p1, p2, h_ref, y_ref, buf, sems,
):
    cell, own, C, D = dims.cell, dims.own, dims.C, dims.D
    role = dims.my_role()
    cols = own + 2
    mine = slice(cell, (1 + own) * cell)

    @pl.when(role == 0)
    def _():
        load_g, load_k, load_h, load_x = load(
            [(g0_hbm, g0), (kout_hbm, kout), (hd_hbm, hd), (x1_hbm, x1)], sems
        )
        load_g.wait()
        g_out[...] = g0[mine, :]
        for w in range(cols):
            patches(g0[column(w, dims), :].astype(F32), p1, w, dims, True)
        load_k.wait()
        conv_back(p1, kout, own, D, cell, h_ref)
        load_h.wait()
        for w in range(own):
            e_out[column(w, dims), :] = gate(
                h_ref[column(w, dims), :], hd[column(w + 2, dims), :]
            ).astype(BF)
        load_x.wait()
        y_ref[...] = x1[...].astype(F32)

    @pl.when(role != 0)
    def _():
        load_a, load_k, load_x, load_g, load_e = load(
            [(a_hbm, a), (kout_hbm, kout), (x_hbm, x), (z_hbm, z), (e_hbm, e_out)], sems
        )
        load_a.wait()
        for w in range(cols):
            patches(hidden_column(a, w, dims), p2, w, dims, False)
        load_k.wait()
        conv(p2, kout, own, D, cell, y_ref)
        load_x.wait()
        y_ref[...] = y_ref[...] + x[mine, :].astype(F32)
        load_g.wait()
        g_out[...] = z[mine, :]
        load_e.wait()

    for d in range(dims.n):
        i, j = d // dims.rows, d % dims.rows
        for q in range(dims.fr):
            f, r = i * dims.f_here + q // dims.r_here, j * dims.r_here + q % dims.r_here
            at = (d * dims.fr + q) * own
            buf[at : at + own, :] = y_ref[pl.ds(f * dims.H + r, own, stride=cell), :]
    sec_out[...] = buf[...].astype(BF)


def unpack_kernel(dims, recv, out_ref, rbuf, buf):
    own = dims.own
    rbuf[...] = recv[...].astype(F32)
    for d in range(dims.n):
        at = dims.slab_of(d) * own
        for q in range(dims.fr):
            src = (d * dims.fr + q) * own
            buf[q, at : at + own, :] = rbuf[src : src + own, :]
    out_ref[...] = buf[...].astype(BF)


def chunk_of(dims, c):
    rows = 27 * c // dims.n
    return rows, -(-rows // 16) * 16


def grads_kernel(
    dims, in_masks, out_masks,
    x_mine, x_beside, a_mine, a_beside, e_mine, e_beside, g_mine, g_beside, keep, send,
    x, a, e, g, p_in, p_out, ut_in, ut_out, win_in, win_out, sems,
):
    cell, own, C, D = dims.cell, dims.own, dims.C, dims.D
    cols = own + 2
    copies = load(
        [
            (a_mine, a.at[0]), (a_beside, a.at[1]), (g_mine, g.at[0]), (g_beside, g.at[1]),
            (x_mine, x.at[0]), (x_beside, x.at[1]), (e_mine, e.at[0]), (e_beside, e.at[1]),
        ],
        sems,
    )

    def sums(c, p, column_of, u, ut, waits, win):
        for s in range(2):
            waits[s].wait()
            for w in range(cols):
                patches(column_of(s, w), p, s * cols + w, dims, False)
        for s in range(2):
            waits[2 + s].wait()
            ut[:, s * own * cell : (s + 1) * own * cell] = u[s].T
        for j in range(3):
            cells = [p[(s * cols + j) * cell : (s * cols + j + own) * cell, :] for s in range(2)]
            part = jnp.dot(ut[...], jnp.concatenate(cells, axis=0), preferred_element_type=F32)
            for ti in range(9):
                at = 3 * ti + j
                win[at * c : (at + 1) * c, :] = part[:, ti * c : (ti + 1) * c].T

    sums(D, p_out, lambda s, w: hidden_column(a.at[s], w, dims), g, ut_out, copies[:4], win_out)
    sums(
        C, p_in, lambda s, w: x[s, column(w, dims), :].astype(F32), e, ut_in, copies[4:], win_in
    )
    me = dims.my_device()

    def rows_of(win, mask, length):
        start = lax.bitwise_xor(me, mask) * length
        if length % 8 == 0:
            return win[pl.ds(pl.multiple_of(start, 8), length), :]
        size = -(-(length + 7) // 8) * 8
        base = lax.div(start, 8) * 8
        rows = win[pl.ds(pl.multiple_of(base, 8), size), :]
        return pltpu.roll(rows, size - (start - base), 0)[:length]

    length_in, padded_in = chunk_of(dims, C)
    length_out, padded_out = chunk_of(dims, D)
    for at, (in_mask, out_mask) in enumerate(zip(in_masks, out_masks)):
        pieces = [(0, rows_of(win_out, out_mask, length_out))]
        rows = rows_of(win_in, in_mask, length_in)
        for h in range(D // LANES):
            pieces.append((padded_out + h * padded_in, rows[:, h * LANES : (h + 1) * LANES]))
        for first, piece in pieces:
            if at % 2 == 0:
                keep[at // 2, first : first + piece.shape[0], :] = piece
            else:
                send[at // 2, first : first + piece.shape[0], :] = piece.astype(BF)


def split_kernel(padded_out, keep, got, out_keep, out_send, in_keep, in_send):
    for at in range(keep.shape[0]):
        v = keep[at] + got[at].astype(F32)
        for dst, sent, part in (
            (out_keep, out_send, v[:padded_out]), (in_keep, in_send, v[padded_out:])
        ):
            if at % 2 == 0:
                dst[at // 2] = part
            else:
                sent[at // 2] = part.astype(BF)


def final_kernel(dims, in_keep, in_got, out_keep, out_got, in_out, out_out):
    length, padded = chunk_of(dims, dims.C)
    halves = dims.D // LANES
    for h in range(halves):
        rows = slice(h * padded, h * padded + length)
        in_out[pl.ds(h, length, stride=halves), :] = in_keep[rows, :] + in_got[rows, :].astype(F32)
    length = out_out.shape[0]
    out_out[...] = out_keep[:length, :] + out_got[:length, :].astype(F32)


def call(dims, kernel, shapes, ins, scratch, cost, name, vmem=None):
    return pl.pallas_call(
        kernel,
        out_shape=shapes,
        in_specs=ins,
        out_specs=jax.tree.map(lambda _: pl.BlockSpec(memory_space=pltpu.VMEM), shapes),
        scratch_shapes=scratch,
        compiler_params=pltpu.CompilerParams(vmem_limit_bytes=vmem or dims.vmem),
        cost_estimate=pl.CostEstimate(flops=cost, bytes_accessed=4 << 20, transcendentals=0),
        name=name,
    )


def halving_steps(dims, order):
    steps = [("rows", 1)] + list(order)
    for axis, size in (("tm", dims.tm), ("rows", dims.rows)):
        apart = 4
        while apart < size:
            steps.append((axis, apart))
            apart *= 2
    steps = [(axis, apart, apart * (dims.rows if axis == "tm" else 1)) for axis, apart in steps]
    masks = [sum(s[2] for b, s in enumerate(steps) if m >> b & 1) for m in range(1 << len(steps))]
    return steps, masks


def group_swap(block, axis, apart):
    count = lax.axis_size(axis)
    return lax.ppermute(block, axis, [(i, i ^ apart) for i in range(count)])


def exchanged(blocks, n):
    got = lax.all_to_all(blocks.reshape(n, -1, blocks.shape[1]), ("tm", "rows"), 0, 0)
    return got.reshape(blocks.shape)


def edge_swap(dims, block, distance):
    pairs = []
    for k in range(dims.n):
        if 0 <= k + distance < dims.n:
            a, b = dims.slab_of(k), dims.n + dims.slab_of(k + distance)
            pairs += [(a, b), (b, a)]
    return lax.ppermute(block, ("segment", "tm", "rows"), pairs)


def added(keep, send, step):
    keep = keep + group_swap(send, step[0], step[1]).astype(F32)
    return keep[0::2], keep[1::2].astype(BF)


def on_device(shape, input_clip, cotangent, kernel_in, kernel_out):
    f_here, r_here, W, C = input_clip.shape
    D = kernel_in.shape[2]
    dims = Dims(shape, f_here, r_here, W, C, D)
    own, cell, n, fr = dims.own, dims.cell, dims.n, dims.fr
    kin, kout = (
        pltpu.with_memory_space_constraint(k, pltpu.HBM) for k in (kernel_in[0], kernel_out[0])
    )
    vm = pl.BlockSpec(memory_space=pltpu.VMEM)
    hbm = pl.BlockSpec(memory_space=pltpu.HBM)
    sds = jax.ShapeDtypeStruct
    scr = pltpu.VMEM
    cols = own + 6
    conv_flops = 2 * 27 * C * D * cell
    e_cols, e_far = dims.edge(3)
    x_shape = sds(((own + 2) * cell, C), BF)
    a_shape = sds(((own + 2) * cell * (D // LANES), LANES), BF)

    send = call(
        dims, partial(pack_kernel, dims), sds((n * fr * cols, C), BF), [vm],
        [scr((fr, W + 16, C), F32), scr((n * fr * cols, C), F32)], 0, "pack",
    )(jnp.where(dims.my_role() == 0, input_clip, cotangent).reshape(fr, W, C))
    recv = exchanged(send, n)

    z, a1, x1, x1_lo, x1_hi, hd = call(
        dims, partial(first_kernel, dims),
        (
            x_shape, a_shape, sds((own * cell, C), BF), sds((e_cols * cell, C), BF),
            sds((e_cols * cell, C), BF), sds(((own + 4) * cell, D), F32),
        ),
        [hbm] * 3,
        [
            scr((n * fr * cols, C), BF), scr(kin.shape, BF), scr(kout.shape, BF),
            scr((n * fr * cols, C), F32), scr((cols * cell, C), F32),
            scr((cols * cell, 9 * C), BF), scr(((own + 2) * cell, 9 * D), BF),
            scr((own * cell, C), F32), pltpu.SemaphoreType.DMA((3,)),
        ],
        conv_flops * 2 * (own + 2), "first",
    )(recv, kin, kout)

    x1_there = group_swap(x1, "segment", 1)
    lefts = [edge_swap(dims, x1_hi, far) for far in range(e_far, 0, -1)]
    rights = [edge_swap(dims, x1_lo, -far) for far in range(1, e_far + 1)]

    g0, x2, a2, e1 = call(
        dims, partial(second_kernel, dims, e_far),
        (x_shape, x_shape, a_shape, sds((own * cell, D), BF)),
        [hbm] * (5 + 2 * e_far),
        [
            scr(kin.shape, BF), scr((cols * cell, C), BF),
            scr(((own + 4) * cell, D), F32), scr(x_shape.shape, BF),
            scr((cols * cell, 9 * C), BF), scr(((own + 4) * cell, 9 * D), BF),
            scr(((own + 4) * cell, D), F32), scr(((own + 2) * cell, C), F32),
            pltpu.SemaphoreType.DMA((4 + 2 * e_far,)),
        ],
        conv_flops * 2 * (own + 2), "second",
    )(*lefts, x1_there, *rights, hd, z, a1, kin)

    g0_there = group_swap(g0, "segment", 1)
    a_beside = group_swap(a2, *OUT_GATHER)
    x_beside = group_swap(x2, *IN_GATHER)
    g0_there, x_beside = lax.optimization_barrier((g0_there, x_beside))

    e, g, sec = call(
        dims, partial(third_kernel, dims),
        (sds((own * cell, D), BF), sds((own * cell, C), BF), sds((n * fr * own, C), BF)),
        [hbm] * 8,
        [
            scr(g0.shape, BF), scr(hd.shape, F32), scr(x1.shape, BF),
            scr(x_shape.shape, BF), scr(x_shape.shape, BF), scr(a_shape.shape, BF),
            scr(kout.shape, BF),
            scr(((own + 2) * cell, 9 * C), BF), scr(((own + 2) * cell, 9 * D), BF),
            scr((own * cell, D), F32), scr((own * cell, C), F32),
            scr((n * fr * own, C), F32), pltpu.SemaphoreType.DMA((5,)),
        ],
        conv_flops * own, "third",
    )(g0_there, hd, x1, z, x2, a2, e1, kout)
    e_beside = group_swap(e, *IN_GATHER)
    g_beside = group_swap(g, *OUT_GATHER)
    back = exchanged(sec, n)
    e_beside, g_beside, back = lax.optimization_barrier((e_beside, g_beside, back))

    in_steps, in_masks = halving_steps(dims, IN_ORDER)
    out_steps, out_masks = halving_steps(dims, OUT_ORDER)
    half = len(in_masks) // 2
    padded_in, padded_out = chunk_of(dims, C)[1], chunk_of(dims, D)[1]
    both = padded_out + padded_in * (D // LANES)
    cells2 = 2 * (own + 2) * cell
    keep, sent = call(
        dims, partial(grads_kernel, dims, in_masks, out_masks),
        (sds((half, both, LANES), F32), sds((half, both, LANES), BF)),
        [hbm] * 8,
        [
            scr((2,) + x_shape.shape, BF), scr((2,) + a_shape.shape, BF),
            scr((2, own * cell, D), BF), scr((2, own * cell, C), BF),
            scr((cells2, 9 * C), BF), scr((cells2, 9 * D), BF),
            scr((D, 2 * own * cell), BF), scr((C, 2 * own * cell), BF),
            scr((27 * C + 64, D), F32), scr((27 * D + 64, C), F32),
            pltpu.SemaphoreType.DMA((8,)),
        ],
        2 * conv_flops * own, "grads", max(dims.vmem, 32 << 20),
    )(x2, x_beside, a2, a_beside, e, e_beside, g, g_beside)
    got = group_swap(sent, "rows", 1)
    quarter = half // 2
    out_keep, out_send, in_keep, in_send = call(
        dims, partial(split_kernel, padded_out),
        (
            sds((quarter, padded_out, LANES), F32), sds((quarter, padded_out, LANES), BF),
            sds((quarter, both - padded_out, LANES), F32),
            sds((quarter, both - padded_out, LANES), BF),
        ),
        [vm, vm], [], 0, "split",
    )(keep, got)
    for out_step, in_step in zip(out_steps[1:-1], in_steps[1:-1]):
        out_keep, out_send = added(out_keep, out_send, out_step)
        in_keep, in_send = added(in_keep, in_send, in_step)
    out_got = group_swap(out_send[0], *out_steps[-1][:2])
    in_got = group_swap(in_send[0], *in_steps[-1][:2])
    shard = 27 * C * D // n // LANES
    in_sum, out_sum = call(
        dims, partial(final_kernel, dims), (sds((shard, LANES), F32),) * 2, [vm] * 4, [], 0, "final",
    )(in_keep[0], in_got, out_keep[0], out_got)

    sections = call(
        dims, partial(unpack_kernel, dims), sds((fr, W, C), BF), [vm],
        [scr((n * fr * own, C), F32), scr((fr, W, C), F32)], 0, "unpack",
    )(back).reshape(f_here, r_here, W, C)
    return sections[None], in_sum.reshape(1, -1), out_sum.reshape(1, -1)


def solution(mesh):
    in_specs = (
        P("tm", "rows", None, None),
        P("tm", "rows", None, None),
        P("segment", None, None),
        P("segment", None, None),
    )
    out_specs = (
        P("segment", "tm", "rows", None, None),
        P("segment", ("tm", "rows")),
        P("segment", ("tm", "rows")),
    )
    return jax.shard_map(
        partial(on_device, dict(mesh.shape)), mesh=mesh, in_specs=in_specs,
        out_specs=out_specs, check_vma=False,
    )
```

time: 137 us -> 98 us (0.72)
  local copies, waits for them, and re-layouts: 15.7 us -> 0.06 us
  other arithmetic: 12.9 us -> 1.03 us
  Pallas kernels: 31.3 us -> 20.7 us
  starting transfers between devices: 23.8 us -> 31.6 us
  waiting for transfers between devices: 33.9 us -> 26.8 us
    pallas_call x6 -> x8, Pallas kernels: 31.3 us -> 20.7 us  [the longest x1 7.85 us: on_device(): call(dims, partial(first_kernel, dims), (x_shape, a_shape, sds((own * cel...]
    ppermute x10 -> x13, starting transfers between devices: 19.5 us -> 27.9 us  [the longest x11 24.2 us: group_swap(): return lax.ppermute(block, axis, [(i, i ^ apart) for i in range(count)])]
    ppermute x10 -> x13, waiting for transfers between devices: 33.9 us -> 26.4 us  [the longest x11 24.4 us: group_swap(): return lax.ppermute(block, axis, [(i, i ^ apart) for i in range(count)])]
    slice x3 -> x0, local copies, waits for them, and re-layouts: 6.42 us -> none  [halved(): low = lax.index_in_dim(parts, 0, dim, keepdims=False)]
    add x8 -> x2, other arithmetic: 4.76 us -> 0.1 us  [added(): keep = keep + group_swap(send, step[0], step[1]).astype(F32)]
    another operation x1 -> x0, local copies, waits for them, and re-layouts: 4.56 us -> none  [reduce_scatter(): parts = parts.reshape((2,) * len(names) + (m, 128))]
    convert_element_type x8 -> x0, other arithmetic: 4.47 us -> none  [halved(): send = jnp.where(flag, low, high).astype(BF)]
    select_n x3 -> x1, other arithmetic: 2.98 us -> 0.93 us  [on_device(): jnp.where(dims.my_role() == 0, input_clip, cotangent).reshape(fr, W, C)]
  transfers between devices with their start and end apart: 11 -> 14, of which waited for: 6 -> 9; matrix products, arithmetic and copies ran while one was open for 18% -> 0% of each run, Pallas kernels for 6% -> 5%
where the time goes in v2:
time: 98 us; the launch traced here: 97.7 us
  starting transfers between devices  31.6 us (32%)
  waiting for transfers between devices  26.8 us (27%)
  Pallas kernels  20.7 us (21%)
  blocking collectives  16.7 us (17%)
  other arithmetic  1.03 us (1%)
    ppermute x11, waiting for transfers between devices, group_swap(): return lax.ppermute(block, axis, [(i, i ^ apart) for i in range(count)])  24.4 us
    ppermute x11, starting transfers between devices, group_swap(): return lax.ppermute(block, axis, [(i, i ^ apart) for i in range(count)])  24.2 us
    all_to_all x1, blocking collectives, exchanged(): lax.all_to_all(blocks.reshape(n, -1, blocks.shape[1]), ('tm', 'rows'), 0, 0)  16.7 us
    pallas_call x1, Pallas kernels, on_device(): call(dims, partial(first_kernel, dims), (x_shape, a_shape, sds((own * cel...  7.85 us
    pallas_call x1, Pallas kernels, on_device(): call(dims, partial(grads_kernel, dims, in_masks, out_masks), (sds((half,...  6.7 us
    pallas_call x1, Pallas kernels, on_device(): call(dims, partial(third_kernel, dims), (sds((own * cell, D), BF), sds((o...  3.92 us
    all_to_all x1, starting transfers between devices, exchanged(): lax.all_to_all(blocks.reshape(n, -1, blocks.shape[1]), ('tm', 'rows'), 0, 0)  3.73 us
    ppermute x2, starting transfers between devices, edge_swap(): return lax.ppermute(block, ('segment', 'tm', 'rows'), pairs)  3.72 us
  transfers between devices with their start and end apart: 14, of which 9 were waited for; matrix products, arithmetic and copies ran while one was open for 0% of the time, Pallas kernels for 5%

profile of v2, /device:TPU:0, one launch (start us, length us, event | category | flops | bytes accessed | tf_op | source)
XLA Modules:
  0.0 97.7 jit_solution(4669973965862441774)
XLA Ops:
  0.6 0.9 broadcast_select_fusion
  1.6 0.1 pack.1
  1.6 16.7 %all_to_all.10 = bf16[16,56,128]{2,1,0:T(8,128)(2,1)S(1)} all-to-all(bf16[16,56,128]{2,1,0:T(8,128)(2,1)S(1)} %bitcast.18), channel_id=1, replica_groups=mesh['segment'=2,'tm'=4,'rows'=4] {'tm','rows'}, dimensions={0} | all-to-all | bytes 458752 | tf_op jit(solution)/shard_map/all_to_all | solution.py:436
  18.3 7.9 %first.1 = (bf16[640,128]{1,0:T(8,128)(2,1)S(1)}, bf16[1280,128]{1,0:T(8,128)(2,1)S(1)}, bf16[512,128]{1,0:T(8,128)(2,1)S(1)}, bf16[192,128]{1,0:T(8,128)(2,1)S(...) custom-call(bf16[896,128]{1,0:T(8,128)(2,1)S(1)} %bitcast.21, bf16[3456,256]{1,0:T(8,128)(2,1)} %bitcast.25, ...), custom_call_target="tpu_custom_call" | custom-call | flops 2264924160 | bytes 4194304 | tf_op jit(solution)/shard_map/first/pallas_call | solution.py:478
  26.2 0.1 collective-permute-start.1
  26.3 3.1 %collective-permute-start = (bf16[192,128]{1,0:T(8,128)(2,1)S(1)}, bf16[192,128]{1,0:T(8,128)(2,1)S(1)}, u32[]{:S(2)}, u32[]{:S(2)}) collective-permute-start(bf16[192,128]{1,0:T(8,128)(2,1)S(1)} %get-tuple-element.29), channel_id=1, source_target_pairs={{0,17},{17,0},{1,18},{18,1},{2,19},{19,2},{3,23},{23,3},{7,22},{22... | collective-permute-start | bytes 147464 | tf_op jit(solution)/shard_map/ppermute | solution.py:446
  29.3 0.7 collective-permute-start.2
  30.0 2.0 %collective-permute-done.refs_0_ = bf16[192,128]{1,0:T(8,128)(2,1)S(1)} collective-permute-done((bf16[192,128]{1,0:T(8,128)(2,1)S(1)}, bf16[192,128]{1,0:T(8,128)(2,1)S(1)}, u32[]{:S(2)}, u32[]{:S(2)}) %collective-permute-start) | collective-permute-done | bytes 49184 | tf_op jit(solution)/shard_map/ppermute | solution.py:446
  32.0 0.0 collective-permute-done.2.refs_2_
  32.0 0.0 collective-permute-done.1.refs_1_
  32.0 0.5 second.1
  32.6 10.8 %collective-permute-start.3 = (bf16[640,128]{1,0:T(8,128)(2,1)S(1)}, bf16[640,128]{1,0:T(8,128)(2,1)S(1)}, u32[]{:S(2)}, u32[]{:S(2)}) collective-permute-start(bf16[640,128]{1,0:T(8,128)(2,1)S(1)} %get-tuple-element.35), channel_id=1, source_target_pairs={{0,16},{16,0},{1,17},{17,1},{2,18},{18,2},{3,19},{19,3},{4,20},{20... | collective-permute-start | bytes 491528 | tf_op jit(solution)/shard_map/ppermute | solution.py:432
  43.3 2.4 %collective-permute-start.4 = (bf16[640,128]{1,0:T(8,128)(2,1)S(1)}, bf16[640,128]{1,0:T(8,128)(2,1)S(1)}, u32[]{:S(2)}, u32[]{:S(2)}) collective-permute-start(bf16[640,128]{1,0:T(8,128)(2,1)S(1)} %get-tuple-element.36.x_hbm.x_mine), channel_id=1, source_target_pairs={{0,2},{1,3},{2,0},{3,1},{4,6},{5,7},{6,4},{7,5},{8,10},{9,11},{10,... | collective-permute-start | bytes 491528 | tf_op jit(solution)/shard_map/ppermute | solution.py:432
  45.7 0.8 collective-permute-start.7
  46.5 0.2 collective-permute-done.3.g0_hbm
  46.7 3.5 %collective-permute-done.4.x_beside = bf16[640,128]{1,0:T(8,128)(2,1)S(1)} collective-permute-done((bf16[640,128]{1,0:T(8,128)(2,1)S(1)}, bf16[640,128]{1,0:T(8,128)(2,1)S(1)}, u32[]{:S(2)}, u32[]{:S(2)}) %collective-permute-start.4) | collective-permute-done | bytes 163872 | tf_op jit(solution)/shard_map/ppermute | solution.py:432
  50.2 3.9 %third.1 = (bf16[512,256]{1,0:T(8,128)(2,1)S(1)}, bf16[512,128]{1,0:T(8,128)(2,1)S(1)}, bf16[512,128]{1,0:T(8,128)(2,1)}) custom-call(bf16[640,128]{1,0:T(8,128)(2,1)S(1)} %collective-permute-done.3.g0_hbm, f32[768,256]{1,0:T(8,128)S(1)} %get-tuple-element.32.refs_3_.hd_hbm, bf16[512,128]{1,0:T(8,128)(2,1)S(1)} %get-tuple-element.30.x1_hbm, ...), custom_call_target="tpu_custom_call" | custom-call | flops 905969664 | bytes 4194304 | tf_op jit(solution)/shard_map/third/pallas_call | solution.py:517
  54.1 1.6 %collective-permute-start.5 = (bf16[512,256]{1,0:T(8,128)(2,1)S(1)}, bf16[512,256]{1,0:T(8,128)(2,1)S(1)}, u32[]{:S(2)}, u32[]{:S(2)}) collective-permute-start(bf16[512,256]{1,0:T(8,128)(2,1)S(1)} %get-tuple-element.40.e_mine), channel_id=1, source_target_pairs={{0,2},{1,3},{2,0},{3,1},{4,6},{5,7},{6,4},{7,5},{8,10},{9,11},{10,... | collective-permute-start | bytes 786440 | tf_op jit(solution)/shard_map/ppermute | solution.py:432
  55.7 3.7 %all-to-all-start.1 = ((bf16[16,32,128]{2,1,0:T(8,128)(2,1)}), bf16[16,32,128]{2,1,0:T(8,128)(2,1)S(1)}, u32[]{:S(2)}, u32[]{:S(2)}) async-start(bf16[16,32,128]{2,1,0:T(8,128)(2,1)} %bitcast.5), calls=%async_computation.1 | async-start | bytes 262144 | tf_op jit(solution)/shard_map/all_to_all | solution.py:436
  59.5 1.7 %collective-permute-start.6 = (bf16[512,128]{1,0:T(8,128)(2,1)S(1)}, bf16[512,128]{1,0:T(8,128)(2,1)S(1)}, u32[]{:S(2)}, u32[]{:S(2)}) collective-permute-start(bf16[512,128]{1,0:T(8,128)(2,1)S(1)} %get-tuple-element.41.g_mine), channel_id=1, source_target_pairs={{0,4},{4,0},{8,12},{12,8},{1,5},{5,1},{9,13},{13,9},{2,6},{6,2},{1... | collective-permute-start | bytes 393224 | tf_op jit(solution)/shard_map/ppermute | solution.py:432
  61.2 6.1 %collective-permute-done.6.g_beside = bf16[512,128]{1,0:T(8,128)(2,1)S(1)} collective-permute-done((bf16[512,128]{1,0:T(8,128)(2,1)S(1)}, bf16[512,128]{1,0:T(8,128)(2,1)S(1)}, u32[]{:S(2)}, u32[]{:S(2)}) %collective-permute-start.6) | collective-permute-done | bytes 131104 | tf_op jit(solution)/shard_map/ppermute | solution.py:432
  67.2 0.4 all-to-all-done.1
  67.6 0.0 collective-permute-done.5.e_beside
  67.6 0.0 collective-permute-done.7.a_beside
  67.6 6.7 %grads.1 = (f32[4,880,128]{2,1,0:T(8,128)S(1)}, bf16[4,880,128]{2,1,0:T(8,128)(2,1)S(1)}) custom-call(bf16[640,128]{1,0:T(8,128)(2,1)S(1)} %get-tuple-element.36.x_hbm.x_mine, bf16[640,128]{1,0:T(8,128)(2,1)S(1)} %collective-permute-done.4.x_beside, bf16[1280,128]{1,0:T(8,128)(2,1)S(1)} %get-tuple-element.38.a_hbm.a_mine, ...), custom_call_target="tpu_custom_call" | custom-call | flops 1811939328 | bytes 4194304 | tf_op jit(solution)/shard_map/grads/pallas_call | solution.py:542
  74.3 0.1 collective-permute-start.8
  74.4 2.4 %collective-permute-done.8.got = bf16[4,880,128]{2,1,0:T(8,128)(2,1)S(1)} collective-permute-done((bf16[4,880,128]{2,1,0:T(8,128)(2,1)S(1)}, bf16[4,880,128]{2,1,0:T(8,128)(2,1)S(1)}, u32[]{:S(2)}, u32[]{:S(2)}) %collective-permute-start.8) | collective-permute-done | bytes 901152 | tf_op jit(solution)/shard_map/ppermute | solution.py:432
  76.8 0.1 split.1
  77.0 1.1 %collective-permute-start.11 = (bf16[2,432,128]{2,1,0:T(8,128)(2,1)S(1)}, bf16[2,432,128]{2,1,0:T(8,128)(2,1)S(1)}, u32[]{:S(2)}, u32[]{:S(2)}) collective-permute-start(bf16[2,432,128]{2,1,0:T(8,128)(2,1)S(1)} %get-tuple-element.52), channel_id=1, source_target_pairs={{0,2},{1,3},{2,0},{3,1},{4,6},{5,7},{6,4},{7,5},{8,10},{9,11},{10,... | collective-permute-start | bytes 663560 | tf_op jit(solution)/shard_map/ppermute | solution.py:432
  78.1 0.7 unpack.1
  78.8 0.6 collective-permute-start.9
  79.4 5.2 %collective-permute-done.11 = bf16[2,432,128]{2,1,0:T(8,128)(2,1)S(1)} collective-permute-done((bf16[2,432,128]{2,1,0:T(8,128)(2,1)S(1)}, bf16[2,432,128]{2,1,0:T(8,128)(2,1)S(1)}, u32[]{:S(2)}, u32[]{:S(2)}) %collective-permute-start.11) | collective-permute-done | bytes 221216 | tf_op jit(solution)/shard_map/ppermute | solution.py:432
  84.6 2.1 %collective-permute-start.12 = (bf16[432,128]{1,0:T(8,128)(2,1)S(1)}, bf16[432,128]{1,0:T(8,128)(2,1)S(1)}, u32[]{:S(2)}, u32[]{:S(2)}) collective-permute-start(bf16[432,128]{1,0:T(8,128)(2,1)S(1)} %fusion.1), channel_id=1, source_target_pairs={{0,8},{4,12},{8,0},{12,4},{1,9},{5,13},{9,1},{13,5},{2,10},{6,14},... | collective-permute-start | bytes 331784 | tf_op jit(solution)/shard_map/ppermute | solution.py:432
  86.7 0.0 collective-permute-done.9
  86.7 0.1 convert_add_fusion
  86.8 3.0 %collective-permute-start.10 = (bf16[448,128]{1,0:T(8,128)(2,1)S(1)}, bf16[448,128]{1,0:T(8,128)(2,1)S(1)}, u32[]{:S(2)}, u32[]{:S(2)}) collective-permute-start(bf16[448,128]{1,0:T(8,128)(2,1)S(1)} %fusion), channel_id=1, source_target_pairs={{0,8},{4,12},{8,0},{12,4},{1,9},{5,13},{9,1},{13,5},{2,10},{6,14},... | collective-permute-start | bytes 344072 | tf_op jit(solution)/shard_map/ppermute | solution.py:432
  89.8 5.5 %collective-permute-done.12.out_got = bf16[432,128]{1,0:T(8,128)(2,1)S(1)} collective-permute-done((bf16[432,128]{1,0:T(8,128)(2,1)S(1)}, bf16[432,128]{1,0:T(8,128)(2,1)S(1)}, u32[]{:S(2)}, u32[]{:S(2)}) %collective-permute-start.12) | collective-permute-done | bytes 110624 | tf_op jit(solution)/shard_map/ppermute | solution.py:432
  95.3 1.5 %collective-permute-done.10.in_got = bf16[448,128]{1,0:T(8,128)(2,1)S(1)} collective-permute-done((bf16[448,128]{1,0:T(8,128)(2,1)S(1)}, bf16[448,128]{1,0:T(8,128)(2,1)S(1)}, u32[]{:S(2)}, u32[]{:S(2)}) %collective-permute-start.10) | collective-permute-done | bytes 114720 | tf_op jit(solution)/shard_map/ppermute | solution.py:432
  96.8 0.8 final.1
  (5 shorter events, 0.1 us)
Async XLA Ops:
  26.2 5.8 %collective-permute-start.1 = (bf16[512,128]{1,0:T(8,128)(2,1)S(1)}, bf16[512,128]{1,0:T(8,128)(2,1)S(1)}, u32[]{:S(2)}, u32[]{:S(2)}) collective-permute-start(bf16[512,128]{1,0:T(8,128)(2,1)S(1)} %get-tuple-element.30.x1_hbm), channel_id=1, source_target_pairs={{0,16},{16,0},{1,17},{17,1},{2,18},{18,2},{3,19},{19,3},{4,20},{20... | collective-permute-start | bytes 393224 | tf_op jit(solution)/shard_map/ppermute | solution.py:432
  26.3 5.7 %collective-permute-start = (bf16[192,128]{1,0:T(8,128)(2,1)S(1)}, bf16[192,128]{1,0:T(8,128)(2,1)S(1)}, u32[]{:S(2)}, u32[]{:S(2)}) collective-permute-start(bf16[192,128]{1,0:T(8,128)(2,1)S(1)} %get-tuple-element.29), channel_id=1, source_target_pairs={{0,17},{17,0},{1,18},{18,1},{2,19},{19,2},{3,23},{23,3},{7,22},{22... | collective-permute-start | bytes 147464 | tf_op jit(solution)/shard_map/ppermute | solution.py:446
  29.3 2.7 %collective-permute-start.2 = (bf16[192,128]{1,0:T(8,128)(2,1)S(1)}, bf16[192,128]{1,0:T(8,128)(2,1)S(1)}, u32[]{:S(2)}, u32[]{:S(2)}) collective-permute-start(bf16[192,128]{1,0:T(8,128)(2,1)S(1)} %get-tuple-element.31), channel_id=1, source_target_pairs={{1,16},{16,1},{2,17},{17,2},{3,18},{18,3},{7,19},{19,7},{6,23},{23... | collective-permute-start | bytes 147464 | tf_op jit(solution)/shard_map/ppermute | solution.py:446
  32.6 14.2 %collective-permute-start.3 = (bf16[640,128]{1,0:T(8,128)(2,1)S(1)}, bf16[640,128]{1,0:T(8,128)(2,1)S(1)}, u32[]{:S(2)}, u32[]{:S(2)}) collective-permute-start(bf16[640,128]{1,0:T(8,128)(2,1)S(1)} %get-tuple-element.35), channel_id=1, source_target_pairs={{0,16},{16,0},{1,17},{17,1},{2,18},{18,2},{3,19},{19,3},{4,20},{20... | collective-permute-start | bytes 491528 | tf_op jit(solution)/shard_map/ppermute | solution.py:432
  43.3 6.9 %collective-permute-start.4 = (bf16[640,128]{1,0:T(8,128)(2,1)S(1)}, bf16[640,128]{1,0:T(8,128)(2,1)S(1)}, u32[]{:S(2)}, u32[]{:S(2)}) collective-permute-start(bf16[640,128]{1,0:T(8,128)(2,1)S(1)} %get-tuple-element.36.x_hbm.x_mine), channel_id=1, source_target_pairs={{0,2},{1,3},{2,0},{3,1},{4,6},{5,7},{6,4},{7,5},{8,10},{9,11},{10,... | collective-permute-start | bytes 491528 | tf_op jit(solution)/shard_map/ppermute | solution.py:432
  45.7 21.9 %collective-permute-start.7 = (bf16[1280,128]{1,0:T(8,128)(2,1)S(1)}, bf16[1280,128]{1,0:T(8,128)(2,1)S(1)}, u32[]{:S(2)}, u32[]{:S(2)}) collective-permute-start(bf16[1280,128]{1,0:T(8,128)(2,1)S(1)} %get-tuple-element.38.a_hbm.a_mine), channel_id=1, source_target_pairs={{0,4},{4,0},{8,12},{12,8},{1,5},{5,1},{9,13},{13,9},{2,6},{6,2},{1... | collective-permute-start | bytes 983048 | tf_op jit(solution)/shard_map/ppermute | solution.py:432
  54.1 13.5 %collective-permute-start.5 = (bf16[512,256]{1,0:T(8,128)(2,1)S(1)}, bf16[512,256]{1,0:T(8,128)(2,1)S(1)}, u32[]{:S(2)}, u32[]{:S(2)}) collective-permute-start(bf16[512,256]{1,0:T(8,128)(2,1)S(1)} %get-tuple-element.40.e_mine), channel_id=1, source_target_pairs={{0,2},{1,3},{2,0},{3,1},{4,6},{5,7},{6,4},{7,5},{8,10},{9,11},{10,... | collective-permute-start | bytes 786440 | tf_op jit(solution)/shard_map/ppermute | solution.py:432
  55.7 11.9 %all-to-all-start.1 = ((bf16[16,32,128]{2,1,0:T(8,128)(2,1)}), bf16[16,32,128]{2,1,0:T(8,128)(2,1)S(1)}, u32[]{:S(2)}, u32[]{:S(2)}) async-start(bf16[16,32,128]{2,1,0:T(8,128)(2,1)} %bitcast.5), calls=%async_computation.1 | async-start | bytes 262144 | tf_op jit(solution)/shard_map/all_to_all | solution.py:436
  59.5 7.8 %collective-permute-start.6 = (bf16[512,128]{1,0:T(8,128)(2,1)S(1)}, bf16[512,128]{1,0:T(8,128)(2,1)S(1)}, u32[]{:S(2)}, u32[]{:S(2)}) collective-permute-start(bf16[512,128]{1,0:T(8,128)(2,1)S(1)} %get-tuple-element.41.g_mine), channel_id=1, source_target_pairs={{0,4},{4,0},{8,12},{12,8},{1,5},{5,1},{9,13},{13,9},{2,6},{6,2},{1... | collective-permute-start | bytes 393224 | tf_op jit(solution)/shard_map/ppermute | solution.py:432
  74.3 2.5 %collective-permute-start.8 = (bf16[4,880,128]{2,1,0:T(8,128)(2,1)S(1)}, bf16[4,880,128]{2,1,0:T(8,128)(2,1)S(1)}, u32[]{:S(2)}, u32[]{:S(2)}) collective-permute-start(bf16[4,880,128]{2,1,0:T(8,128)(2,1)S(1)} %get-tuple-element.48), channel_id=1, source_target_pairs={{0,1},{1,0},{2,3},{3,2},{4,5},{5,4},{6,7},{7,6},{8,9},{9,8},{10,11... | collective-permute-start | bytes 2703368 | tf_op jit(solution)/shard_map/ppermute | solution.py:432
  77.0 7.5 %collective-permute-start.11 = (bf16[2,432,128]{2,1,0:T(8,128)(2,1)S(1)}, bf16[2,432,128]{2,1,0:T(8,128)(2,1)S(1)}, u32[]{:S(2)}, u32[]{:S(2)}) collective-permute-start(bf16[2,432,128]{2,1,0:T(8,128)(2,1)S(1)} %get-tuple-element.52), channel_id=1, source_target_pairs={{0,2},{1,3},{2,0},{3,1},{4,6},{5,7},{6,4},{7,5},{8,10},{9,11},{10,... | collective-permute-start | bytes 663560 | tf_op jit(solution)/shard_map/ppermute | solution.py:432
  78.8 7.9 %collective-permute-start.9 = (bf16[2,448,128]{2,1,0:T(8,128)(2,1)S(1)}, bf16[2,448,128]{2,1,0:T(8,128)(2,1)S(1)}, u32[]{:S(2)}, u32[]{:S(2)}) collective-permute-start(bf16[2,448,128]{2,1,0:T(8,128)(2,1)S(1)} %get-tuple-element.50), channel_id=1, source_target_pairs={{0,4},{4,0},{8,12},{12,8},{1,5},{5,1},{9,13},{13,9},{2,6},{6,2},{1... | collective-permute-start | bytes 688136 | tf_op jit(solution)/shard_map/ppermute | solution.py:432
  84.6 10.7 %collective-permute-start.12 = (bf16[432,128]{1,0:T(8,128)(2,1)S(1)}, bf16[432,128]{1,0:T(8,128)(2,1)S(1)}, u32[]{:S(2)}, u32[]{:S(2)}) collective-permute-start(bf16[432,128]{1,0:T(8,128)(2,1)S(1)} %fusion.1), channel_id=1, source_target_pairs={{0,8},{4,12},{8,0},{12,4},{1,9},{5,13},{9,1},{13,5},{2,10},{6,14},... | collective-permute-start | bytes 331784 | tf_op jit(solution)/shard_map/ppermute | solution.py:432
  86.8 10.1 %collective-permute-start.10 = (bf16[448,128]{1,0:T(8,128)(2,1)S(1)}, bf16[448,128]{1,0:T(8,128)(2,1)S(1)}, u32[]{:S(2)}, u32[]{:S(2)}) collective-permute-start(bf16[448,128]{1,0:T(8,128)(2,1)S(1)} %fusion), channel_id=1, source_target_pairs={{0,8},{4,12},{8,0},{12,4},{1,9},{5,13},{9,1},{13,5},{2,10},{6,14},... | collective-permute-start | bytes 344072 | tf_op jit(solution)/shard_map/ppermute | solution.py:432

commit v3 on v2

--- a/solution.py
+++ b/solution.py
@@ -59,20 +59,24 @@
 def patches(v, dst, at, dims, reverse):
     F, H, c = dims.F, dims.H, v.shape[1]
     sides = sides_of(v, dims)
+    cell = dims.cell
     for i in range(3):
         s = sides[2 - i] if reverse else sides[i]
+        whole = s.reshape(cell, c).astype(BF)
         for t in range(3):
-            m = 2 - t
+            m = (2 - t) * H
             if m == 0:
-                moved = s
-            elif reverse:
-                moved = jnp.concatenate([s[m:], jnp.zeros((m, H, c), F32)], axis=0)
+                moved = whole
+            elif m % 16 == 0:
+                gap = jnp.zeros((m, c), BF)
+                parts = [whole[m:], gap] if reverse else [gap, whole[: cell - m]]
+                moved = jnp.concatenate(parts, axis=0)
             else:
-                moved = jnp.concatenate([jnp.zeros((m, H, c), F32), s[: F - m]], axis=0)
+                gap, flat = jnp.zeros((m, c), F32), s.reshape(cell, c)
+                parts = [flat[m:], gap] if reverse else [gap, flat[: cell - m]]
+                moved = jnp.concatenate(parts, axis=0).astype(BF)
             lane = (3 * t + i) * c
-            dst[at * dims.cell : (at + 1) * dims.cell, lane : lane + c] = moved.reshape(
-                F * H, c
-            ).astype(BF)
+            dst[at * cell : (at + 1) * cell, lane : lane + c] = moved
 
 
 def taps_of(k_ref, j, rows, axis):
@@ -92,6 +96,43 @@
             acc_ref[...] = part
         else:
             acc_ref[...] += part
+
+
+def conv_block(p_ref, k_ref, first, columns, c, cell):
+    total = None
+    for j in range(3):
+        part = jnp.dot(
+            p_ref[(first + j) * cell : (first + j + columns) * cell, :],
+            taps_of(k_ref, j, c, 0),
+            preferred_element_type=F32,
+        )
+        total = part if total is None else total + part
+    return total
+
+
+def blocks_of(columns, count):
+    size = -(-columns // count)
+    return [(at, min(size, columns - at)) for at in range(0, columns, size)]
+
+
+def blocks_after(columns, earlier):
+    head = earlier[0][1] - 2
+    if len(earlier) < 2 or head < 1 or head >= columns:
+        return [(0, columns)]
+    return [(0, head), (head, columns - head)]
+
+
+def conv_back_block(p_ref, k_ref, first, columns, c_out, cell):
+    total = None
+    for j in range(3):
+        part = lax.dot_general(
+            p_ref[(first + 2 - j) * cell : (first + 2 - j + columns) * cell, :],
+            taps_of(k_ref, j, c_out, 1),
+            NT,
+            preferred_element_type=F32,
+        )
+        total = part if total is None else total + part
+    return total
 
 
 def conv_back(p_ref, k_ref, columns, c_out, cell, acc_ref):
@@ -182,15 +223,19 @@
         for w in range(own + 4):
             patches(slab[column(w + 1, dims), :], p1, w, dims, False)
         load_in.wait()
-        mine = slice(cell, (3 + own) * cell)
-        conv(p1, kin, own + 2, C, cell, hd_out.at[mine])
-        for w in range(own + 2):
-            h = hd_out[column(w + 1, dims), :]
-            a = jnp.where(within(w, 1, k, dims), h * sigmoid(h), 0.0)
-            store_hidden(a_out, w, a, dims)
-            patches(a, p2, w, dims, False)
+        for first, count in blocks_of(own + 2, 2):
+            block = conv_block(p1, kin, first, count, C, cell)
+            for w in range(first, first + count):
+                h = block[column(w - first, dims), :]
+                hd_out[column(w + 1, dims), :] = h
+                a = jnp.where(within(w, 1, k, dims), h * sigmoid(h), 0.0)
+                store_hidden(a_out, w, a, dims)
+                patches(a, p2, w, dims, False)
         load_out.wait()
-        conv(p2, kout, own, D, cell, y_ref)
+        for first, count in blocks_after(own, blocks_of(own + 2, 2)):
+            y_ref[first * cell : (first + count) * cell, :] = conv_block(
+                p2, kout, first, count, D, cell
+            )
         x1_out[...] = (slab[3 * cell : (3 + own) * cell, :] + y_ref[...]).astype(BF)
         e_rows = lo_out.shape[0]
         lo_out[...] = x1_out[:e_rows, :]
@@ -208,9 +253,9 @@
 def second_kernel(dims, n_edge, *refs):
     edges = 2 * n_edge + 1
     x_hbm = refs[:edges]
-    hd_hbm, z_hbm, a_hbm, kin_hbm = refs[edges : edges + 4]
+    hd_hbm, z_hbm, a_hbm, kin = refs[edges : edges + 4]
     g0_out, x_out, a_out, e_out = refs[edges + 4 : edges + 8]
-    kin, x1, hd, z, p1, p2, h_ref, y_ref, sems = refs[edges + 8 :]
+    x1, hd, z, p1, p2, y_ref, sems = refs[edges + 8 :]
     cell, own, C, D = dims.cell, dims.own, dims.C, dims.D
     role, k = dims.my_role(), dims.my_slab()
 
@@ -226,7 +271,7 @@
             rows = ref.shape[0]
             pairs.append((ref, x1.at[pl.ds(at, rows), :]))
             at += rows
-        copies = load(pairs + [(kin_hbm, kin), (hd_hbm, hd), (z_hbm, z)], sems)
+        copies = load(pairs + [(hd_hbm, hd), (z_hbm, z)], sems)
         for copy in copies[:edges]:
             copy.wait()
         x_out[...] = x1[2 * cell : (4 + own) * cell, :]
@@ -234,27 +279,31 @@
             patches(x1[column(w, dims), :].astype(F32), p1, w, dims, False)
         for copy in copies[edges:]:
             copy.wait()
-        conv(p1, kin, own + 4, C, cell, h_ref)
-        for w in range(own + 4):
-            h = h_ref[column(w, dims), :]
-            ok = within(w, 2, k, dims)
-            s = sigmoid(h)
-            if 1 <= w < 3 + own:
-                store_hidden(a_out, w - 1, jnp.where(ok, h * s, 0.0), dims)
-            e = hd[column(w, dims), :] * s * (1.0 + h * (1.0 - s))
-            e = jnp.where(ok, e, 0.0)
-            if 2 <= w < 2 + own:
-                e_out[column(w - 2, dims), :] = e.astype(BF)
-            patches(e, p2, w, dims, True)
-        conv_back(p2, kin, own + 2, C, cell, y_ref)
+        for first, count in blocks_of(own + 4, 2):
+            block = conv_block(p1, kin, first, count, C, cell)
+            for w in range(first, first + count):
+                h = block[column(w - first, dims), :]
+                ok = within(w, 2, k, dims)
+                s = sigmoid(h)
+                if 1 <= w < 3 + own:
+                    store_hidden(a_out, w - 1, jnp.where(ok, h * s, 0.0), dims)
+                e = hd[column(w, dims), :] * s * (1.0 + h * (1.0 - s))
+                e = jnp.where(ok, e, 0.0)
+                if 2 <= w < 2 + own:
+                    e_out[column(w - 2, dims), :] = e.astype(BF)
+                patches(e, p2, w, dims, True)
+        for first, count in blocks_after(own + 2, blocks_of(own + 4, 2)):
+            y_ref[first * cell : (first + count) * cell, :] = conv_back_block(
+                p2, kin, first, count, C, cell
+            )
         for w in range(own + 2):
             v = z[column(w, dims), :].astype(F32) + y_ref[column(w, dims), :]
             g0_out[column(w, dims), :] = jnp.where(within(w, 1, k, dims), v, 0.0).astype(BF)
 
 
 def third_kernel(
-    dims, g0_hbm, hd_hbm, x1_hbm, z_hbm, x_hbm, a_hbm, e_hbm, kout_hbm, e_out, g_out, sec_out,
-    g0, hd, x1, z, x, a, kout, p1, p2, h_ref, y_ref, buf, sems,
+    dims, g0_hbm, hd_hbm, x1_hbm, z_hbm, x_hbm, a_hbm, e_hbm, kout, e_out, g_out, sec_out,
+    g0, hd, x1, z, x, a, p1, p2, y_ref, buf, sems,
 ):
     cell, own, C, D = dims.cell, dims.own, dims.C, dims.D
     role = dims.my_role()
@@ -263,32 +312,31 @@
 
     @pl.when(role == 0)
     def _():
-        load_g, load_k, load_h, load_x = load(
-            [(g0_hbm, g0), (kout_hbm, kout), (hd_hbm, hd), (x1_hbm, x1)], sems
+        load_g, load_h, load_x = load(
+            [(g0_hbm, g0), (hd_hbm, hd), (x1_hbm, x1)], sems
         )
         load_g.wait()
         g_out[...] = g0[mine, :]
         for w in range(cols):
             patches(g0[column(w, dims), :].astype(F32), p1, w, dims, True)
-        load_k.wait()
-        conv_back(p1, kout, own, D, cell, h_ref)
         load_h.wait()
-        for w in range(own):
-            e_out[column(w, dims), :] = gate(
-                h_ref[column(w, dims), :], hd[column(w + 2, dims), :]
-            ).astype(BF)
+        for first, count in blocks_of(own, 2):
+            block = conv_back_block(p1, kout, first, count, D, cell)
+            for w in range(first, first + count):
+                e_out[column(w, dims), :] = gate(
+                    block[column(w - first, dims), :], hd[column(w + 2, dims), :]
+                ).astype(BF)
         load_x.wait()
         y_ref[...] = x1[...].astype(F32)
 
     @pl.when(role != 0)
     def _():
-        load_a, load_k, load_x, load_g, load_e = load(
-            [(a_hbm, a), (kout_hbm, kout), (x_hbm, x), (z_hbm, z), (e_hbm, e_out)], sems
+        load_a, load_x, load_g, load_e = load(
+            [(a_hbm, a), (x_hbm, x), (z_hbm, z), (e_hbm, e_out)], sems
         )
         load_a.wait()
         for w in range(cols):
             patches(hidden_column(a, w, dims), p2, w, dims, False)
-        load_k.wait()
         conv(p2, kout, own, D, cell, y_ref)
         load_x.wait()
         y_ref[...] = y_ref[...] + x[mine, :].astype(F32)
@@ -456,9 +504,8 @@
     D = kernel_in.shape[2]
     dims = Dims(shape, f_here, r_here, W, C, D)
     own, cell, n, fr = dims.own, dims.cell, dims.n, dims.fr
-    kin, kout = (
-        pltpu.with_memory_space_constraint(k, pltpu.HBM) for k in (kernel_in[0], kernel_out[0])
-    )
+    kin, kout = kernel_in[0], kernel_out[0]
+    kin_hbm, kout_hbm = (pltpu.with_memory_space_constraint(k, pltpu.HBM) for k in (kin, kout))
     vm = pl.BlockSpec(memory_space=pltpu.VMEM)
     hbm = pl.BlockSpec(memory_space=pltpu.HBM)
     sds = jax.ShapeDtypeStruct
@@ -489,7 +536,7 @@
             scr((own * cell, C), F32), pltpu.SemaphoreType.DMA((3,)),
         ],
         conv_flops * 2 * (own + 2), "first",
-    )(recv, kin, kout)
+    )(recv, kin_hbm, kout_hbm)
 
     x1_there = group_swap(x1, "segment", 1)
     lefts = [edge_swap(dims, x1_hi, far) for far in range(e_far, 0, -1)]
@@ -498,12 +545,12 @@
     g0, x2, a2, e1 = call(
         dims, partial(second_kernel, dims, e_far),
         (x_shape, x_shape, a_shape, sds((own * cell, D), BF)),
-        [hbm] * (5 + 2 * e_far),
+        [hbm] * (4 + 2 * e_far) + [vm],
         [
-            scr(kin.shape, BF), scr((cols * cell, C), BF),
+            scr((cols * cell, C), BF),
             scr(((own + 4) * cell, D), F32), scr(x_shape.shape, BF),
             scr((cols * cell, 9 * C), BF), scr(((own + 4) * cell, 9 * D), BF),
-            scr(((own + 4) * cell, D), F32), scr(((own + 2) * cell, C), F32),
+            scr(((own + 2) * cell, C), F32),
             pltpu.SemaphoreType.DMA((4 + 2 * e_far,)),
         ],
         conv_flops * 2 * (own + 2), "second",
@@ -512,24 +559,23 @@
     g0_there = group_swap(g0, "segment", 1)
     a_beside = group_swap(a2, *OUT_GATHER)
     x_beside = group_swap(x2, *IN_GATHER)
-    g0_there, x_beside = lax.optimization_barrier((g0_there, x_beside))
 
     e, g, sec = call(
         dims, partial(third_kernel, dims),
         (sds((own * cell, D), BF), sds((own * cell, C), BF), sds((n * fr * own, C), BF)),
-        [hbm] * 8,
+        [hbm] * 7 + [vm],
         [
             scr(g0.shape, BF), scr(hd.shape, F32), scr(x1.shape, BF),
             scr(x_shape.shape, BF), scr(x_shape.shape, BF), scr(a_shape.shape, BF),
-            scr(kout.shape, BF),
             scr(((own + 2) * cell, 9 * C), BF), scr(((own + 2) * cell, 9 * D), BF),
-            scr((own * cell, D), F32), scr((own * cell, C), F32),
+            scr((own * cell, C), F32),
             scr((n * fr * own, C), F32), pltpu.SemaphoreType.DMA((5,)),
         ],
         conv_flops * own, "third",
     )(g0_there, hd, x1, z, x2, a2, e1, kout)
     e_beside = group_swap(e, *IN_GATHER)
     g_beside = group_swap(g, *OUT_GATHER)
+    sec, x_beside = lax.optimization_barrier((sec, x_beside))
     back = exchanged(sec, n)
     e_beside, g_beside, back = lax.optimization_barrier((e_beside, g_beside, back))
 

time: 98 us -> 89.5 us (0.913)
  waiting for transfers between devices: 26.8 us -> 23.4 us
  Pallas kernels: 20.7 us -> 17.3 us
  starting transfers between devices: 31.6 us -> 30 us
    ppermute x11, waiting for transfers between devices: 24.4 us -> 21 us  [group_swap(): return lax.ppermute(block, axis, [(i, i ^ apart) for i in range(count)])]
    pallas_call x1, Pallas kernels: 7.85 us -> 5.63 us  [on_device(): call(dims, partial(first_kernel, dims), (x_shape, a_shape, sds((own * cel...]
    ppermute x11, starting transfers between devices: 24.2 us -> 22.1 us  [group_swap(): return lax.ppermute(block, axis, [(i, i ^ apart) for i in range(count)])]
    pallas_call x1, Pallas kernels: 3.92 us -> 2.92 us  [on_device(): call(dims, partial(third_kernel, dims), (sds((own * cell, D), BF), sds((o...]
  transfers between devices with their start and end apart: 14 -> 14, of which waited for: 9 -> 8; matrix products, arithmetic and copies ran while one was open for 0% -> 0% of each run, Pallas kernels for 5% -> 4%
where the time goes in v3:
time: 89.5 us; the launch traced here: 89.2 us
  starting transfers between devices  30 us (34%)
  waiting for transfers between devices  23.4 us (26%)
  Pallas kernels  17.3 us (19%)
  blocking collectives  16.7 us (19%)
  other arithmetic  1.03 us (1%)
    ppermute x11, starting transfers between devices, group_swap(): return lax.ppermute(block, axis, [(i, i ^ apart) for i in range(count)])  22.1 us
    ppermute x11, waiting for transfers between devices, group_swap(): return lax.ppermute(block, axis, [(i, i ^ apart) for i in range(count)])  21 us
    all_to_all x1, blocking collectives, exchanged(): lax.all_to_all(blocks.reshape(n, -1, blocks.shape[1]), ('tm', 'rows'), 0, 0)  16.7 us
    pallas_call x1, Pallas kernels, on_device(): call(dims, partial(grads_kernel, dims, in_masks, out_masks), (sds((half,...  6.7 us
    pallas_call x1, Pallas kernels, on_device(): call(dims, partial(first_kernel, dims), (x_shape, a_shape, sds((own * cel...  5.63 us
    all_to_all x1, starting transfers between devices, exchanged(): lax.all_to_all(blocks.reshape(n, -1, blocks.shape[1]), ('tm', 'rows'), 0, 0)  4.18 us
    ppermute x2, starting transfers between devices, edge_swap(): return lax.ppermute(block, ('segment', 'tm', 'rows'), pairs)  3.71 us
    pallas_call x1, Pallas kernels, on_device(): call(dims, partial(third_kernel, dims), (sds((own * cell, D), BF), sds((o...  2.92 us
  transfers between devices with their start and end apart: 14, of which 8 were waited for; matrix products, arithmetic and copies ran while one was open for 0% of the time, Pallas kernels for 4%

profile of v3, /device:TPU:0, one launch (start us, length us, event | category | flops | bytes accessed | tf_op | source)
XLA Modules:
  0.0 89.2 jit_solution(14588453393247026560)
XLA Ops:
  0.6 0.9 %broadcast_select_fusion = bf16[2,2,128,128]{3,2,1,0:T(8,128)(2,1)S(1)} fusion(bf16[2,2,128,128]{3,2,1,0:T(8,128)(2,1)} %param.4, bf16[2,2,128,128]{3,2,1,0:T(8,128)(2,1)} %param.5, pred[]{:T(512)S(6)} %eq.3), kind=kLoop, calls=%fused_computation.6 | loop fusion | flops 65536 | bytes 393217 | tf_op jit(solution)/shard_map/jit(_where)/select_n | solution.py:522
  1.6 0.1 pack.1
  1.6 16.7 %all_to_all.10 = bf16[16,56,128]{2,1,0:T(8,128)(2,1)S(1)} all-to-all(bf16[16,56,128]{2,1,0:T(8,128)(2,1)S(1)} %bitcast.20), channel_id=1, replica_groups=mesh['segment'=2,'tm'=4,'rows'=4] {'tm','rows'}, dimensions={0} | all-to-all | bytes 458752 | tf_op jit(solution)/shard_map/all_to_all | solution.py:484
  18.3 0.0 copy-start.1
  18.3 5.6 %first.1 = (bf16[640,128]{1,0:T(8,128)(2,1)S(1)}, bf16[1280,128]{1,0:T(8,128)(2,1)S(1)}, bf16[512,128]{1,0:T(8,128)(2,1)S(1)}, bf16[192,128]{1,0:T(8,128)(2,1)S(...) custom-call(bf16[896,128]{1,0:T(8,128)(2,1)S(1)} %bitcast.23, bf16[3456,256]{1,0:T(8,128)(2,1)} %bitcast.24, ...), custom_call_target="tpu_custom_call" | custom-call | flops 2264924160 | bytes 4194304 | tf_op jit(solution)/shard_map/first/pallas_call | solution.py:525
  24.0 0.1 collective-permute-start.1
  24.1 3.0 %collective-permute-start = (bf16[192,128]{1,0:T(8,128)(2,1)S(1)}, bf16[192,128]{1,0:T(8,128)(2,1)S(1)}, u32[]{:S(2)}, u32[]{:S(2)}) collective-permute-start(bf16[192,128]{1,0:T(8,128)(2,1)S(1)} %get-tuple-element.29), channel_id=1, source_target_pairs={{0,17},{17,0},{1,18},{18,1},{2,19},{19,2},{3,23},{23,3},{7,22},{22... | collective-permute-start | bytes 147464 | tf_op jit(solution)/shard_map/ppermute | solution.py:494
  27.1 0.7 collective-permute-start.2
  27.8 2.0 %collective-permute-done.refs_0_ = bf16[192,128]{1,0:T(8,128)(2,1)S(1)} collective-permute-done((bf16[192,128]{1,0:T(8,128)(2,1)S(1)}, bf16[192,128]{1,0:T(8,128)(2,1)S(1)}, u32[]{:S(2)}, u32[]{:S(2)}) %collective-permute-start) | collective-permute-done | bytes 49184 | tf_op jit(solution)/shard_map/ppermute | solution.py:494
  29.8 0.0 collective-permute-done.2.refs_2_
  29.8 0.0 collective-permute-done.1.refs_1_
  29.8 0.0 copy-done.1
  29.8 0.0 copy-start
  29.8 0.4 second.1
  30.2 7.3 %collective-permute-start.3 = (bf16[640,128]{1,0:T(8,128)(2,1)S(1)}, bf16[640,128]{1,0:T(8,128)(2,1)S(1)}, u32[]{:S(2)}, u32[]{:S(2)}) collective-permute-start(bf16[640,128]{1,0:T(8,128)(2,1)S(1)} %get-tuple-element.35), channel_id=1, source_target_pairs={{0,16},{16,0},{1,17},{17,1},{2,18},{18,2},{3,19},{19,3},{4,20},{20... | collective-permute-start | bytes 491528 | tf_op jit(solution)/shard_map/ppermute | solution.py:480
  37.5 2.4 %collective-permute-start.6 = (bf16[640,128]{1,0:T(8,128)(2,1)S(1)}, bf16[640,128]{1,0:T(8,128)(2,1)S(1)}, u32[]{:S(2)}, u32[]{:S(2)}) collective-permute-start(bf16[640,128]{1,0:T(8,128)(2,1)S(1)} %get-tuple-element.36.x_hbm.x_mine), channel_id=1, source_target_pairs={{0,2},{1,3},{2,0},{3,1},{4,6},{5,7},{6,4},{7,5},{8,10},{9,11},{10,... | collective-permute-start | bytes 491528 | tf_op jit(solution)/shard_map/ppermute | solution.py:480
  39.9 0.8 collective-permute-start.7
  40.7 0.2 collective-permute-done.3.g0_hbm
  40.9 0.0 copy-done
  40.9 2.9 %third.1 = (bf16[512,256]{1,0:T(8,128)(2,1)S(1)}, bf16[512,128]{1,0:T(8,128)(2,1)S(1)}, bf16[512,128]{1,0:T(8,128)(2,1)}) custom-call(bf16[640,128]{1,0:T(8,128)(2,1)S(1)} %collective-permute-done.3.g0_hbm, f32[768,256]{1,0:T(8,128)S(1)} %get-tuple-element.32.refs_3_.hd_hbm, bf16[512,128]{1,0:T(8,128)(2,1)S(1)} %get-tuple-element.30.x1_hbm, ...), custom_call_target="tpu_custom_call" | custom-call | flops 905969664 | bytes 4194304 | tf_op jit(solution)/shard_map/third/pallas_call | solution.py:563
  43.8 2.8 %collective-permute-start.4 = (bf16[512,256]{1,0:T(8,128)(2,1)S(1)}, bf16[512,256]{1,0:T(8,128)(2,1)S(1)}, u32[]{:S(2)}, u32[]{:S(2)}) collective-permute-start(bf16[512,256]{1,0:T(8,128)(2,1)S(1)} %get-tuple-element.39.e_mine), channel_id=1, source_target_pairs={{0,2},{1,3},{2,0},{3,1},{4,6},{5,7},{6,4},{7,5},{8,10},{9,11},{10,... | collective-permute-start | bytes 786440 | tf_op jit(solution)/shard_map/ppermute | solution.py:480
  46.6 0.0 collective-permute-done.6.x_beside
  46.6 4.2 %all-to-all-start.1 = ((bf16[16,32,128]{2,1,0:T(8,128)(2,1)}), bf16[16,32,128]{2,1,0:T(8,128)(2,1)S(1)}, u32[]{:S(2)}, u32[]{:S(2)}) async-start(bf16[16,32,128]{2,1,0:T(8,128)(2,1)} %bitcast.5), calls=%async_computation.1 | async-start | bytes 262144 | tf_op jit(solution)/shard_map/all_to_all | solution.py:484
  50.8 1.9 %collective-permute-start.5 = (bf16[512,128]{1,0:T(8,128)(2,1)S(1)}, bf16[512,128]{1,0:T(8,128)(2,1)S(1)}, u32[]{:S(2)}, u32[]{:S(2)}) collective-permute-start(bf16[512,128]{1,0:T(8,128)(2,1)S(1)} %get-tuple-element.40.g_mine), channel_id=1, source_target_pairs={{0,4},{4,0},{8,12},{12,8},{1,5},{5,1},{9,13},{13,9},{2,6},{6,2},{1... | collective-permute-start | bytes 393224 | tf_op jit(solution)/shard_map/ppermute | solution.py:480
  52.7 6.1 %collective-permute-done.5.g_beside = bf16[512,128]{1,0:T(8,128)(2,1)S(1)} collective-permute-done((bf16[512,128]{1,0:T(8,128)(2,1)S(1)}, bf16[512,128]{1,0:T(8,128)(2,1)S(1)}, u32[]{:S(2)}, u32[]{:S(2)}) %collective-permute-start.5) | collective-permute-done | bytes 131104 | tf_op jit(solution)/shard_map/ppermute | solution.py:480
  58.8 0.4 all-to-all-done.1
  59.2 0.0 collective-permute-done.4.e_beside
  59.2 0.0 collective-permute-done.7.a_beside
  59.2 6.7 %grads.1 = (f32[4,880,128]{2,1,0:T(8,128)S(1)}, bf16[4,880,128]{2,1,0:T(8,128)(2,1)S(1)}) custom-call(bf16[640,128]{1,0:T(8,128)(2,1)S(1)} %get-tuple-element.36.x_hbm.x_mine, bf16[640,128]{1,0:T(8,128)(2,1)S(1)} %collective-permute-done.6.x_beside, bf16[1280,128]{1,0:T(8,128)(2,1)S(1)} %get-tuple-element.37.a_hbm.a_mine, ...), custom_call_target="tpu_custom_call" | custom-call | flops 1811939328 | bytes 4194304 | tf_op jit(solution)/shard_map/grads/pallas_call | solution.py:588
  65.9 0.1 collective-permute-start.8
  66.0 2.4 %collective-permute-done.8.got = bf16[4,880,128]{2,1,0:T(8,128)(2,1)S(1)} collective-permute-done((bf16[4,880,128]{2,1,0:T(8,128)(2,1)S(1)}, bf16[4,880,128]{2,1,0:T(8,128)(2,1)S(1)}, u32[]{:S(2)}, u32[]{:S(2)}) %collective-permute-start.8) | collective-permute-done | bytes 901152 | tf_op jit(solution)/shard_map/ppermute | solution.py:480
  68.4 0.1 split.1
  68.6 1.2 %collective-permute-start.11 = (bf16[2,432,128]{2,1,0:T(8,128)(2,1)S(1)}, bf16[2,432,128]{2,1,0:T(8,128)(2,1)S(1)}, u32[]{:S(2)}, u32[]{:S(2)}) collective-permute-start(bf16[2,432,128]{2,1,0:T(8,128)(2,1)S(1)} %get-tuple-element.52), channel_id=1, source_target_pairs={{0,2},{1,3},{2,0},{3,1},{4,6},{5,7},{6,4},{7,5},{8,10},{9,11},{10,... | collective-permute-start | bytes 663560 | tf_op jit(solution)/shard_map/ppermute | solution.py:480
  69.7 0.7 unpack.1
  70.4 0.6 collective-permute-start.9
  71.0 5.1 %collective-permute-done.11 = bf16[2,432,128]{2,1,0:T(8,128)(2,1)S(1)} collective-permute-done((bf16[2,432,128]{2,1,0:T(8,128)(2,1)S(1)}, bf16[2,432,128]{2,1,0:T(8,128)(2,1)S(1)}, u32[]{:S(2)}, u32[]{:S(2)}) %collective-permute-start.11) | collective-permute-done | bytes 221216 | tf_op jit(solution)/shard_map/ppermute | solution.py:480
  76.2 2.1 %collective-permute-start.12 = (bf16[432,128]{1,0:T(8,128)(2,1)S(1)}, bf16[432,128]{1,0:T(8,128)(2,1)S(1)}, u32[]{:S(2)}, u32[]{:S(2)}) collective-permute-start(bf16[432,128]{1,0:T(8,128)(2,1)S(1)} %fusion.1), channel_id=1, source_target_pairs={{0,8},{4,12},{8,0},{12,4},{1,9},{5,13},{9,1},{13,5},{2,10},{6,14},... | collective-permute-start | bytes 331784 | tf_op jit(solution)/shard_map/ppermute | solution.py:480
  78.3 0.0 collective-permute-done.9
  78.3 0.1 convert_add_fusion
  78.3 3.0 %collective-permute-start.10 = (bf16[448,128]{1,0:T(8,128)(2,1)S(1)}, bf16[448,128]{1,0:T(8,128)(2,1)S(1)}, u32[]{:S(2)}, u32[]{:S(2)}) collective-permute-start(bf16[448,128]{1,0:T(8,128)(2,1)S(1)} %fusion), channel_id=1, source_target_pairs={{0,8},{4,12},{8,0},{12,4},{1,9},{5,13},{9,1},{13,5},{2,10},{6,14},... | collective-permute-start | bytes 344072 | tf_op jit(solution)/shard_map/ppermute | solution.py:480
  81.3 5.6 %collective-permute-done.12.out_got = bf16[432,128]{1,0:T(8,128)(2,1)S(1)} collective-permute-done((bf16[432,128]{1,0:T(8,128)(2,1)S(1)}, bf16[432,128]{1,0:T(8,128)(2,1)S(1)}, u32[]{:S(2)}, u32[]{:S(2)}) %collective-permute-start.12) | collective-permute-done | bytes 110624 | tf_op jit(solution)/shard_map/ppermute | solution.py:480
  86.9 1.5 %collective-permute-done.10.in_got = bf16[448,128]{1,0:T(8,128)(2,1)S(1)} collective-permute-done((bf16[448,128]{1,0:T(8,128)(2,1)S(1)}, bf16[448,128]{1,0:T(8,128)(2,1)S(1)}, u32[]{:S(2)}, u32[]{:S(2)}) %collective-permute-start.10) | collective-permute-done | bytes 114720 | tf_op jit(solution)/shard_map/ppermute | solution.py:480
  88.4 0.8 final.1
  (5 shorter events, 0.1 us)
Async XLA Ops:
  18.3 11.5 %copy-start.1 = (bf16[1,3456,256]{2,1,0:T(8,128)(2,1)S(1)}, bf16[1,3456,256]{2,1,0:T(8,128)(2,1)}, u32[]{:S(2)}) copy-start(bf16[1,3456,256]{2,1,0:T(8,128)(2,1)} %param.6) | copy-start | bytes 5308420
  24.0 5.8 %collective-permute-start.1 = (bf16[512,128]{1,0:T(8,128)(2,1)S(1)}, bf16[512,128]{1,0:T(8,128)(2,1)S(1)}, u32[]{:S(2)}, u32[]{:S(2)}) collective-permute-start(bf16[512,128]{1,0:T(8,128)(2,1)S(1)} %get-tuple-element.30.x1_hbm), channel_id=1, source_target_pairs={{0,16},{16,0},{1,17},{17,1},{2,18},{18,2},{3,19},{19,3},{4,20},{20... | collective-permute-start | bytes 393224 | tf_op jit(solution)/shard_map/ppermute | solution.py:480
  24.1 5.7 %collective-permute-start = (bf16[192,128]{1,0:T(8,128)(2,1)S(1)}, bf16[192,128]{1,0:T(8,128)(2,1)S(1)}, u32[]{:S(2)}, u32[]{:S(2)}) collective-permute-start(bf16[192,128]{1,0:T(8,128)(2,1)S(1)} %get-tuple-element.29), channel_id=1, source_target_pairs={{0,17},{17,0},{1,18},{18,1},{2,19},{19,2},{3,23},{23,3},{7,22},{22... | collective-permute-start | bytes 147464 | tf_op jit(solution)/shard_map/ppermute | solution.py:494
  27.1 2.7 %collective-permute-start.2 = (bf16[192,128]{1,0:T(8,128)(2,1)S(1)}, bf16[192,128]{1,0:T(8,128)(2,1)S(1)}, u32[]{:S(2)}, u32[]{:S(2)}) collective-permute-start(bf16[192,128]{1,0:T(8,128)(2,1)S(1)} %get-tuple-element.31), channel_id=1, source_target_pairs={{1,16},{16,1},{2,17},{17,2},{3,18},{18,3},{7,19},{19,7},{6,23},{23... | collective-permute-start | bytes 147464 | tf_op jit(solution)/shard_map/ppermute | solution.py:494
  29.8 11.1 %copy-start = (bf16[1,6912,128]{2,1,0:T(8,128)(2,1)S(1)}, bf16[1,6912,128]{2,1,0:T(8,128)(2,1)}, u32[]{:S(2)}) copy-start(bf16[1,6912,128]{2,1,0:T(8,128)(2,1)} %param.7) | copy-start | bytes 5308420
  30.2 10.7 %collective-permute-start.3 = (bf16[640,128]{1,0:T(8,128)(2,1)S(1)}, bf16[640,128]{1,0:T(8,128)(2,1)S(1)}, u32[]{:S(2)}, u32[]{:S(2)}) collective-permute-start(bf16[640,128]{1,0:T(8,128)(2,1)S(1)} %get-tuple-element.35), channel_id=1, source_target_pairs={{0,16},{16,0},{1,17},{17,1},{2,18},{18,2},{3,19},{19,3},{4,20},{20... | collective-permute-start | bytes 491528 | tf_op jit(solution)/shard_map/ppermute | solution.py:480
  37.5 9.1 %collective-permute-start.6 = (bf16[640,128]{1,0:T(8,128)(2,1)S(1)}, bf16[640,128]{1,0:T(8,128)(2,1)S(1)}, u32[]{:S(2)}, u32[]{:S(2)}) collective-permute-start(bf16[640,128]{1,0:T(8,128)(2,1)S(1)} %get-tuple-element.36.x_hbm.x_mine), channel_id=1, source_target_pairs={{0,2},{1,3},{2,0},{3,1},{4,6},{5,7},{6,4},{7,5},{8,10},{9,11},{10,... | collective-permute-start | bytes 491528 | tf_op jit(solution)/shard_map/ppermute | solution.py:480
  39.9 19.3 %collective-permute-start.7 = (bf16[1280,128]{1,0:T(8,128)(2,1)S(1)}, bf16[1280,128]{1,0:T(8,128)(2,1)S(1)}, u32[]{:S(2)}, u32[]{:S(2)}) collective-permute-start(bf16[1280,128]{1,0:T(8,128)(2,1)S(1)} %get-tuple-element.37.a_hbm.a_mine), channel_id=1, source_target_pairs={{0,4},{4,0},{8,12},{12,8},{1,5},{5,1},{9,13},{13,9},{2,6},{6,2},{1... | collective-permute-start | bytes 983048 | tf_op jit(solution)/shard_map/ppermute | solution.py:480
  43.8 15.4 %collective-permute-start.4 = (bf16[512,256]{1,0:T(8,128)(2,1)S(1)}, bf16[512,256]{1,0:T(8,128)(2,1)S(1)}, u32[]{:S(2)}, u32[]{:S(2)}) collective-permute-start(bf16[512,256]{1,0:T(8,128)(2,1)S(1)} %get-tuple-element.39.e_mine), channel_id=1, source_target_pairs={{0,2},{1,3},{2,0},{3,1},{4,6},{5,7},{6,4},{7,5},{8,10},{9,11},{10,... | collective-permute-start | bytes 786440 | tf_op jit(solution)/shard_map/ppermute | solution.py:480
  46.6 12.6 %all-to-all-start.1 = ((bf16[16,32,128]{2,1,0:T(8,128)(2,1)}), bf16[16,32,128]{2,1,0:T(8,128)(2,1)S(1)}, u32[]{:S(2)}, u32[]{:S(2)}) async-start(bf16[16,32,128]{2,1,0:T(8,128)(2,1)} %bitcast.5), calls=%async_computation.1 | async-start | bytes 262144 | tf_op jit(solution)/shard_map/all_to_all | solution.py:484
  50.8 8.0 %collective-permute-start.5 = (bf16[512,128]{1,0:T(8,128)(2,1)S(1)}, bf16[512,128]{1,0:T(8,128)(2,1)S(1)}, u32[]{:S(2)}, u32[]{:S(2)}) collective-permute-start(bf16[512,128]{1,0:T(8,128)(2,1)S(1)} %get-tuple-element.40.g_mine), channel_id=1, source_target_pairs={{0,4},{4,0},{8,12},{12,8},{1,5},{5,1},{9,13},{13,9},{2,6},{6,2},{1... | collective-permute-start | bytes 393224 | tf_op jit(solution)/shard_map/ppermute | solution.py:480
  65.9 2.5 %collective-permute-start.8 = (bf16[4,880,128]{2,1,0:T(8,128)(2,1)S(1)}, bf16[4,880,128]{2,1,0:T(8,128)(2,1)S(1)}, u32[]{:S(2)}, u32[]{:S(2)}) collective-permute-start(bf16[4,880,128]{2,1,0:T(8,128)(2,1)S(1)} %get-tuple-element.48), channel_id=1, source_target_pairs={{0,1},{1,0},{2,3},{3,2},{4,5},{5,4},{6,7},{7,6},{8,9},{9,8},{10,11... | collective-permute-start | bytes 2703368 | tf_op jit(solution)/shard_map/ppermute | solution.py:480
  68.6 7.5 %collective-permute-start.11 = (bf16[2,432,128]{2,1,0:T(8,128)(2,1)S(1)}, bf16[2,432,128]{2,1,0:T(8,128)(2,1)S(1)}, u32[]{:S(2)}, u32[]{:S(2)}) collective-permute-start(bf16[2,432,128]{2,1,0:T(8,128)(2,1)S(1)} %get-tuple-element.52), channel_id=1, source_target_pairs={{0,2},{1,3},{2,0},{3,1},{4,6},{5,7},{6,4},{7,5},{8,10},{9,11},{10,... | collective-permute-start | bytes 663560 | tf_op jit(solution)/shard_map/ppermute | solution.py:480
  70.4 7.9 %collective-permute-start.9 = (bf16[2,448,128]{2,1,0:T(8,128)(2,1)S(1)}, bf16[2,448,128]{2,1,0:T(8,128)(2,1)S(1)}, u32[]{:S(2)}, u32[]{:S(2)}) collective-permute-start(bf16[2,448,128]{2,1,0:T(8,128)(2,1)S(1)} %get-tuple-element.50), channel_id=1, source_target_pairs={{0,4},{4,0},{8,12},{12,8},{1,5},{5,1},{9,13},{13,9},{2,6},{6,2},{1... | collective-permute-start | bytes 688136 | tf_op jit(solution)/shard_map/ppermute | solution.py:480
  76.2 10.7 %collective-permute-start.12 = (bf16[432,128]{1,0:T(8,128)(2,1)S(1)}, bf16[432,128]{1,0:T(8,128)(2,1)S(1)}, u32[]{:S(2)}, u32[]{:S(2)}) collective-permute-start(bf16[432,128]{1,0:T(8,128)(2,1)S(1)} %fusion.1), channel_id=1, source_target_pairs={{0,8},{4,12},{8,0},{12,4},{1,9},{5,13},{9,1},{13,5},{2,10},{6,14},... | collective-permute-start | bytes 331784 | tf_op jit(solution)/shard_map/ppermute | solution.py:480
  78.3 10.1 %collective-permute-start.10 = (bf16[448,128]{1,0:T(8,128)(2,1)S(1)}, bf16[448,128]{1,0:T(8,128)(2,1)S(1)}, u32[]{:S(2)}, u32[]{:S(2)}) collective-permute-start(bf16[448,128]{1,0:T(8,128)(2,1)S(1)} %fusion), channel_id=1, source_target_pairs={{0,8},{4,12},{8,0},{12,4},{1,9},{5,13},{9,1},{13,5},{2,10},{6,14},... | collective-permute-start | bytes 344072 | tf_op jit(solution)/shard_map/ppermute | solution.py:480

commit v4 on v3

--- a/solution.py
+++ b/solution.py
@@ -11,10 +11,8 @@
 F32 = jnp.float32
 NT = (((1,), (1,)), ((), ()))
 LANES = 128
-IN_GATHER = ("rows", 2)
-OUT_GATHER = ("tm", 1)
-IN_ORDER = (("tm", 1), ("tm", 2))
-OUT_ORDER = (("rows", 2), ("tm", 2))
+IN_ORDER = (("tm", 1), ("rows", 2), ("tm", 2))
+OUT_ORDER = (("rows", 2), ("tm", 1), ("tm", 2))
 
 
 class Dims:
@@ -199,16 +197,13 @@
 
 
 def first_kernel(
-    dims, recv_hbm, kin_hbm, kout_hbm, z_out, a_out, x1_out, lo_out, hi_out, hd_out,
-    recv, kin, kout, rbuf, slab, p1, p2, y_ref, sems,
+    dims, recv, kin_hbm, kout_hbm, z_out, a_out, x1_out, lo_out, hi_out, hd_out,
+    kin, kout, rbuf, slab, p1, p2, y_ref, sems,
 ):
     cell, own, C, D = dims.cell, dims.own, dims.C, dims.D
-    load_recv, load_in, load_out = load(
-        [(recv_hbm, recv), (kin_hbm, kin), (kout_hbm, kout)], sems
-    )
+    load_in, load_out = load([(kin_hbm, kin), (kout_hbm, kout)], sems)
     cols = own + 6
     role, k = dims.my_role(), dims.my_slab()
-    load_recv.wait()
     rbuf[...] = recv[...].astype(F32)
     for s in range(dims.n):
         i, j = s // dims.rows, s % dims.rows
@@ -252,33 +247,26 @@
 
 def second_kernel(dims, n_edge, *refs):
     edges = 2 * n_edge + 1
-    x_hbm = refs[:edges]
-    hd_hbm, z_hbm, a_hbm, kin = refs[edges : edges + 4]
+    pieces = refs[:edges]
+    hd, z, _, kin = refs[edges : edges + 4]
     g0_out, x_out, a_out, e_out = refs[edges + 4 : edges + 8]
-    x1, hd, z, p1, p2, y_ref, sems = refs[edges + 8 :]
+    p1, p2, y_ref, sems = refs[edges + 8 :]
     cell, own, C, D = dims.cell, dims.own, dims.C, dims.D
     role, k = dims.my_role(), dims.my_slab()
 
     @pl.when(role == 0)
     def _():
-        for copy in load([(z_hbm, x_out), (a_hbm, a_out)], sems):
+        for copy in load([(z, x_out), (refs[edges + 2], a_out)], sems):
             copy.wait()
 
     @pl.when(role != 0)
     def _():
-        pairs, at = [], 0
-        for ref in x_hbm:
-            rows = ref.shape[0]
-            pairs.append((ref, x1.at[pl.ds(at, rows), :]))
-            at += rows
-        copies = load(pairs + [(hd_hbm, hd), (z_hbm, z)], sems)
-        for copy in copies[:edges]:
-            copy.wait()
-        x_out[...] = x1[2 * cell : (4 + own) * cell, :]
-        for w in range(own + 6):
-            patches(x1[column(w, dims), :].astype(F32), p1, w, dims, False)
-        for copy in copies[edges:]:
-            copy.wait()
+        columns = [(ref, at) for ref in pieces for at in range(ref.shape[0] // cell)]
+        for w, (ref, at) in enumerate(columns):
+            v = ref[column(at, dims), :]
+            if 2 <= w < own + 4:
+                x_out[column(w - 2, dims), :] = v
+            patches(v.astype(F32), p1, w, dims, False)
         for first, count in blocks_of(own + 4, 2):
             block = conv_block(p1, kin, first, count, C, cell)
             for w in range(first, first + count):
@@ -302,8 +290,8 @@
 
 
 def third_kernel(
-    dims, g0_hbm, hd_hbm, x1_hbm, z_hbm, x_hbm, a_hbm, e_hbm, kout, e_out, g_out, sec_out,
-    g0, hd, x1, z, x, a, p1, p2, y_ref, buf, sems,
+    dims, g0, hd, x1, z, x, a, e_in, kout, e_out, g_out, sec_out,
+    p1, p2, y_ref, buf,
 ):
     cell, own, C, D = dims.cell, dims.own, dims.C, dims.D
     role = dims.my_role()
@@ -312,37 +300,25 @@
 
     @pl.when(role == 0)
     def _():
-        load_g, load_h, load_x = load(
-            [(g0_hbm, g0), (hd_hbm, hd), (x1_hbm, x1)], sems
-        )
-        load_g.wait()
         g_out[...] = g0[mine, :]
         for w in range(cols):
             patches(g0[column(w, dims), :].astype(F32), p1, w, dims, True)
-        load_h.wait()
         for first, count in blocks_of(own, 2):
             block = conv_back_block(p1, kout, first, count, D, cell)
             for w in range(first, first + count):
                 e_out[column(w, dims), :] = gate(
                     block[column(w - first, dims), :], hd[column(w + 2, dims), :]
                 ).astype(BF)
-        load_x.wait()
         y_ref[...] = x1[...].astype(F32)
 
     @pl.when(role != 0)
     def _():
-        load_a, load_x, load_g, load_e = load(
-            [(a_hbm, a), (x_hbm, x), (z_hbm, z), (e_hbm, e_out)], sems
-        )
-        load_a.wait()
         for w in range(cols):
             patches(hidden_column(a, w, dims), p2, w, dims, False)
         conv(p2, kout, own, D, cell, y_ref)
-        load_x.wait()
         y_ref[...] = y_ref[...] + x[mine, :].astype(F32)
-        load_g.wait()
         g_out[...] = z[mine, :]
-        load_e.wait()
+        e_out[...] = e_in[...]
 
     for d in range(dims.n):
         i, j = d // dims.rows, d % dims.rows
@@ -369,43 +345,30 @@
     return rows, -(-rows // 16) * 16
 
 
-def grads_kernel(
-    dims, in_masks, out_masks,
-    x_mine, x_beside, a_mine, a_beside, e_mine, e_beside, g_mine, g_beside, keep, send,
-    x, a, e, g, p_in, p_out, ut_in, ut_out, win_in, win_out, sems,
+def grad_kernel(
+    dims, c, masks, v_mine, v_beside, u_mine, u_beside, keep, send, p, ut, win
 ):
-    cell, own, C, D = dims.cell, dims.own, dims.C, dims.D
+    cell, own = dims.cell, dims.own
     cols = own + 2
-    copies = load(
-        [
-            (a_mine, a.at[0]), (a_beside, a.at[1]), (g_mine, g.at[0]), (g_beside, g.at[1]),
-            (x_mine, x.at[0]), (x_beside, x.at[1]), (e_mine, e.at[0]), (e_beside, e.at[1]),
-        ],
-        sems,
-    )
-
-    def sums(c, p, column_of, u, ut, waits, win):
-        for s in range(2):
-            waits[s].wait()
-            for w in range(cols):
-                patches(column_of(s, w), p, s * cols + w, dims, False)
-        for s in range(2):
-            waits[2 + s].wait()
-            ut[:, s * own * cell : (s + 1) * own * cell] = u[s].T
-        for j in range(3):
-            cells = [p[(s * cols + j) * cell : (s * cols + j + own) * cell, :] for s in range(2)]
-            part = jnp.dot(ut[...], jnp.concatenate(cells, axis=0), preferred_element_type=F32)
-            for ti in range(9):
-                at = 3 * ti + j
-                win[at * c : (at + 1) * c, :] = part[:, ti * c : (ti + 1) * c].T
-
-    sums(D, p_out, lambda s, w: hidden_column(a.at[s], w, dims), g, ut_out, copies[:4], win_out)
-    sums(
-        C, p_in, lambda s, w: x[s, column(w, dims), :].astype(F32), e, ut_in, copies[4:], win_in
-    )
+    for s, v in enumerate((v_mine, v_beside)):
+        for w in range(cols):
+            if c == dims.C:
+                values = v[column(w, dims), :].astype(F32)
+            else:
+                values = hidden_column(v, w, dims)
+            patches(values, p, s * cols + w, dims, False)
+    for s, u in enumerate((u_mine, u_beside)):
+        ut[:, s * own * cell : (s + 1) * own * cell] = u[...].T
+    for j in range(3):
+        cells = [p[(s * cols + j) * cell : (s * cols + j + own) * cell, :] for s in range(2)]
+        part = jnp.dot(ut[...], jnp.concatenate(cells, axis=0), preferred_element_type=F32)
+        for ti in range(9):
+            at = 3 * ti + j
+            win[at * c : (at + 1) * c, :] = part[:, ti * c : (ti + 1) * c].T
     me = dims.my_device()
-
-    def rows_of(win, mask, length):
+    length, padded = chunk_of(dims, c)
+
+    def rows_of(mask):
         start = lax.bitwise_xor(me, mask) * length
         if length % 8 == 0:
             return win[pl.ds(pl.multiple_of(start, 8), length), :]
@@ -414,30 +377,24 @@
         rows = win[pl.ds(pl.multiple_of(base, 8), size), :]
         return pltpu.roll(rows, size - (start - base), 0)[:length]
 
-    length_in, padded_in = chunk_of(dims, C)
-    length_out, padded_out = chunk_of(dims, D)
-    for at, (in_mask, out_mask) in enumerate(zip(in_masks, out_masks)):
-        pieces = [(0, rows_of(win_out, out_mask, length_out))]
-        rows = rows_of(win_in, in_mask, length_in)
-        for h in range(D // LANES):
-            pieces.append((padded_out + h * padded_in, rows[:, h * LANES : (h + 1) * LANES]))
-        for first, piece in pieces:
+    for at, mask in enumerate(masks):
+        rows = rows_of(mask)
+        for h in range(rows.shape[1] // LANES):
+            piece = rows[:, h * LANES : (h + 1) * LANES]
+            to = slice(h * padded, h * padded + length)
             if at % 2 == 0:
-                keep[at // 2, first : first + piece.shape[0], :] = piece
+                keep[at // 2, to, :] = piece
             else:
-                send[at // 2, first : first + piece.shape[0], :] = piece.astype(BF)
-
-
-def split_kernel(padded_out, keep, got, out_keep, out_send, in_keep, in_send):
+                send[at // 2, to, :] = piece.astype(BF)
+
+
+def add_kernel(keep, got, keep_out, send_out):
     for at in range(keep.shape[0]):
         v = keep[at] + got[at].astype(F32)
-        for dst, sent, part in (
-            (out_keep, out_send, v[:padded_out]), (in_keep, in_send, v[padded_out:])
-        ):
-            if at % 2 == 0:
-                dst[at // 2] = part
-            else:
-                sent[at // 2] = part.astype(BF)
+        if at % 2 == 0:
+            keep_out[at // 2] = v
+        else:
+            send_out[at // 2] = v.astype(BF)
 
 
 def final_kernel(dims, in_keep, in_got, out_keep, out_got, in_out, out_out):
@@ -464,7 +421,7 @@
 
 
 def halving_steps(dims, order):
-    steps = [("rows", 1)] + list(order)
+    steps = list(order)
     for axis, size in (("tm", dims.tm), ("rows", dims.rows)):
         apart = 4
         while apart < size:
@@ -494,9 +451,18 @@
     return lax.ppermute(block, ("segment", "tm", "rows"), pairs)
 
 
-def added(keep, send, step):
-    keep = keep + group_swap(send, step[0], step[1]).astype(F32)
-    return keep[0::2], keep[1::2].astype(BF)
+def added(dims, keep, send, step, name, also=None):
+    got = group_swap(send, step[0], step[1])
+    if also is not None:
+        got, also = lax.optimization_barrier((got, also))
+    half, rows, lanes = keep.shape
+    vm = pl.BlockSpec(memory_space=pltpu.VMEM)
+    shape = (half // 2, rows, lanes)
+    keep, send = call(
+        dims, add_kernel,
+        (jax.ShapeDtypeStruct(shape, F32), jax.ShapeDtypeStruct(shape, BF)), [vm, vm], [], 0, name,
+    )(keep, got)
+    return keep, send, also
 
 
 def on_device(shape, input_clip, cotangent, kernel_in, kernel_out):
@@ -528,12 +494,12 @@
             x_shape, a_shape, sds((own * cell, C), BF), sds((e_cols * cell, C), BF),
             sds((e_cols * cell, C), BF), sds(((own + 4) * cell, D), F32),
         ),
-        [hbm] * 3,
+        [vm, hbm, hbm],
         [
-            scr((n * fr * cols, C), BF), scr(kin.shape, BF), scr(kout.shape, BF),
+            scr(kin.shape, BF), scr(kout.shape, BF),
             scr((n * fr * cols, C), F32), scr((cols * cell, C), F32),
             scr((cols * cell, 9 * C), BF), scr(((own + 2) * cell, 9 * D), BF),
-            scr((own * cell, C), F32), pltpu.SemaphoreType.DMA((3,)),
+            scr((own * cell, C), F32), pltpu.SemaphoreType.DMA((2,)),
         ],
         conv_flops * 2 * (own + 2), "first",
     )(recv, kin_hbm, kout_hbm)
@@ -545,74 +511,63 @@
     g0, x2, a2, e1 = call(
         dims, partial(second_kernel, dims, e_far),
         (x_shape, x_shape, a_shape, sds((own * cell, D), BF)),
-        [hbm] * (4 + 2 * e_far) + [vm],
+        [vm] * (5 + 2 * e_far),
         [
-            scr((cols * cell, C), BF),
-            scr(((own + 4) * cell, D), F32), scr(x_shape.shape, BF),
             scr((cols * cell, 9 * C), BF), scr(((own + 4) * cell, 9 * D), BF),
             scr(((own + 2) * cell, C), F32),
-            pltpu.SemaphoreType.DMA((4 + 2 * e_far,)),
+            pltpu.SemaphoreType.DMA((2,)),
         ],
         conv_flops * 2 * (own + 2), "second",
     )(*lefts, x1_there, *rights, hd, z, a1, kin)
 
     g0_there = group_swap(g0, "segment", 1)
-    a_beside = group_swap(a2, *OUT_GATHER)
-    x_beside = group_swap(x2, *IN_GATHER)
+    a_beside = group_swap(a2, "rows", 1)
+    x_beside = group_swap(x2, "rows", 1)
 
     e, g, sec = call(
         dims, partial(third_kernel, dims),
         (sds((own * cell, D), BF), sds((own * cell, C), BF), sds((n * fr * own, C), BF)),
-        [hbm] * 7 + [vm],
+        [vm] * 8,
         [
-            scr(g0.shape, BF), scr(hd.shape, F32), scr(x1.shape, BF),
-            scr(x_shape.shape, BF), scr(x_shape.shape, BF), scr(a_shape.shape, BF),
             scr(((own + 2) * cell, 9 * C), BF), scr(((own + 2) * cell, 9 * D), BF),
             scr((own * cell, C), F32),
-            scr((n * fr * own, C), F32), pltpu.SemaphoreType.DMA((5,)),
+            scr((n * fr * own, C), F32),
         ],
         conv_flops * own, "third",
     )(g0_there, hd, x1, z, x2, a2, e1, kout)
-    e_beside = group_swap(e, *IN_GATHER)
-    g_beside = group_swap(g, *OUT_GATHER)
-    sec, x_beside = lax.optimization_barrier((sec, x_beside))
-    back = exchanged(sec, n)
-    e_beside, g_beside, back = lax.optimization_barrier((e_beside, g_beside, back))
+    e_beside = group_swap(e, "rows", 1)
+    g_beside = group_swap(g, "rows", 1)
 
     in_steps, in_masks = halving_steps(dims, IN_ORDER)
     out_steps, out_masks = halving_steps(dims, OUT_ORDER)
     half = len(in_masks) // 2
-    padded_in, padded_out = chunk_of(dims, C)[1], chunk_of(dims, D)[1]
-    both = padded_out + padded_in * (D // LANES)
-    cells2 = 2 * (own + 2) * cell
-    keep, sent = call(
-        dims, partial(grads_kernel, dims, in_masks, out_masks),
-        (sds((half, both, LANES), F32), sds((half, both, LANES), BF)),
-        [hbm] * 8,
-        [
-            scr((2,) + x_shape.shape, BF), scr((2,) + a_shape.shape, BF),
-            scr((2, own * cell, D), BF), scr((2, own * cell, C), BF),
-            scr((cells2, 9 * C), BF), scr((cells2, 9 * D), BF),
-            scr((D, 2 * own * cell), BF), scr((C, 2 * own * cell), BF),
-            scr((27 * C + 64, D), F32), scr((27 * D + 64, C), F32),
-            pltpu.SemaphoreType.DMA((8,)),
-        ],
-        2 * conv_flops * own, "grads", max(dims.vmem, 32 << 20),
-    )(x2, x_beside, a2, a_beside, e, e_beside, g, g_beside)
-    got = group_swap(sent, "rows", 1)
-    quarter = half // 2
-    out_keep, out_send, in_keep, in_send = call(
-        dims, partial(split_kernel, padded_out),
-        (
-            sds((quarter, padded_out, LANES), F32), sds((quarter, padded_out, LANES), BF),
-            sds((quarter, both - padded_out, LANES), F32),
-            sds((quarter, both - padded_out, LANES), BF),
-        ),
-        [vm, vm], [], 0, "split",
-    )(keep, got)
-    for out_step, in_step in zip(out_steps[1:-1], in_steps[1:-1]):
-        out_keep, out_send = added(out_keep, out_send, out_step)
-        in_keep, in_send = added(in_keep, in_send, in_step)
+
+    def grad(c, c_out, masks, v, v_beside, u, u_beside, name):
+        rows = chunk_of(dims, c)[1] * (c_out // LANES)
+        return call(
+            dims, partial(grad_kernel, dims, c, masks),
+            (sds((half, rows, LANES), F32), sds((half, rows, LANES), BF)),
+            [vm] * 4,
+            [
+                scr((2 * (own + 2) * cell, 9 * c), BF), scr((c_out, 2 * own * cell), BF),
+                scr((27 * c + 64, c_out), F32),
+            ],
+            conv_flops * own, name,
+        )(v, v_beside, u, u_beside)
+
+    out_keep, out_send = grad(D, C, out_masks, a2, a_beside, g, g_beside, "grad_out")
+    e, e_beside, out_send = lax.optimization_barrier((e, e_beside, out_send))
+    in_keep, in_send = grad(C, D, in_masks, x2, x_beside, e, e_beside, "grad_in")
+    sec, in_keep, out_keep = lax.optimization_barrier((sec, in_keep, out_keep))
+    back = exchanged(sec, n)
+    for at in range(len(in_steps) - 1):
+        out_keep, out_send, back_out = added(
+            dims, out_keep, out_send, out_steps[at], "add_out", back if False else None
+        )
+        in_keep, in_send, back_in = added(
+            dims, in_keep, in_send, in_steps[at], "add_in", back if at == 1 else None
+        )
+        back = back if back_in is None else back_in
     out_got = group_swap(out_send[0], *out_steps[-1][:2])
     in_got = group_swap(in_send[0], *in_steps[-1][:2])
     shard = 27 * C * D // n // LANES

time: 89.5 us -> 84.5 us (0.944)
  starting transfers between devices: 30 us -> 25.4 us
  Pallas kernels: 17.3 us -> 15.6 us
  waiting for transfers between devices: 23.4 us -> 24.8 us
    ppermute x11 -> x12, starting transfers between devices: 22.1 us -> 18.2 us  [group_swap(): return lax.ppermute(block, axis, [(i, i ^ apart) for i in range(count)])]
    ppermute x11 -> x12, waiting for transfers between devices: 21 us -> 22.8 us  [group_swap(): return lax.ppermute(block, axis, [(i, i ^ apart) for i in range(count)])]
    pallas_call x2 -> x6, Pallas kernels: 6.84 us -> 5.92 us  [the longest x2 5.7 us: grad(): call(dims, partial(grad_kernel, dims, c, masks), (sds((half, rows, LANES)...]
  transfers between devices with their start and end apart: 14 -> 15, of which waited for: 8 -> 7; matrix products, arithmetic and copies ran while one was open for 0% -> 0% of each run, Pallas kernels for 4% -> 8%
where the time goes in v4:
time: 84.5 us; the launch traced here: 84.2 us
  starting transfers between devices  25.4 us (30%)
  waiting for transfers between devices  24.8 us (29%)
  blocking collectives  16.7 us (20%)
  Pallas kernels  15.6 us (18%)
  other arithmetic  0.93 us (1%)
    ppermute x12, waiting for transfers between devices, group_swap(): return lax.ppermute(block, axis, [(i, i ^ apart) for i in range(count)])  22.8 us
    ppermute x12, starting transfers between devices, group_swap(): return lax.ppermute(block, axis, [(i, i ^ apart) for i in range(count)])  18.2 us
    all_to_all x1, blocking collectives, exchanged(): lax.all_to_all(blocks.reshape(n, -1, blocks.shape[1]), ('tm', 'rows'), 0, 0)  16.7 us
    pallas_call x2, Pallas kernels, grad(): call(dims, partial(grad_kernel, dims, c, masks), (sds((half, rows, LANES)...  5.7 us
    pallas_call x1, Pallas kernels, on_device(): call(dims, partial(first_kernel, dims), (x_shape, a_shape, sds((own * cel...  5.48 us
    ppermute x2, starting transfers between devices, edge_swap(): return lax.ppermute(block, ('segment', 'tm', 'rows'), pairs)  3.72 us
    all_to_all x1, starting transfers between devices, exchanged(): lax.all_to_all(blocks.reshape(n, -1, blocks.shape[1]), ('tm', 'rows'), 0, 0)  3.51 us
    pallas_call x1, Pallas kernels, on_device(): call(dims, partial(third_kernel, dims), (sds((own * cell, D), BF), sds((o...  2.29 us
  transfers between devices with their start and end apart: 15, of which 7 were waited for; matrix products, arithmetic and copies ran while one was open for 0% of the time, Pallas kernels for 8%

profile of v4, /device:TPU:0, one launch (start us, length us, event | category | flops | bytes accessed | tf_op | source)
XLA Modules:
  0.0 84.2 jit_solution(1403291847469295381)
XLA Ops:
  0.6 0.9 %broadcast_select_fusion = bf16[2,2,128,128]{3,2,1,0:T(8,128)(2,1)S(1)} fusion(bf16[2,2,128,128]{3,2,1,0:T(8,128)(2,1)} %param.4, bf16[2,2,128,128]{3,2,1,0:T(8,128)(2,1)} %param.5, pred[]{:T(512)S(6)} %eq.3), kind=kLoop, calls=%fused_computation | loop fusion | flops 65536 | bytes 393217 | tf_op jit(solution)/shard_map/jit(_where)/select_n | solution.py:488
  1.6 0.1 pack.1
  1.6 16.7 %all_to_all.10 = bf16[16,56,128]{2,1,0:T(8,128)(2,1)S(1)} all-to-all(bf16[16,56,128]{2,1,0:T(8,128)(2,1)S(1)} %bitcast.16), channel_id=1, replica_groups=mesh['segment'=2,'tm'=4,'rows'=4] {'tm','rows'}, dimensions={0} | all-to-all | bytes 458752 | tf_op jit(solution)/shard_map/all_to_all | solution.py:441
  18.3 0.0 copy-start.1
  18.3 5.5 %first.1 = (bf16[640,128]{1,0:T(8,128)(2,1)S(1)}, bf16[1280,128]{1,0:T(8,128)(2,1)S(1)}, bf16[512,128]{1,0:T(8,128)(2,1)S(1)}, bf16[192,128]{1,0:T(8,128)(2,1)S(...) custom-call(bf16[896,128]{1,0:T(8,128)(2,1)S(1)} %bitcast.19, bf16[3456,256]{1,0:T(8,128)(2,1)} %bitcast.22, ...), custom_call_target="tpu_custom_call" | custom-call | flops 2264924160 | bytes 4194304 | tf_op jit(solution)/shard_map/first/pallas_call | solution.py:491
  23.8 0.1 collective-permute-start.1
  23.9 3.1 %collective-permute-start = (bf16[192,128]{1,0:T(8,128)(2,1)S(1)}, bf16[192,128]{1,0:T(8,128)(2,1)S(1)}, u32[]{:S(2)}, u32[]{:S(2)}) collective-permute-start(bf16[192,128]{1,0:T(8,128)(2,1)S(1)} %get-tuple-element.38), channel_id=1, source_target_pairs={{0,17},{17,0},{1,18},{18,1},{2,19},{19,2},{3,23},{23,3},{7,22},{22... | collective-permute-start | bytes 147464 | tf_op jit(solution)/shard_map/ppermute | solution.py:451
  27.0 0.7 collective-permute-start.2
  27.6 2.0 %collective-permute-done.refs_0_ = bf16[192,128]{1,0:T(8,128)(2,1)S(1)} collective-permute-done((bf16[192,128]{1,0:T(8,128)(2,1)S(1)}, bf16[192,128]{1,0:T(8,128)(2,1)S(1)}, u32[]{:S(2)}, u32[]{:S(2)}) %collective-permute-start) | collective-permute-done | bytes 49184 | tf_op jit(solution)/shard_map/ppermute | solution.py:451
  29.6 0.0 collective-permute-done.2.refs_2_
  29.6 0.0 collective-permute-done.1.refs_1_
  29.6 0.0 copy-done.1
  29.6 0.0 copy-start
  29.7 0.4 second.1
  30.0 6.5 %collective-permute-start.3 = (bf16[640,128]{1,0:T(8,128)(2,1)S(1)}, bf16[640,128]{1,0:T(8,128)(2,1)S(1)}, u32[]{:S(2)}, u32[]{:S(2)}) collective-permute-start(bf16[640,128]{1,0:T(8,128)(2,1)S(1)} %get-tuple-element.44), channel_id=1, source_target_pairs={{0,16},{16,0},{1,17},{17,1},{2,18},{18,2},{3,19},{19,3},{4,20},{20... | collective-permute-start | bytes 491528 | tf_op jit(solution)/shard_map/ppermute | solution.py:437
  36.6 2.0 %collective-permute-start.6 = (bf16[1280,128]{1,0:T(8,128)(2,1)S(1)}, bf16[1280,128]{1,0:T(8,128)(2,1)S(1)}, u32[]{:S(2)}, u32[]{:S(2)}) collective-permute-start(bf16[1280,128]{1,0:T(8,128)(2,1)S(1)} %get-tuple-element.46.a.v_mine), channel_id=1, source_target_pairs={{0,1},{1,0},{2,3},{3,2},{4,5},{5,4},{6,7},{7,6},{8,9},{9,8},{10,11... | collective-permute-start | bytes 983048 | tf_op jit(solution)/shard_map/ppermute | solution.py:437
  38.6 1.4 %collective-permute-done.3.g0 = bf16[640,128]{1,0:T(8,128)(2,1)S(1)} collective-permute-done((bf16[640,128]{1,0:T(8,128)(2,1)S(1)}, bf16[640,128]{1,0:T(8,128)(2,1)S(1)}, u32[]{:S(2)}, u32[]{:S(2)}) %collective-permute-start.3) | collective-permute-done | bytes 163872 | tf_op jit(solution)/shard_map/ppermute | solution.py:437
  39.9 0.0 copy-done
  39.9 2.3 %third.1 = (bf16[512,256]{1,0:T(8,128)(2,1)S(1)}, bf16[512,128]{1,0:T(8,128)(2,1)S(1)}, bf16[512,128]{1,0:T(8,128)(2,1)}) custom-call(bf16[640,128]{1,0:T(8,128)(2,1)S(1)} %collective-permute-done.3.g0, f32[768,256]{1,0:T(8,128)S(1)} %get-tuple-element.41.refs_3_.hd, bf16[512,128]{1,0:T(8,128)(2,1)S(1)} %get-tuple-element.39.x1, ...), custom_call_target="tpu_custom_call" | custom-call | flops 905969664 | bytes 4194304 | tf_op jit(solution)/shard_map/third/pallas_call | solution.py:527
  42.2 1.5 %collective-permute-start.5 = (bf16[512,256]{1,0:T(8,128)(2,1)S(1)}, bf16[512,256]{1,0:T(8,128)(2,1)S(1)}, u32[]{:S(2)}, u32[]{:S(2)}) collective-permute-start(bf16[512,256]{1,0:T(8,128)(2,1)S(1)} %get-tuple-element.52.u_mine), channel_id=1, source_target_pairs={{0,1},{1,0},{2,3},{3,2},{4,5},{5,4},{6,7},{7,6},{8,9},{9,8},{10,11... | collective-permute-start | bytes 786440 | tf_op jit(solution)/shard_map/ppermute | solution.py:437
  43.7 0.0 collective-permute-start.7
  43.7 0.5 collective-permute-start.4
  44.2 0.8 collective-permute-done.7.u_beside
  45.1 0.0 collective-permute-done.6.v_beside
  45.1 3.1 %grad_out.1 = (f32[4,432,128]{2,1,0:T(8,128)S(1)}, bf16[4,432,128]{2,1,0:T(8,128)(2,1)}) custom-call(bf16[1280,128]{1,0:T(8,128)(2,1)S(1)} %get-tuple-element.46.a.v_mine, bf16[1280,128]{1,0:T(8,128)(2,1)S(1)} %collective-permute-done.6.v_beside, bf16[512,128]{1,0:T(8,128)(2,1)S(1)} %get-tuple-element.50.u_mine, ...), custom_call_target="tpu_custom_call" | custom-call | flops 905969664 | bytes 4194304 | tf_op jit(solution)/shard_map/grad_out/pallas_call | solution.py:547
  48.2 0.0 collective-permute-done.5.u_beside
  48.2 0.0 collective-permute-done.4.v_beside
  48.2 2.5 %grad_in.1 = (f32[4,448,128]{2,1,0:T(8,128)S(1)}, bf16[4,448,128]{2,1,0:T(8,128)(2,1)S(1)}) custom-call(bf16[640,128]{1,0:T(8,128)(2,1)S(1)} %get-tuple-element.45.x.v_mine, bf16[640,128]{1,0:T(8,128)(2,1)S(1)} %collective-permute-done.4.v_beside, bf16[512,256]{1,0:T(8,128)(2,1)S(1)} %get-tuple-element.52.u_mine, ...), custom_call_target="tpu_custom_call" | custom-call | flops 905969664 | bytes 4194304 | tf_op jit(solution)/shard_map/grad_in/pallas_call | solution.py:547
  50.8 3.0 %collective-permute-start.8 = (bf16[4,448,128]{2,1,0:T(8,128)(2,1)S(1)}, bf16[4,448,128]{2,1,0:T(8,128)(2,1)S(1)}, u32[]{:S(2)}, u32[]{:S(2)}) collective-permute-start(bf16[4,448,128]{2,1,0:T(8,128)(2,1)S(1)} %get-tuple-element.57), channel_id=1, source_target_pairs={{0,4},{4,0},{8,12},{12,8},{1,5},{5,1},{9,13},{13,9},{2,6},{6,2},{1... | collective-permute-start | bytes 1376264 | tf_op jit(solution)/shard_map/ppermute | solution.py:437
  53.8 0.4 collective-permute-start.11
  54.2 3.5 %all-to-all-start.1 = ((bf16[16,32,128]{2,1,0:T(8,128)(2,1)}), bf16[16,32,128]{2,1,0:T(8,128)(2,1)S(1)}, u32[]{:S(2)}, u32[]{:S(2)}) async-start(bf16[16,32,128]{2,1,0:T(8,128)(2,1)} %bitcast.5), calls=%async_computation.1 | async-start | bytes 262144 | tf_op jit(solution)/shard_map/all_to_all | solution.py:441
  57.7 8.3 %collective-permute-done.8.got = bf16[4,448,128]{2,1,0:T(8,128)(2,1)S(1)} collective-permute-done((bf16[4,448,128]{2,1,0:T(8,128)(2,1)S(1)}, bf16[4,448,128]{2,1,0:T(8,128)(2,1)S(1)}, u32[]{:S(2)}, u32[]{:S(2)}) %collective-permute-start.8) | collective-permute-done | bytes 458784 | tf_op jit(solution)/shard_map/ppermute | solution.py:437
  66.0 0.1 add_in.2
  66.1 0.4 collective-permute-start.9
  66.5 0.6 collective-permute-done.11.got
  67.1 0.1 add_out.2
  67.1 0.7 collective-permute-start.12
  67.9 0.0 all-to-all-done.1
  67.9 4.9 %collective-permute-done.9.got = bf16[2,448,128]{2,1,0:T(8,128)(2,1)S(1)} collective-permute-done((bf16[2,448,128]{2,1,0:T(8,128)(2,1)S(1)}, bf16[2,448,128]{2,1,0:T(8,128)(2,1)S(1)}, u32[]{:S(2)}, u32[]{:S(2)}) %collective-permute-start.9) | collective-permute-done | bytes 229408 | tf_op jit(solution)/shard_map/ppermute | solution.py:437
  72.8 0.4 collective-permute-start.10
  73.2 0.0 collective-permute-done.12.got
  73.2 2.7 %collective-permute-start.13 = (bf16[432,128]{1,0:T(8,128)(2,1)S(1)}, bf16[432,128]{1,0:T(8,128)(2,1)S(1)}, u32[]{:S(2)}, u32[]{:S(2)}) collective-permute-start(bf16[432,128]{1,0:T(8,128)(2,1)S(1)} %bitcast.25), channel_id=1, source_target_pairs={{0,8},{4,12},{8,0},{12,4},{1,9},{5,13},{9,1},{13,5},{2,10},{6,14},... | collective-permute-start | bytes 331784 | tf_op jit(solution)/shard_map/ppermute | solution.py:437
  75.9 0.7 unpack.1
  76.6 6.8 %collective-permute-done.13.out_got = bf16[432,128]{1,0:T(8,128)(2,1)S(1)} collective-permute-done((bf16[432,128]{1,0:T(8,128)(2,1)S(1)}, bf16[432,128]{1,0:T(8,128)(2,1)S(1)}, u32[]{:S(2)}, u32[]{:S(2)}) %collective-permute-start.13) | collective-permute-done | bytes 110624 | tf_op jit(solution)/shard_map/ppermute | solution.py:437
  83.4 0.0 collective-permute-done.10.in_got
  83.4 0.8 final.1
  (2 shorter events, 0.1 us)
Async XLA Ops:
  18.3 11.3 %copy-start.1 = (bf16[1,3456,256]{2,1,0:T(8,128)(2,1)S(1)}, bf16[1,3456,256]{2,1,0:T(8,128)(2,1)}, u32[]{:S(2)}) copy-start(bf16[1,3456,256]{2,1,0:T(8,128)(2,1)} %param.6) | copy-start | bytes 5308420
  23.8 5.8 %collective-permute-start.1 = (bf16[512,128]{1,0:T(8,128)(2,1)S(1)}, bf16[512,128]{1,0:T(8,128)(2,1)S(1)}, u32[]{:S(2)}, u32[]{:S(2)}) collective-permute-start(bf16[512,128]{1,0:T(8,128)(2,1)S(1)} %get-tuple-element.39.x1), channel_id=1, source_target_pairs={{0,16},{16,0},{1,17},{17,1},{2,18},{18,2},{3,19},{19,3},{4,20},{20... | collective-permute-start | bytes 393224 | tf_op jit(solution)/shard_map/ppermute | solution.py:437
  23.9 5.7 %collective-permute-start = (bf16[192,128]{1,0:T(8,128)(2,1)S(1)}, bf16[192,128]{1,0:T(8,128)(2,1)S(1)}, u32[]{:S(2)}, u32[]{:S(2)}) collective-permute-start(bf16[192,128]{1,0:T(8,128)(2,1)S(1)} %get-tuple-element.38), channel_id=1, source_target_pairs={{0,17},{17,0},{1,18},{18,1},{2,19},{19,2},{3,23},{23,3},{7,22},{22... | collective-permute-start | bytes 147464 | tf_op jit(solution)/shard_map/ppermute | solution.py:451
  27.0 2.7 %collective-permute-start.2 = (bf16[192,128]{1,0:T(8,128)(2,1)S(1)}, bf16[192,128]{1,0:T(8,128)(2,1)S(1)}, u32[]{:S(2)}, u32[]{:S(2)}) collective-permute-start(bf16[192,128]{1,0:T(8,128)(2,1)S(1)} %get-tuple-element.40), channel_id=1, source_target_pairs={{1,16},{16,1},{2,17},{17,2},{3,18},{18,3},{7,19},{19,7},{6,23},{23... | collective-permute-start | bytes 147464 | tf_op jit(solution)/shard_map/ppermute | solution.py:451
  29.6 10.3 %copy-start = (bf16[1,6912,128]{2,1,0:T(8,128)(2,1)S(1)}, bf16[1,6912,128]{2,1,0:T(8,128)(2,1)}, u32[]{:S(2)}) copy-start(bf16[1,6912,128]{2,1,0:T(8,128)(2,1)} %param.7) | copy-start | bytes 5308420
  30.0 9.9 %collective-permute-start.3 = (bf16[640,128]{1,0:T(8,128)(2,1)S(1)}, bf16[640,128]{1,0:T(8,128)(2,1)S(1)}, u32[]{:S(2)}, u32[]{:S(2)}) collective-permute-start(bf16[640,128]{1,0:T(8,128)(2,1)S(1)} %get-tuple-element.44), channel_id=1, source_target_pairs={{0,16},{16,0},{1,17},{17,1},{2,18},{18,2},{3,19},{19,3},{4,20},{20... | collective-permute-start | bytes 491528 | tf_op jit(solution)/shard_map/ppermute | solution.py:437
  36.6 8.5 %collective-permute-start.6 = (bf16[1280,128]{1,0:T(8,128)(2,1)S(1)}, bf16[1280,128]{1,0:T(8,128)(2,1)S(1)}, u32[]{:S(2)}, u32[]{:S(2)}) collective-permute-start(bf16[1280,128]{1,0:T(8,128)(2,1)S(1)} %get-tuple-element.46.a.v_mine), channel_id=1, source_target_pairs={{0,1},{1,0},{2,3},{3,2},{4,5},{5,4},{6,7},{7,6},{8,9},{9,8},{10,11... | collective-permute-start | bytes 983048 | tf_op jit(solution)/shard_map/ppermute | solution.py:437
  42.2 6.0 %collective-permute-start.5 = (bf16[512,256]{1,0:T(8,128)(2,1)S(1)}, bf16[512,256]{1,0:T(8,128)(2,1)S(1)}, u32[]{:S(2)}, u32[]{:S(2)}) collective-permute-start(bf16[512,256]{1,0:T(8,128)(2,1)S(1)} %get-tuple-element.52.u_mine), channel_id=1, source_target_pairs={{0,1},{1,0},{2,3},{3,2},{4,5},{5,4},{6,7},{7,6},{8,9},{9,8},{10,11... | collective-permute-start | bytes 786440 | tf_op jit(solution)/shard_map/ppermute | solution.py:437
  43.7 1.3 %collective-permute-start.7 = (bf16[512,128]{1,0:T(8,128)(2,1)S(1)}, bf16[512,128]{1,0:T(8,128)(2,1)S(1)}, u32[]{:S(2)}, u32[]{:S(2)}) collective-permute-start(bf16[512,128]{1,0:T(8,128)(2,1)S(1)} %get-tuple-element.50.u_mine), channel_id=1, source_target_pairs={{0,1},{1,0},{2,3},{3,2},{4,5},{5,4},{6,7},{7,6},{8,9},{9,8},{10,11... | collective-permute-start | bytes 393224 | tf_op jit(solution)/shard_map/ppermute | solution.py:437
  43.7 4.5 %collective-permute-start.4 = (bf16[640,128]{1,0:T(8,128)(2,1)S(1)}, bf16[640,128]{1,0:T(8,128)(2,1)S(1)}, u32[]{:S(2)}, u32[]{:S(2)}) collective-permute-start(bf16[640,128]{1,0:T(8,128)(2,1)S(1)} %get-tuple-element.45.x.v_mine), channel_id=1, source_target_pairs={{0,1},{1,0},{2,3},{3,2},{4,5},{5,4},{6,7},{7,6},{8,9},{9,8},{10,11... | collective-permute-start | bytes 491528 | tf_op jit(solution)/shard_map/ppermute | solution.py:437
  50.8 15.2 %collective-permute-start.8 = (bf16[4,448,128]{2,1,0:T(8,128)(2,1)S(1)}, bf16[4,448,128]{2,1,0:T(8,128)(2,1)S(1)}, u32[]{:S(2)}, u32[]{:S(2)}) collective-permute-start(bf16[4,448,128]{2,1,0:T(8,128)(2,1)S(1)} %get-tuple-element.57), channel_id=1, source_target_pairs={{0,4},{4,0},{8,12},{12,8},{1,5},{5,1},{9,13},{13,9},{2,6},{6,2},{1... | collective-permute-start | bytes 1376264 | tf_op jit(solution)/shard_map/ppermute | solution.py:437
  53.8 13.3 %collective-permute-start.11 = (bf16[4,432,128]{2,1,0:T(8,128)(2,1)}, bf16[4,432,128]{2,1,0:T(8,128)(2,1)S(1)}, u32[]{:S(2)}, u32[]{:S(2)}) collective-permute-start(bf16[4,432,128]{2,1,0:T(8,128)(2,1)} %get-tuple-element.66), channel_id=1, source_target_pairs={{0,2},{1,3},{2,0},{3,1},{4,6},{5,7},{6,4},{7,5},{8,10},{9,11},{10,... | collective-permute-start | bytes 1327112 | tf_op jit(solution)/shard_map/ppermute | solution.py:437
  54.2 13.7 %all-to-all-start.1 = ((bf16[16,32,128]{2,1,0:T(8,128)(2,1)}), bf16[16,32,128]{2,1,0:T(8,128)(2,1)S(1)}, u32[]{:S(2)}, u32[]{:S(2)}) async-start(bf16[16,32,128]{2,1,0:T(8,128)(2,1)} %bitcast.5), calls=%async_computation.1 | async-start | bytes 262144 | tf_op jit(solution)/shard_map/all_to_all | solution.py:441
  66.1 6.7 %collective-permute-start.9 = (bf16[2,448,128]{2,1,0:T(8,128)(2,1)S(1)}, bf16[2,448,128]{2,1,0:T(8,128)(2,1)S(1)}, u32[]{:S(2)}, u32[]{:S(2)}) collective-permute-start(bf16[2,448,128]{2,1,0:T(8,128)(2,1)S(1)} %get-tuple-element.58), channel_id=1, source_target_pairs={{0,2},{1,3},{2,0},{3,1},{4,6},{5,7},{6,4},{7,5},{8,10},{9,11},{10,... | collective-permute-start | bytes 688136 | tf_op jit(solution)/shard_map/ppermute | solution.py:437
  67.1 6.0 %collective-permute-start.12 = (bf16[2,432,128]{2,1,0:T(8,128)(2,1)S(1)}, bf16[2,432,128]{2,1,0:T(8,128)(2,1)S(1)}, u32[]{:S(2)}, u32[]{:S(2)}) collective-permute-start(bf16[2,432,128]{2,1,0:T(8,128)(2,1)S(1)} %get-tuple-element.68), channel_id=1, source_target_pairs={{0,4},{4,0},{8,12},{12,8},{1,5},{5,1},{9,13},{13,9},{2,6},{6,2},{1... | collective-permute-start | bytes 663560 | tf_op jit(solution)/shard_map/ppermute | solution.py:437
  72.8 10.6 %collective-permute-start.10 = (bf16[448,128]{1,0:T(8,128)(2,1)S(1)}, bf16[448,128]{1,0:T(8,128)(2,1)S(1)}, u32[]{:S(2)}, u32[]{:S(2)}) collective-permute-start(bf16[448,128]{1,0:T(8,128)(2,1)S(1)} %bitcast.24), channel_id=1, source_target_pairs={{0,8},{4,12},{8,0},{12,4},{1,9},{5,13},{9,1},{13,5},{2,10},{6,14},... | collective-permute-start | bytes 344072 | tf_op jit(solution)/shard_map/ppermute | solution.py:437
  73.2 10.1 %collective-permute-start.13 = (bf16[432,128]{1,0:T(8,128)(2,1)S(1)}, bf16[432,128]{1,0:T(8,128)(2,1)S(1)}, u32[]{:S(2)}, u32[]{:S(2)}) collective-permute-start(bf16[432,128]{1,0:T(8,128)(2,1)S(1)} %bitcast.25), channel_id=1, source_target_pairs={{0,8},{4,12},{8,0},{12,4},{1,9},{5,13},{9,1},{13,5},{2,10},{6,14},... | collective-permute-start | bytes 331784 | tf_op jit(solution)/shard_map/ppermute | solution.py:437

commit v5 on v4

--- a/solution.py
+++ b/solution.py
@@ -345,11 +345,19 @@
     return rows, -(-rows // 16) * 16
 
 
-def grad_kernel(
-    dims, c, masks, v_mine, v_beside, u_mine, u_beside, keep, send, p, ut, win
-):
+def streams_of(dims, c, c_out):
+    padded = chunk_of(dims, c)[1]
+    if c_out > LANES:
+        return [(padded, 0)] * (c_out // LANES)
+    head = -(-padded // 32) * 16
+    return [(head, 0), (padded - head, head)] if padded > head else [(padded, 0)]
+
+
+def grad_kernel(dims, c, masks, v_mine, v_beside, u_mine, u_beside, *refs):
     cell, own = dims.cell, dims.own
     cols = own + 2
+    p, ut, win = refs[-3:]
+    streams = streams_of(dims, c, ut.shape[0])
     for s, v in enumerate((v_mine, v_beside)):
         for w in range(cols):
             if c == dims.C:
@@ -366,7 +374,7 @@
             at = 3 * ti + j
             win[at * c : (at + 1) * c, :] = part[:, ti * c : (ti + 1) * c].T
     me = dims.my_device()
-    length, padded = chunk_of(dims, c)
+    length, _ = chunk_of(dims, c)
 
     def rows_of(mask):
         start = lax.bitwise_xor(me, mask) * length
@@ -379,13 +387,14 @@
 
     for at, mask in enumerate(masks):
         rows = rows_of(mask)
-        for h in range(rows.shape[1] // LANES):
-            piece = rows[:, h * LANES : (h + 1) * LANES]
-            to = slice(h * padded, h * padded + length)
+        for b, (count, head) in enumerate(streams):
+            lane = b * LANES if rows.shape[1] > LANES else 0
+            piece = rows[head : min(head + count, length), lane : lane + LANES]
+            to = slice(0, piece.shape[0])
             if at % 2 == 0:
-                keep[at // 2, to, :] = piece
+                refs[2 * b][at // 2, to, :] = piece
             else:
-                send[at // 2, to, :] = piece.astype(BF)
+                refs[2 * b + 1][at // 2, to, :] = piece.astype(BF)
 
 
 def add_kernel(keep, got, keep_out, send_out):
@@ -397,14 +406,18 @@
             send_out[at // 2] = v.astype(BF)
 
 
-def final_kernel(dims, in_keep, in_got, out_keep, out_got, in_out, out_out):
-    length, padded = chunk_of(dims, dims.C)
-    halves = dims.D // LANES
-    for h in range(halves):
-        rows = slice(h * padded, h * padded + length)
-        in_out[pl.ds(h, length, stride=halves), :] = in_keep[rows, :] + in_got[rows, :].astype(F32)
-    length = out_out.shape[0]
-    out_out[...] = out_keep[:length, :] + out_got[:length, :].astype(F32)
+def final_kernel(dims, n_in, *refs):
+    in_out, out_out = refs[-2:]
+    pairs = list(zip(refs[0:-2:2], refs[1:-2:2]))
+    length, _ = chunk_of(dims, dims.C)
+    for h, (keep, got) in enumerate(pairs[:n_in]):
+        rows = slice(0, length)
+        in_out[pl.ds(h, length, stride=n_in), :] = keep[rows, :] + got[rows, :].astype(F32)
+    first, length = 0, out_out.shape[0]
+    for keep, got in pairs[n_in:]:
+        count = min(keep.shape[0], length - first)
+        out_out[first : first + count, :] = keep[:count, :] + got[:count, :].astype(F32)
+        first += count
 
 
 def call(dims, kernel, shapes, ins, scratch, cost, name, vmem=None):
@@ -543,37 +556,47 @@
     half = len(in_masks) // 2
 
     def grad(c, c_out, masks, v, v_beside, u, u_beside, name):
-        rows = chunk_of(dims, c)[1] * (c_out // LANES)
-        return call(
-            dims, partial(grad_kernel, dims, c, masks),
-            (sds((half, rows, LANES), F32), sds((half, rows, LANES), BF)),
-            [vm] * 4,
+        shapes = []
+        for rows, _ in streams_of(dims, c, c_out):
+            shapes += [sds((half, rows, LANES), F32), sds((half, rows, LANES), BF)]
+        sums = call(
+            dims, partial(grad_kernel, dims, c, masks), tuple(shapes), [vm] * 4,
             [
                 scr((2 * (own + 2) * cell, 9 * c), BF), scr((c_out, 2 * own * cell), BF),
                 scr((27 * c + 64, c_out), F32),
             ],
             conv_flops * own, name,
         )(v, v_beside, u, u_beside)
-
-    out_keep, out_send = grad(D, C, out_masks, a2, a_beside, g, g_beside, "grad_out")
-    e, e_beside, out_send = lax.optimization_barrier((e, e_beside, out_send))
-    in_keep, in_send = grad(C, D, in_masks, x2, x_beside, e, e_beside, "grad_in")
-    sec, in_keep, out_keep = lax.optimization_barrier((sec, in_keep, out_keep))
-    back = exchanged(sec, n)
+        return [tuple(sums[at : at + 2]) for at in range(0, len(sums), 2)]
+
+    out_parts = grad(D, C, out_masks, a2, a_beside, g, g_beside, "grad_out")
+    e, e_beside, first_part = lax.optimization_barrier((e, e_beside, out_parts[0]))
+    out_parts[0] = first_part
+    in_parts = grad(C, D, in_masks, x2, x_beside, e, e_beside, "grad_in")
+    back = None
     for at in range(len(in_steps) - 1):
-        out_keep, out_send, back_out = added(
-            dims, out_keep, out_send, out_steps[at], "add_out", back if False else None
-        )
-        in_keep, in_send, back_in = added(
-            dims, in_keep, in_send, in_steps[at], "add_in", back if at == 1 else None
-        )
-        back = back if back_in is None else back_in
-    out_got = group_swap(out_send[0], *out_steps[-1][:2])
-    in_got = group_swap(in_send[0], *in_steps[-1][:2])
+        for parts, steps, name in (
+            (out_parts, out_steps, "add_out"), (in_parts, in_steps, "add_in")
+        ):
+            for b, (keep, sent) in enumerate(parts):
+                last = at == 1 and parts is in_parts and b == len(parts) - 1
+                keep, sent, also = added(
+                    dims, keep, sent, steps[at], name, back if last else None
+                )
+                back = also if last else back
+                if at == 0 and parts is out_parts and b == 0:
+                    sec, keep, sent = lax.optimization_barrier((sec, keep, sent))
+                    back = exchanged(sec, n)
+                parts[b] = (keep, sent)
+    ends = []
+    for parts, step in ((in_parts, in_steps[-1]), (out_parts, out_steps[-1])):
+        for keep, sent in parts:
+            ends += [keep[0], group_swap(sent[0], *step[:2])]
     shard = 27 * C * D // n // LANES
     in_sum, out_sum = call(
-        dims, partial(final_kernel, dims), (sds((shard, LANES), F32),) * 2, [vm] * 4, [], 0, "final",
-    )(in_keep[0], in_got, out_keep[0], out_got)
+        dims, partial(final_kernel, dims, len(in_parts)), (sds((shard, LANES), F32),) * 2,
+        [vm] * len(ends), [], 0, "final",
+    )(*ends)
 
     sections = call(
         dims, partial(unpack_kernel, dims), sds((fr, W, C), BF), [vm],

time: 84.5 us -> 83.2 us (0.985)
  waiting for transfers between devices: 24.8 us -> 11 us
  starting transfers between devices: 25.4 us -> 38.7 us
    ppermute x12 -> x18, waiting for transfers between devices: 22.8 us -> 8.95 us  [group_swap(): return lax.ppermute(block, axis, [(i, i ^ apart) for i in range(count)])]
    ppermute x12 -> x18, starting transfers between devices: 18.2 us -> 29.5 us  [group_swap(): return lax.ppermute(block, axis, [(i, i ^ apart) for i in range(count)])]
    all_to_all x1, starting transfers between devices: 3.51 us -> 5.49 us  [exchanged(): lax.all_to_all(blocks.reshape(n, -1, blocks.shape[1]), ('tm', 'rows'), 0, 0)]
  transfers between devices with their start and end apart: 15 -> 21, of which waited for: 7 -> 6; matrix products, arithmetic and copies ran while one was open for 0% -> 0% of each run, Pallas kernels for 8% -> 10%
where the time goes in v5:
time: 83.2 us; the launch traced here: 82.9 us
  starting transfers between devices  38.7 us (47%)
  blocking collectives  16.7 us (20%)
  Pallas kernels  14.8 us (18%)
  waiting for transfers between devices  11 us (13%)
  other arithmetic  0.93 us (1%)
    ppermute x18, starting transfers between devices, group_swap(): return lax.ppermute(block, axis, [(i, i ^ apart) for i in range(count)])  29.5 us
    all_to_all x1, blocking collectives, exchanged(): lax.all_to_all(blocks.reshape(n, -1, blocks.shape[1]), ('tm', 'rows'), 0, 0)  16.7 us
    ppermute x18, waiting for transfers between devices, group_swap(): return lax.ppermute(block, axis, [(i, i ^ apart) for i in range(count)])  8.95 us
    all_to_all x1, starting transfers between devices, exchanged(): lax.all_to_all(blocks.reshape(n, -1, blocks.shape[1]), ('tm', 'rows'), 0, 0)  5.49 us
    pallas_call x1, Pallas kernels, on_device(): call(dims, partial(first_kernel, dims), (x_shape, a_shape, sds((own * cel...  5.48 us
    pallas_call x2, Pallas kernels, grad(): call(dims, partial(grad_kernel, dims, c, masks), tuple(shapes), [vm] * 4,...  4.91 us
    ppermute x2, starting transfers between devices, edge_swap(): return lax.ppermute(block, ('segment', 'tm', 'rows'), pairs)  3.72 us
    pallas_call x1, Pallas kernels, on_device(): call(dims, partial(third_kernel, dims), (sds((own * cell, D), BF), sds((o...  2.29 us
  transfers between devices with their start and end apart: 21, of which 6 were waited for; matrix products, arithmetic and copies ran while one was open for 0% of the time, Pallas kernels for 10%

profile of v5, /device:TPU:0, one launch (start us, length us, event | category | flops | bytes accessed | tf_op | source)
XLA Modules:
  0.0 82.9 jit_solution(8457856030395042638)
XLA Ops:
  0.6 0.9 %broadcast_select_fusion = bf16[2,2,128,128]{3,2,1,0:T(8,128)(2,1)S(1)} fusion(bf16[2,2,128,128]{3,2,1,0:T(8,128)(2,1)} %param.4, bf16[2,2,128,128]{3,2,1,0:T(8,128)(2,1)} %param.5, pred[]{:T(512)S(6)} %eq.3), kind=kLoop, calls=%fused_computation | loop fusion | flops 65536 | bytes 393217 | tf_op jit(solution)/shard_map/jit(_where)/select_n | solution.py:501
  1.6 0.1 pack.1
  1.6 16.7 %all_to_all.10 = bf16[16,56,128]{2,1,0:T(8,128)(2,1)S(1)} all-to-all(bf16[16,56,128]{2,1,0:T(8,128)(2,1)S(1)} %bitcast.20), channel_id=1, replica_groups=mesh['segment'=2,'tm'=4,'rows'=4] {'tm','rows'}, dimensions={0} | all-to-all | bytes 458752 | tf_op jit(solution)/shard_map/all_to_all | solution.py:454
  18.3 0.0 copy-start.1
  18.3 5.5 %first.1 = (bf16[640,128]{1,0:T(8,128)(2,1)S(1)}, bf16[1280,128]{1,0:T(8,128)(2,1)S(1)}, bf16[512,128]{1,0:T(8,128)(2,1)S(1)}, bf16[192,128]{1,0:T(8,128)(2,1)S(...) custom-call(bf16[896,128]{1,0:T(8,128)(2,1)S(1)} %bitcast.23, bf16[3456,256]{1,0:T(8,128)(2,1)} %bitcast.28, ...), custom_call_target="tpu_custom_call" | custom-call | flops 2264924160 | bytes 4194304 | tf_op jit(solution)/shard_map/first/pallas_call | solution.py:504
  23.8 0.1 collective-permute-start.1
  23.9 3.1 %collective-permute-start = (bf16[192,128]{1,0:T(8,128)(2,1)S(1)}, bf16[192,128]{1,0:T(8,128)(2,1)S(1)}, u32[]{:S(2)}, u32[]{:S(2)}) collective-permute-start(bf16[192,128]{1,0:T(8,128)(2,1)S(1)} %get-tuple-element.51), channel_id=1, source_target_pairs={{0,17},{17,0},{1,18},{18,1},{2,19},{19,2},{3,23},{23,3},{7,22},{22... | collective-permute-start | bytes 147464 | tf_op jit(solution)/shard_map/ppermute | solution.py:464
  27.0 0.7 collective-permute-start.2
  27.6 2.0 %collective-permute-done.refs_0_ = bf16[192,128]{1,0:T(8,128)(2,1)S(1)} collective-permute-done((bf16[192,128]{1,0:T(8,128)(2,1)S(1)}, bf16[192,128]{1,0:T(8,128)(2,1)S(1)}, u32[]{:S(2)}, u32[]{:S(2)}) %collective-permute-start) | collective-permute-done | bytes 49184 | tf_op jit(solution)/shard_map/ppermute | solution.py:464
  29.6 0.0 collective-permute-done.2.refs_2_
  29.6 0.0 collective-permute-done.1.refs_1_
  29.6 0.0 copy-done.1
  29.6 0.0 copy-start
  29.7 0.4 second.1
  30.0 6.5 %collective-permute-start.4 = (bf16[640,128]{1,0:T(8,128)(2,1)S(1)}, bf16[640,128]{1,0:T(8,128)(2,1)S(1)}, u32[]{:S(2)}, u32[]{:S(2)}) collective-permute-start(bf16[640,128]{1,0:T(8,128)(2,1)S(1)} %get-tuple-element.58), channel_id=1, source_target_pairs={{0,16},{16,0},{1,17},{17,1},{2,18},{18,2},{3,19},{19,3},{4,20},{20... | collective-permute-start | bytes 491528 | tf_op jit(solution)/shard_map/ppermute | solution.py:450
  36.6 2.0 %collective-permute-start.6 = (bf16[1280,128]{1,0:T(8,128)(2,1)S(1)}, bf16[1280,128]{1,0:T(8,128)(2,1)S(1)}, u32[]{:S(2)}, u32[]{:S(2)}) collective-permute-start(bf16[1280,128]{1,0:T(8,128)(2,1)S(1)} %get-tuple-element.59.a.v_mine), channel_id=1, source_target_pairs={{0,1},{1,0},{2,3},{3,2},{4,5},{5,4},{6,7},{7,6},{8,9},{9,8},{10,11... | collective-permute-start | bytes 983048 | tf_op jit(solution)/shard_map/ppermute | solution.py:450
  38.6 1.4 %collective-permute-done.4.g0 = bf16[640,128]{1,0:T(8,128)(2,1)S(1)} collective-permute-done((bf16[640,128]{1,0:T(8,128)(2,1)S(1)}, bf16[640,128]{1,0:T(8,128)(2,1)S(1)}, u32[]{:S(2)}, u32[]{:S(2)}) %collective-permute-start.4) | collective-permute-done | bytes 163872 | tf_op jit(solution)/shard_map/ppermute | solution.py:450
  39.9 0.0 copy-done
  39.9 2.3 %third.1 = (bf16[512,256]{1,0:T(8,128)(2,1)S(1)}, bf16[512,128]{1,0:T(8,128)(2,1)S(1)}, bf16[512,128]{1,0:T(8,128)(2,1)}) custom-call(bf16[640,128]{1,0:T(8,128)(2,1)S(1)} %collective-permute-done.4.g0, f32[768,256]{1,0:T(8,128)S(1)} %get-tuple-element.54.refs_3_.hd, bf16[512,128]{1,0:T(8,128)(2,1)S(1)} %get-tuple-element.52.x1, ...), custom_call_target="tpu_custom_call" | custom-call | flops 905969664 | bytes 4194304 | tf_op jit(solution)/shard_map/third/pallas_call | solution.py:540
  42.2 1.5 %collective-permute-start.5 = (bf16[512,256]{1,0:T(8,128)(2,1)S(1)}, bf16[512,256]{1,0:T(8,128)(2,1)S(1)}, u32[]{:S(2)}, u32[]{:S(2)}) collective-permute-start(bf16[512,256]{1,0:T(8,128)(2,1)S(1)} %get-tuple-element.65.u_mine), channel_id=1, source_target_pairs={{0,1},{1,0},{2,3},{3,2},{4,5},{5,4},{6,7},{7,6},{8,9},{9,8},{10,11... | collective-permute-start | bytes 786440 | tf_op jit(solution)/shard_map/ppermute | solution.py:450
  43.7 0.0 collective-permute-start.7
  43.7 0.5 collective-permute-start.3
  44.2 0.8 %collective-permute-done.7.u_beside = bf16[512,128]{1,0:T(8,128)(2,1)S(1)} collective-permute-done((bf16[512,128]{1,0:T(8,128)(2,1)S(1)}, bf16[512,128]{1,0:T(8,128)(2,1)S(1)}, u32[]{:S(2)}, u32[]{:S(2)}) %collective-permute-start.7) | collective-permute-done | bytes 131104 | tf_op jit(solution)/shard_map/ppermute | solution.py:450
  45.1 0.0 collective-permute-done.6.v_beside
  45.1 2.4 %grad_out.1 = (f32[4,224,128]{2,1,0:T(8,128)S(1)}, bf16[4,224,128]{2,1,0:T(8,128)(2,1)S(1)}, f32[4,208,128]{2,1,0:T(8,128)S(1)}, bf16[4,208,128]{2,1,0:T(8,128)(2,1)S(1)}) custom-call(bf16[1280,128]{1,0:T(8,128)(2,1)S(1)} %get-tuple-element.59.a.v_mine, bf16[1280,128]{1,0:T(8,128)(2,1)S(1)} %collective-permute-done.6.v_beside, ...), custom_call_target="tpu_custom_call" | custom-call | flops 905969664 | bytes 4194304 | tf_op jit(solution)/shard_map/grad_out/pallas_call | solution.py:562
  47.5 0.0 collective-permute-done.5.u_beside
  47.5 1.6 %collective-permute-start.10 = (bf16[4,224,128]{2,1,0:T(8,128)(2,1)S(1)}, bf16[4,224,128]{2,1,0:T(8,128)(2,1)S(1)}, u32[]{:S(2)}, u32[]{:S(2)}) collective-permute-start(bf16[4,224,128]{2,1,0:T(8,128)(2,1)S(1)} %get-tuple-element.72), channel_id=1, source_target_pairs={{0,2},{1,3},{2,0},{3,1},{4,6},{5,7},{6,4},{7,5},{8,10},{9,11},{10,... | collective-permute-start | bytes 688136 | tf_op jit(solution)/shard_map/ppermute | solution.py:450
  49.1 0.0 collective-permute-done.3.v_beside
  49.1 2.5 %grad_in.1 = (f32[4,224,128]{2,1,0:T(8,128)S(1)}, bf16[4,224,128]{2,1,0:T(8,128)(2,1)S(1)}, f32[4,224,128]{2,1,0:T(8,128)S(1)}, bf16[4,224,128]{2,1,0:T(8,128)(2,1)S(1)}) custom-call(bf16[640,128]{1,0:T(8,128)(2,1)S(1)} %get-tuple-element.57.x.v_mine, bf16[640,128]{1,0:T(8,128)(2,1)S(1)} %collective-permute-done.3.v_beside, ...), custom_call_target="tpu_custom_call" | custom-call | flops 905969664 | bytes 4194304 | tf_op jit(solution)/shard_map/grad_in/pallas_call | solution.py:562
  51.7 1.8 %collective-permute-start.11 = (bf16[4,224,128]{2,1,0:T(8,128)(2,1)S(1)}, bf16[4,224,128]{2,1,0:T(8,128)(2,1)S(1)}, u32[]{:S(2)}, u32[]{:S(2)}) collective-permute-start(bf16[4,224,128]{2,1,0:T(8,128)(2,1)S(1)} %get-tuple-element.78), channel_id=1, source_target_pairs={{0,4},{4,0},{8,12},{12,8},{1,5},{5,1},{9,13},{13,9},{2,6},{6,2},{1... | collective-permute-start | bytes 688136 | tf_op jit(solution)/shard_map/ppermute | solution.py:450
  53.5 0.3 collective-permute-start.8
  53.8 1.4 %collective-permute-start.17 = (bf16[4,208,128]{2,1,0:T(8,128)(2,1)S(1)}, bf16[4,208,128]{2,1,0:T(8,128)(2,1)S(1)}, u32[]{:S(2)}, u32[]{:S(2)}) collective-permute-start(bf16[4,208,128]{2,1,0:T(8,128)(2,1)S(1)} %get-tuple-element.92), channel_id=1, source_target_pairs={{0,2},{1,3},{2,0},{3,1},{4,6},{5,7},{6,4},{7,5},{8,10},{9,11},{10,... | collective-permute-start | bytes 638984 | tf_op jit(solution)/shard_map/ppermute | solution.py:450
  55.2 0.2 collective-permute-done.10.got
  55.5 5.5 %all-to-all-start.1 = ((bf16[16,32,128]{2,1,0:T(8,128)(2,1)}), bf16[16,32,128]{2,1,0:T(8,128)(2,1)S(1)}, u32[]{:S(2)}, u32[]{:S(2)}) async-start(bf16[16,32,128]{2,1,0:T(8,128)(2,1)} %bitcast.5), calls=%async_computation.1 | async-start | bytes 262144 | tf_op jit(solution)/shard_map/all_to_all | solution.py:454
  61.0 1.9 %collective-permute-start.15 = (bf16[2,224,128]{2,1,0:T(8,128)(2,1)S(1)}, bf16[2,224,128]{2,1,0:T(8,128)(2,1)S(1)}, u32[]{:S(2)}, u32[]{:S(2)}) collective-permute-start(bf16[2,224,128]{2,1,0:T(8,128)(2,1)S(1)} %get-tuple-element.88), channel_id=1, source_target_pairs={{0,4},{4,0},{8,12},{12,8},{1,5},{5,1},{9,13},{13,9},{2,6},{6,2},{1... | collective-permute-start | bytes 344072 | tf_op jit(solution)/shard_map/ppermute | solution.py:450
  62.9 0.0 collective-permute-done.11.got
  62.9 1.5 %collective-permute-start.12 = (bf16[2,224,128]{2,1,0:T(8,128)(2,1)S(1)}, bf16[2,224,128]{2,1,0:T(8,128)(2,1)S(1)}, u32[]{:S(2)}, u32[]{:S(2)}) collective-permute-start(bf16[2,224,128]{2,1,0:T(8,128)(2,1)S(1)} %get-tuple-element.80), channel_id=1, source_target_pairs={{0,2},{1,3},{2,0},{3,1},{4,6},{5,7},{6,4},{7,5},{8,10},{9,11},{10,... | collective-permute-start | bytes 344072 | tf_op jit(solution)/shard_map/ppermute | solution.py:450
  64.5 0.0 collective-permute-done.8.got
  64.5 1.6 %collective-permute-start.9 = (bf16[2,224,128]{2,1,0:T(8,128)(2,1)S(1)}, bf16[2,224,128]{2,1,0:T(8,128)(2,1)S(1)}, u32[]{:S(2)}, u32[]{:S(2)}) collective-permute-start(bf16[2,224,128]{2,1,0:T(8,128)(2,1)S(1)} %get-tuple-element.69), channel_id=1, source_target_pairs={{0,2},{1,3},{2,0},{3,1},{4,6},{5,7},{6,4},{7,5},{8,10},{9,11},{10,... | collective-permute-start | bytes 344072 | tf_op jit(solution)/shard_map/ppermute | solution.py:450
  66.1 0.0 collective-permute-done.17.got
  66.2 2.5 %collective-permute-start.18 = (bf16[2,208,128]{2,1,0:T(8,128)(2,1)S(1)}, bf16[2,208,128]{2,1,0:T(8,128)(2,1)S(1)}, u32[]{:S(2)}, u32[]{:S(2)}) collective-permute-start(bf16[2,208,128]{2,1,0:T(8,128)(2,1)S(1)} %get-tuple-element.94), channel_id=1, source_target_pairs={{0,4},{4,0},{8,12},{12,8},{1,5},{5,1},{9,13},{13,9},{2,6},{6,2},{1... | collective-permute-start | bytes 319496 | tf_op jit(solution)/shard_map/ppermute | solution.py:450
  68.7 0.4 collective-permute-done.15.got
  69.2 2.4 %collective-permute-start.16 = (bf16[224,128]{1,0:T(8,128)(2,1)S(1)}, bf16[224,128]{1,0:T(8,128)(2,1)S(1)}, u32[]{:S(2)}, u32[]{:S(2)}) collective-permute-start(bf16[224,128]{1,0:T(8,128)(2,1)S(1)} %bitcast.30), channel_id=1, source_target_pairs={{0,8},{4,12},{8,0},{12,4},{1,9},{5,13},{9,1},{13,5},{2,10},{6,14},... | collective-permute-start | bytes 172040 | tf_op jit(solution)/shard_map/ppermute | solution.py:450
  71.6 0.0 collective-permute-done.12.got
  71.6 0.6 collective-permute-start.13
  72.2 0.0 collective-permute-done.9.got
  72.2 0.0 all-to-all-done.1
  72.3 2.4 %collective-permute-start.14 = (bf16[224,128]{1,0:T(8,128)(2,1)S(1)}, bf16[224,128]{1,0:T(8,128)(2,1)S(1)}, u32[]{:S(2)}, u32[]{:S(2)}) collective-permute-start(bf16[224,128]{1,0:T(8,128)(2,1)S(1)} %bitcast.32), channel_id=1, source_target_pairs={{0,8},{4,12},{8,0},{12,4},{1,9},{5,13},{9,1},{13,5},{2,10},{6,14},... | collective-permute-start | bytes 172040 | tf_op jit(solution)/shard_map/ppermute | solution.py:450
  74.7 0.0 collective-permute-done.18.got
  74.7 0.6 collective-permute-start.19
  75.4 0.7 unpack.1
  76.0 6.1 %collective-permute-done.19.refs_7_ = bf16[208,128]{1,0:T(8,128)(2,1)S(1)} collective-permute-done((bf16[208,128]{1,0:T(8,128)(2,1)S(1)}, bf16[208,128]{1,0:T(8,128)(2,1)S(1)}, u32[]{:S(2)}, u32[]{:S(2)}) %collective-permute-start.19) | collective-permute-done | bytes 53280 | tf_op jit(solution)/shard_map/ppermute | solution.py:450
  82.1 0.0 collective-permute-done.16.refs_5_
  82.1 0.0 collective-permute-done.13.refs_1_
  82.1 0.0 collective-permute-done.14.refs_3_
  82.1 0.8 final.1
  (8 shorter events, 0.3 us)
Async XLA Ops:
  18.3 11.3 %copy-start.1 = (bf16[1,3456,256]{2,1,0:T(8,128)(2,1)S(1)}, bf16[1,3456,256]{2,1,0:T(8,128)(2,1)}, u32[]{:S(2)}) copy-start(bf16[1,3456,256]{2,1,0:T(8,128)(2,1)} %param.6) | copy-start | bytes 5308420
  23.8 5.8 %collective-permute-start.1 = (bf16[512,128]{1,0:T(8,128)(2,1)S(1)}, bf16[512,128]{1,0:T(8,128)(2,1)S(1)}, u32[]{:S(2)}, u32[]{:S(2)}) collective-permute-start(bf16[512,128]{1,0:T(8,128)(2,1)S(1)} %get-tuple-element.52.x1), channel_id=1, source_target_pairs={{0,16},{16,0},{1,17},{17,1},{2,18},{18,2},{3,19},{19,3},{4,20},{20... | collective-permute-start | bytes 393224 | tf_op jit(solution)/shard_map/ppermute | solution.py:450
  23.9 5.7 %collective-permute-start = (bf16[192,128]{1,0:T(8,128)(2,1)S(1)}, bf16[192,128]{1,0:T(8,128)(2,1)S(1)}, u32[]{:S(2)}, u32[]{:S(2)}) collective-permute-start(bf16[192,128]{1,0:T(8,128)(2,1)S(1)} %get-tuple-element.51), channel_id=1, source_target_pairs={{0,17},{17,0},{1,18},{18,1},{2,19},{19,2},{3,23},{23,3},{7,22},{22... | collective-permute-start | bytes 147464 | tf_op jit(solution)/shard_map/ppermute | solution.py:464
  27.0 2.7 %collective-permute-start.2 = (bf16[192,128]{1,0:T(8,128)(2,1)S(1)}, bf16[192,128]{1,0:T(8,128)(2,1)S(1)}, u32[]{:S(2)}, u32[]{:S(2)}) collective-permute-start(bf16[192,128]{1,0:T(8,128)(2,1)S(1)} %get-tuple-element.53), channel_id=1, source_target_pairs={{1,16},{16,1},{2,17},{17,2},{3,18},{18,3},{7,19},{19,7},{6,23},{23... | collective-permute-start | bytes 147464 | tf_op jit(solution)/shard_map/ppermute | solution.py:464
  29.6 10.3 %copy-start = (bf16[1,6912,128]{2,1,0:T(8,128)(2,1)S(1)}, bf16[1,6912,128]{2,1,0:T(8,128)(2,1)}, u32[]{:S(2)}) copy-start(bf16[1,6912,128]{2,1,0:T(8,128)(2,1)} %param.7) | copy-start | bytes 5308420
  30.0 9.9 %collective-permute-start.4 = (bf16[640,128]{1,0:T(8,128)(2,1)S(1)}, bf16[640,128]{1,0:T(8,128)(2,1)S(1)}, u32[]{:S(2)}, u32[]{:S(2)}) collective-permute-start(bf16[640,128]{1,0:T(8,128)(2,1)S(1)} %get-tuple-element.58), channel_id=1, source_target_pairs={{0,16},{16,0},{1,17},{17,1},{2,18},{18,2},{3,19},{19,3},{4,20},{20... | collective-permute-start | bytes 491528 | tf_op jit(solution)/shard_map/ppermute | solution.py:450
  36.6 8.5 %collective-permute-start.6 = (bf16[1280,128]{1,0:T(8,128)(2,1)S(1)}, bf16[1280,128]{1,0:T(8,128)(2,1)S(1)}, u32[]{:S(2)}, u32[]{:S(2)}) collective-permute-start(bf16[1280,128]{1,0:T(8,128)(2,1)S(1)} %get-tuple-element.59.a.v_mine), channel_id=1, source_target_pairs={{0,1},{1,0},{2,3},{3,2},{4,5},{5,4},{6,7},{7,6},{8,9},{9,8},{10,11... | collective-permute-start | bytes 983048 | tf_op jit(solution)/shard_map/ppermute | solution.py:450
  42.2 5.2 %collective-permute-start.5 = (bf16[512,256]{1,0:T(8,128)(2,1)S(1)}, bf16[512,256]{1,0:T(8,128)(2,1)S(1)}, u32[]{:S(2)}, u32[]{:S(2)}) collective-permute-start(bf16[512,256]{1,0:T(8,128)(2,1)S(1)} %get-tuple-element.65.u_mine), channel_id=1, source_target_pairs={{0,1},{1,0},{2,3},{3,2},{4,5},{5,4},{6,7},{7,6},{8,9},{9,8},{10,11... | collective-permute-start | bytes 786440 | tf_op jit(solution)/shard_map/ppermute | solution.py:450
  43.7 1.3 %collective-permute-start.7 = (bf16[512,128]{1,0:T(8,128)(2,1)S(1)}, bf16[512,128]{1,0:T(8,128)(2,1)S(1)}, u32[]{:S(2)}, u32[]{:S(2)}) collective-permute-start(bf16[512,128]{1,0:T(8,128)(2,1)S(1)} %get-tuple-element.62.u_mine), channel_id=1, source_target_pairs={{0,1},{1,0},{2,3},{3,2},{4,5},{5,4},{6,7},{7,6},{8,9},{9,8},{10,11... | collective-permute-start | bytes 393224 | tf_op jit(solution)/shard_map/ppermute | solution.py:450
  43.7 5.4 %collective-permute-start.3 = (bf16[640,128]{1,0:T(8,128)(2,1)S(1)}, bf16[640,128]{1,0:T(8,128)(2,1)S(1)}, u32[]{:S(2)}, u32[]{:S(2)}) collective-permute-start(bf16[640,128]{1,0:T(8,128)(2,1)S(1)} %get-tuple-element.57.x.v_mine), channel_id=1, source_target_pairs={{0,1},{1,0},{2,3},{3,2},{4,5},{5,4},{6,7},{7,6},{8,9},{9,8},{10,11... | collective-permute-start | bytes 491528 | tf_op jit(solution)/shard_map/ppermute | solution.py:450
  47.5 7.9 %collective-permute-start.10 = (bf16[4,224,128]{2,1,0:T(8,128)(2,1)S(1)}, bf16[4,224,128]{2,1,0:T(8,128)(2,1)S(1)}, u32[]{:S(2)}, u32[]{:S(2)}) collective-permute-start(bf16[4,224,128]{2,1,0:T(8,128)(2,1)S(1)} %get-tuple-element.72), channel_id=1, source_target_pairs={{0,2},{1,3},{2,0},{3,1},{4,6},{5,7},{6,4},{7,5},{8,10},{9,11},{10,... | collective-permute-start | bytes 688136 | tf_op jit(solution)/shard_map/ppermute | solution.py:450
  51.7 11.2 %collective-permute-start.11 = (bf16[4,224,128]{2,1,0:T(8,128)(2,1)S(1)}, bf16[4,224,128]{2,1,0:T(8,128)(2,1)S(1)}, u32[]{:S(2)}, u32[]{:S(2)}) collective-permute-start(bf16[4,224,128]{2,1,0:T(8,128)(2,1)S(1)} %get-tuple-element.78), channel_id=1, source_target_pairs={{0,4},{4,0},{8,12},{12,8},{1,5},{5,1},{9,13},{13,9},{2,6},{6,2},{1... | collective-permute-start | bytes 688136 | tf_op jit(solution)/shard_map/ppermute | solution.py:450
  53.5 11.0 %collective-permute-start.8 = (bf16[4,224,128]{2,1,0:T(8,128)(2,1)S(1)}, bf16[4,224,128]{2,1,0:T(8,128)(2,1)S(1)}, u32[]{:S(2)}, u32[]{:S(2)}) collective-permute-start(bf16[4,224,128]{2,1,0:T(8,128)(2,1)S(1)} %get-tuple-element.68), channel_id=1, source_target_pairs={{0,4},{4,0},{8,12},{12,8},{1,5},{5,1},{9,13},{13,9},{2,6},{6,2},{1... | collective-permute-start | bytes 688136 | tf_op jit(solution)/shard_map/ppermute | solution.py:450
  53.8 12.4 %collective-permute-start.17 = (bf16[4,208,128]{2,1,0:T(8,128)(2,1)S(1)}, bf16[4,208,128]{2,1,0:T(8,128)(2,1)S(1)}, u32[]{:S(2)}, u32[]{:S(2)}) collective-permute-start(bf16[4,208,128]{2,1,0:T(8,128)(2,1)S(1)} %get-tuple-element.92), channel_id=1, source_target_pairs={{0,2},{1,3},{2,0},{3,1},{4,6},{5,7},{6,4},{7,5},{8,10},{9,11},{10,... | collective-permute-start | bytes 638984 | tf_op jit(solution)/shard_map/ppermute | solution.py:450
  55.5 16.8 %all-to-all-start.1 = ((bf16[16,32,128]{2,1,0:T(8,128)(2,1)}), bf16[16,32,128]{2,1,0:T(8,128)(2,1)S(1)}, u32[]{:S(2)}, u32[]{:S(2)}) async-start(bf16[16,32,128]{2,1,0:T(8,128)(2,1)} %bitcast.5), calls=%async_computation.1 | async-start | bytes 262144 | tf_op jit(solution)/shard_map/all_to_all | solution.py:454
  61.0 8.2 %collective-permute-start.15 = (bf16[2,224,128]{2,1,0:T(8,128)(2,1)S(1)}, bf16[2,224,128]{2,1,0:T(8,128)(2,1)S(1)}, u32[]{:S(2)}, u32[]{:S(2)}) collective-permute-start(bf16[2,224,128]{2,1,0:T(8,128)(2,1)S(1)} %get-tuple-element.88), channel_id=1, source_target_pairs={{0,4},{4,0},{8,12},{12,8},{1,5},{5,1},{9,13},{13,9},{2,6},{6,2},{1... | collective-permute-start | bytes 344072 | tf_op jit(solution)/shard_map/ppermute | solution.py:450
  62.9 8.7 %collective-permute-start.12 = (bf16[2,224,128]{2,1,0:T(8,128)(2,1)S(1)}, bf16[2,224,128]{2,1,0:T(8,128)(2,1)S(1)}, u32[]{:S(2)}, u32[]{:S(2)}) collective-permute-start(bf16[2,224,128]{2,1,0:T(8,128)(2,1)S(1)} %get-tuple-element.80), channel_id=1, source_target_pairs={{0,2},{1,3},{2,0},{3,1},{4,6},{5,7},{6,4},{7,5},{8,10},{9,11},{10,... | collective-permute-start | bytes 344072 | tf_op jit(solution)/shard_map/ppermute | solution.py:450
  64.5 7.7 %collective-permute-start.9 = (bf16[2,224,128]{2,1,0:T(8,128)(2,1)S(1)}, bf16[2,224,128]{2,1,0:T(8,128)(2,1)S(1)}, u32[]{:S(2)}, u32[]{:S(2)}) collective-permute-start(bf16[2,224,128]{2,1,0:T(8,128)(2,1)S(1)} %get-tuple-element.69), channel_id=1, source_target_pairs={{0,2},{1,3},{2,0},{3,1},{4,6},{5,7},{6,4},{7,5},{8,10},{9,11},{10,... | collective-permute-start | bytes 344072 | tf_op jit(solution)/shard_map/ppermute | solution.py:450
  66.2 8.5 %collective-permute-start.18 = (bf16[2,208,128]{2,1,0:T(8,128)(2,1)S(1)}, bf16[2,208,128]{2,1,0:T(8,128)(2,1)S(1)}, u32[]{:S(2)}, u32[]{:S(2)}) collective-permute-start(bf16[2,208,128]{2,1,0:T(8,128)(2,1)S(1)} %get-tuple-element.94), channel_id=1, source_target_pairs={{0,4},{4,0},{8,12},{12,8},{1,5},{5,1},{9,13},{13,9},{2,6},{6,2},{1... | collective-permute-start | bytes 319496 | tf_op jit(solution)/shard_map/ppermute | solution.py:450
  69.2 13.0 %collective-permute-start.16 = (bf16[224,128]{1,0:T(8,128)(2,1)S(1)}, bf16[224,128]{1,0:T(8,128)(2,1)S(1)}, u32[]{:S(2)}, u32[]{:S(2)}) collective-permute-start(bf16[224,128]{1,0:T(8,128)(2,1)S(1)} %bitcast.30), channel_id=1, source_target_pairs={{0,8},{4,12},{8,0},{12,4},{1,9},{5,13},{9,1},{13,5},{2,10},{6,14},... | collective-permute-start | bytes 172040 | tf_op jit(solution)/shard_map/ppermute | solution.py:450
  71.6 10.5 %collective-permute-start.13 = (bf16[224,128]{1,0:T(8,128)(2,1)S(1)}, bf16[224,128]{1,0:T(8,128)(2,1)S(1)}, u32[]{:S(2)}, u32[]{:S(2)}) collective-permute-start(bf16[224,128]{1,0:T(8,128)(2,1)S(1)} %bitcast.31), channel_id=1, source_target_pairs={{0,8},{4,12},{8,0},{12,4},{1,9},{5,13},{9,1},{13,5},{2,10},{6,14},... | collective-permute-start | bytes 172040 | tf_op jit(solution)/shard_map/ppermute | solution.py:450
  72.3 9.8 %collective-permute-start.14 = (bf16[224,128]{1,0:T(8,128)(2,1)S(1)}, bf16[224,128]{1,0:T(8,128)(2,1)S(1)}, u32[]{:S(2)}, u32[]{:S(2)}) collective-permute-start(bf16[224,128]{1,0:T(8,128)(2,1)S(1)} %bitcast.32), channel_id=1, source_target_pairs={{0,8},{4,12},{8,0},{12,4},{1,9},{5,13},{9,1},{13,5},{2,10},{6,14},... | collective-permute-start | bytes 172040 | tf_op jit(solution)/shard_map/ppermute | solution.py:450
  74.7 7.4 %collective-permute-start.19 = (bf16[208,128]{1,0:T(8,128)(2,1)S(1)}, bf16[208,128]{1,0:T(8,128)(2,1)S(1)}, u32[]{:S(2)}, u32[]{:S(2)}) collective-permute-start(bf16[208,128]{1,0:T(8,128)(2,1)S(1)} %bitcast.33), channel_id=1, source_target_pairs={{0,8},{4,12},{8,0},{12,4},{1,9},{5,13},{9,1},{13,5},{2,10},{6,14},... | collective-permute-start | bytes 159752 | tf_op jit(solution)/shard_map/ppermute | solution.py:450
